TPU v7x, 32 devices: a whole 2x2x4 slice. The times are simulated.
32 devices in a mesh: src: 2 (over x), rcv: 4 (over z), sp: 4 (over y, core).
Axes of the slice: x: 2, y: 2, z: 4, core: 2. Of those that a mesh axis runs over, the one named last changes fastest.
Arguments:
- shot_traces: float32 [32, 64, 1024], P('sp', 'src', 'rcv'), may hold values from -0.06 to 0.06
- surface_receiver_traces: float32 [32, 128, 1024], P('sp', 'rcv', 'src'), may hold values from -0.06 to 0.06
- obliquity: float32 [32], P('sp'), may hold values from 0.3 to 1
- lowest_receiver_index: int32 [32], P('sp'), may hold values from 0 to 31
- hi_index: int32 [32], P('sp'), may hold values from 96 to 127
Outputs:
- multiples: float32 [512, 2, 64, 128], P('sp', None, 'src', 'rcv')
All inputs are finite; a program needn't handle non-finite values.
Results may differ from a plain program's by a relative error of at most 0.000098.
Values sent between devices are 32-bit elements; how exact they have to be, the bound alone decides.
No kernel may reach another device: no remote copies, remote signals or barrier semaphores. Data moves between devices by JAX's collectives and lax.ppermute only.
A program may use at most 128 MiB of HBM per device.

v0:
```python
import math

import jax
import jax.numpy as jnp
import ml_dtypes
import numpy as np
from jax import lax
from jax.experimental import pallas as pl
from jax.experimental.pallas import tpu as pltpu
from jax.sharding import PartitionSpec as P

NF = 512
VMEM = pl.BlockSpec(memory_space=pltpu.VMEM)
SMEM = pl.BlockSpec(memory_space=pltpu.SMEM)


def split_table(samples, bins, parts):
    times = np.arange(samples, dtype=np.int64)[:, None]
    freqs = np.arange(bins, dtype=np.int64)[None, :]
    phases = (times * freqs % samples) * (2.0 * math.pi / samples)
    table = np.stack([np.cos(phases), -np.sin(phases)]).astype(np.float32)
    table = table.reshape(2, samples, parts, bins // parts).transpose(2, 1, 0, 3)
    table = table.reshape(parts, samples, 2 * (bins // parts))
    high = table.astype(ml_dtypes.bfloat16)
    low = (table - high.astype(np.float32)).astype(ml_dtypes.bfloat16)
    return high, low


def transform_kernel(pieces, parts, ramp, *refs):
    where_ref, refs = refs[0], refs[1:]
    if ramp:
        (obliquity_ref, lowest_ref, highest_ref), refs = refs[:3], refs[3:]
    piece_refs, refs = refs[:pieces], refs[pieces:]
    (high_ref, low_ref), refs = refs[:2], refs[2:]
    out_refs, (x_high, x_low) = refs[:parts], refs[parts:]
    me_time, me_sp, first_point = where_ref[0], where_ref[1], where_ref[2]
    points, rows, width = piece_refs[0].shape
    bins = out_refs[0].shape[-1]
    for j in range(pieces):
        x = piece_refs[j][...].reshape(points * rows, width)
        high = x.astype(jnp.bfloat16)
        low = (x - high.astype(jnp.float32)).astype(jnp.bfloat16)
        columns = pl.ds(pl.multiple_of((me_time ^ j) * width, width), width)
        x_high[:, columns] = high
        x_low[:, columns] = low
    if ramp:
        first = where_ref[3]
        receiver = first + lax.broadcasted_iota(jnp.int32, (rows, bins), 0)
        tapers = []
        for i in range(points):
            lowest, highest = lowest_ref[first_point + i], highest_ref[first_point + i]
            rising = jnp.clip((receiver - lowest + 1).astype(jnp.float32) / ramp, 0.0, 1.0)
            falling = jnp.clip((highest - receiver + 1).astype(jnp.float32) / ramp, 0.0, 1.0)
            tapers.append(obliquity_ref[first_point + i] * rising * falling)
    for k in range(parts):
        part = me_sp ^ k
        w_high, w_low = high_ref[part], low_ref[part]
        spectrum = (
            jnp.dot(x_high[...], w_high, preferred_element_type=jnp.float32)
            + jnp.dot(x_low[...], w_high, preferred_element_type=jnp.float32)
            + jnp.dot(x_high[...], w_low, preferred_element_type=jnp.float32)
        )
        for c in range(2):
            half = spectrum[:, c * bins : (c + 1) * bins].reshape(points, rows, bins)
            if ramp:
                for i in range(points):
                    out_refs[k][c, i] = half[i] * tapers[i]
            else:
                out_refs[k][c] = half


def transform(pieces, table, where, parts, ramp=0, taper=()):
    points, rows, width = pieces[0].shape
    samples, bins = table[0].shape[1], table[0].shape[2] // 2
    shape = (2, points, rows, bins)
    return pl.pallas_call(
        lambda *refs: transform_kernel(len(pieces), parts, ramp, *refs),
        out_shape=[jax.ShapeDtypeStruct(shape, jnp.float32)] * parts,
        in_specs=[SMEM] * (1 + len(taper)) + [VMEM] * (len(pieces) + 2),
        out_specs=[VMEM] * parts,
        scratch_shapes=[pltpu.VMEM((points * rows, samples), jnp.bfloat16)] * 2,
        compiler_params=pltpu.CompilerParams(vmem_limit_bytes=32 * 2**20),
        cost_estimate=pl.CostEstimate(
            flops=6 * points * rows * samples * bins * 2 * parts,
            bytes_accessed=8 * points * rows * samples + 8 * samples * bins * parts,
            transcendentals=0,
        ),
        name="transform",
    )(where, *taper, *pieces, *table)


GROUP = 2


def product_kernel(count, *refs):
    shot_refs, receiver_refs, out_ref = refs[:count], refs[count : 2 * count], refs[2 * count]
    _, shots, receivers, bins = out_ref.shape
    points = shot_refs[0].shape[1]

    def shot_group(g, _):
        def add_point(k, x, sums):
            r_re, r_im = receiver_refs[k][0, x], receiver_refs[k][1, x]
            r_sum = r_re + r_im
            new = []
            for i in range(GROUP):
                s_re = shot_refs[k][0, x, pl.ds(g * GROUP + i, 1), :]
                s_im = shot_refs[k][1, x, pl.ds(g * GROUP + i, 1), :]
                s_sum = s_re + s_im
                a, b, c = sums[3 * i : 3 * i + 3]
                new += [a + s_re * r_re, b + s_im * r_im, c + s_sum * r_sum]
            return tuple(new)

        sums = (jnp.zeros((receivers, bins), jnp.float32),) * (3 * GROUP)
        for k in range(count):
            sums = lax.fori_loop(0, points, lambda x, s, k=k: add_point(k, x, s), sums, unroll=2)
        for i in range(GROUP):
            a, b, c = sums[3 * i : 3 * i + 3]
            out_ref[0, g * GROUP + i] = a - b
            out_ref[1, g * GROUP + i] = c - a - b
        return 0

    lax.fori_loop(0, shots // GROUP, shot_group, 0)


def product(shot_blocks, receiver_blocks):
    count = len(shot_blocks)
    _, points, shots, bins = shot_blocks[0].shape
    receivers = receiver_blocks[0].shape[2]
    return pl.pallas_call(
        lambda *refs: product_kernel(count, *refs),
        out_shape=jax.ShapeDtypeStruct((2, shots, receivers, bins), jnp.float32),
        in_specs=[VMEM] * (2 * count),
        out_specs=VMEM,
        compiler_params=pltpu.CompilerParams(vmem_limit_bytes=32 * 2**20),
        cost_estimate=pl.CostEstimate(
            flops=8 * count * points * shots * receivers * bins,
            bytes_accessed=8 * (count * points * (shots + receivers) + shots * receivers) * bins,
            transcendentals=0,
        ),
        name="product",
    )(*shot_blocks, *receiver_blocks)


def exchange(block, axis, size, step):
    return lax.ppermute(block, axis, [(i, i ^ step) for i in range(size)])


def solution(mesh):
    n_src, n_rcv, n_sp = mesh.shape["src"], mesh.shape["rcv"], mesh.shape["sp"]

    def local(shot_traces, surface_receiver_traces, obliquity, lowest_receiver_index, hi_index):
        receivers = surface_receiver_traces.shape[1]
        samples = shot_traces.shape[2] * n_rcv
        table = tuple(jnp.asarray(t) for t in split_table(samples, NF, n_sp))
        me_src, me_rcv, me_sp = (lax.axis_index(a) for a in ("src", "rcv", "sp"))

        shot_pieces = [shot_traces] + [exchange(shot_traces, "rcv", n_rcv, j) for j in range(1, n_rcv)]
        receiver_pieces = [surface_receiver_traces] + [
            exchange(surface_receiver_traces, "src", n_src, j) for j in range(1, n_src)
        ]
        zero = jnp.int32(0)
        receiver_out = transform(
            receiver_pieces,
            table,
            jnp.stack([me_src, me_sp, zero, me_rcv * receivers]),
            n_sp,
            receivers * n_rcv // 8,
            (obliquity, lowest_receiver_index, hi_index),
        )
        receiver_blocks = [receiver_out[0]] + [
            exchange(receiver_out[k], "sp", n_sp, k) for k in range(1, n_sp)
        ]
        shot_out = transform(shot_pieces, table, jnp.stack([me_rcv, me_sp, zero, zero]), n_sp)
        shot_blocks = [shot_out[0]] + [exchange(shot_out[k], "sp", n_sp, k) for k in range(1, n_sp)]
        out = product(shot_blocks, receiver_blocks)
        return out.transpose(3, 0, 1, 2)

    placed = (P("sp", "src", "rcv"), P("sp", "rcv", "src"), P("sp"), P("sp"), P("sp"))
    return jax.shard_map(
        local, mesh=mesh, in_specs=placed, out_specs=P("sp", None, "src", "rcv"), check_vma=False
    )
```

profile of v0, /device:TPU:17, one launch (start us, length us, event | category | flops | bytes accessed | tf_op | source)
XLA Modules:
  0.0 65.4 jit_solution(2353407468280465893)
XLA Ops:
  0.0 0.0 collective-permute-start.1
  0.0 1.3 %collective-permute-start = (f32[8,32,256]{2,1,0:T(8,128)}, f32[8,32,256]{2,1,0:T(8,128)S(1)}, u32[]{:S(2)}, u32[]{:S(2)}) collective-permute-start(f32[8,32,256]{2,1,0:T(8,128)} %refs_1_.2), channel_id=1, source_target_pairs={{0,4},{4,0},{8,12},{12,8},{1,5},{5,1},{9,13},{13,9},{2,6},{6,2},{1... | collective-permute-start | bytes 786440 | tf_op jit(solution)/shard_map/ppermute | solution.py:145
  1.4 1.3 %collective-permute-start.2 = (f32[8,32,256]{2,1,0:T(8,128)}, f32[8,32,256]{2,1,0:T(8,128)S(1)}, u32[]{:S(2)}, u32[]{:S(2)}) collective-permute-start(f32[8,32,256]{2,1,0:T(8,128)} %refs_1_.2), channel_id=1, source_target_pairs={{0,12},{4,8},{8,4},{12,0},{1,13},{5,9},{9,5},{13,1},{2,14},{6,10},... | collective-permute-start | bytes 786440 | tf_op jit(solution)/shard_map/ppermute | solution.py:145
  2.6 1.2 %collective-permute-start.6 = (f32[8,32,512]{2,1,0:T(8,128)}, f32[8,32,512]{2,1,0:T(8,128)S(1)}, u32[]{:S(2)}, u32[]{:S(2)}) collective-permute-start(f32[8,32,512]{2,1,0:T(8,128)} %refs_4_.1), channel_id=1, source_target_pairs={{0,16},{16,0},{1,17},{17,1},{2,18},{18,2},{3,19},{19,3},{4,20},{20... | collective-permute-start | bytes 1572872 | tf_op jit(solution)/shard_map/ppermute | solution.py:145
  3.9 0.0 copy-start.2
  3.9 0.0 copy-start.3
  3.9 0.0 copy-start.4
  3.9 0.1 pad_add_fusion.refs_0_
  4.0 0.0 copy-start
  4.0 7.3 %collective-permute-done.1.refs_3_ = f32[8,32,256]{2,1,0:T(8,128)S(1)} collective-permute-done((f32[8,32,256]{2,1,0:T(8,128)}, f32[8,32,256]{2,1,0:T(8,128)S(1)}, u32[]{:S(2)}, u32[]{:S(2)}) %collective-permute-start.1) | collective-permute-done | bytes 262176 | tf_op jit(solution)/shard_map/ppermute | solution.py:145
  11.3 1.7 %collective-permute-done.refs_2_ = f32[8,32,256]{2,1,0:T(8,128)S(1)} collective-permute-done((f32[8,32,256]{2,1,0:T(8,128)}, f32[8,32,256]{2,1,0:T(8,128)S(1)}, u32[]{:S(2)}, u32[]{:S(2)}) %collective-permute-start) | collective-permute-done | bytes 262176 | tf_op jit(solution)/shard_map/ppermute | solution.py:145
  13.0 13.2 %collective-permute-done.2.refs_4_ = f32[8,32,256]{2,1,0:T(8,128)S(1)} collective-permute-done((f32[8,32,256]{2,1,0:T(8,128)}, f32[8,32,256]{2,1,0:T(8,128)S(1)}, u32[]{:S(2)}, u32[]{:S(2)}) %collective-permute-start.2) | collective-permute-done | bytes 262176 | tf_op jit(solution)/shard_map/ppermute | solution.py:145
  26.2 0.0 copy-start.1
  26.2 0.9 %copy-done.1 = f32[8,32,256]{2,1,0:T(8,128)S(1)} copy-done((f32[8,32,256]{2,1,0:T(8,128)S(1)}, f32[8,32,256]{2,1,0:T(8,128)}, u32[]{:S(2)}) %copy-start.1) | copy-done | bytes 262168
  27.1 0.0 copy-start.5
  27.1 1.6 %copy-done.5 = bf16[4,1024,256]{2,1,0:T(8,128)(2,1)S(1)} copy-done((bf16[4,1024,256]{2,1,0:T(8,128)(2,1)S(1)}, bf16[4,1024,256]{2,1,0:T(8,128)(2,1)}, u32[]{:S(2)}) %copy-start.5) | copy-done | bytes 2097176
  28.7 0.0 copy-start.7
  28.7 1.6 %copy-done.7 = bf16[4,1024,256]{2,1,0:T(8,128)(2,1)S(1)} copy-done((bf16[4,1024,256]{2,1,0:T(8,128)(2,1)S(1)}, bf16[4,1024,256]{2,1,0:T(8,128)(2,1)}, u32[]{:S(2)}) %copy-start.7) | copy-done | bytes 2097176
  30.3 0.0 copy-start.6
  30.3 2.6 %transform.2 = (f32[2,8,32,128]{3,2,1,0:T(8,128)S(1)}, f32[2,8,32,128]{3,2,1,0:T(8,128)S(1)}, f32[2,8,32,128]{3,2,1,0:T(8,128)S(1)}, f32[2,8,32,128]{3,2,1,0:T(8,128)S(1)}) custom-call(s32[4]{0:T(128)S(1)} %pad_add_fusion.refs_0_, f32[8,32,256]{2,1,0:T(8,128)S(1)} %copy-done.1, f32[8,32,256]{2,1,0:T(8,128)S(1)} %collective-permute-done.refs_2_, ...), custom_call_target="tpu_custom_call" | custom-call | flops 1610612736 | bytes 6291456 | tf_op jit(solution)/shard_map/transform/pallas_call | solution.py:76
  32.9 0.6 collective-permute-start.3
  33.5 0.1 pad_add_fusion.1.refs_0_
  33.5 1.2 %collective-permute-start.4 = (f32[2,8,32,128]{3,2,1,0:T(8,128)S(1)}, f32[2,8,32,128]{3,2,1,0:T(8,128)S(1)}, u32[]{:S(2)}, u32[]{:S(2)}) collective-permute-start(f32[2,8,32,128]{3,2,1,0:T(8,128)S(1)} %get-tuple-element.15), channel_id=1, source_target_pairs={{0,2},{1,3},{2,0},{3,1},{4,6},{5,7},{6,4},{7,5},{8,10},{9,11},{10,... | collective-permute-start | bytes 786440 | tf_op jit(solution)/shard_map/ppermute | solution.py:145
  34.8 0.4 collective-permute-start.5
  35.2 0.0 collective-permute-done.6.refs_5_
  35.2 0.0 copy-done.2
  35.2 0.0 copy-done.3
  35.2 0.0 copy-done.4
  35.2 0.0 copy-done
  35.2 0.0 copy-done.6
  35.2 2.6 %transform.3 = (f32[2,8,32,128]{3,2,1,0:T(8,128)S(1)}, f32[2,8,32,128]{3,2,1,0:T(8,128)S(1)}, f32[2,8,32,128]{3,2,1,0:T(8,128)S(1)}, f32[2,8,32,128]{3,2,1,0:T(8,128)S(1)}) custom-call(s32[4]{0:T(128)S(1)} %pad_add_fusion.1.refs_0_, f32[8]{0:T(128)S(1)} %copy-done.2, s32[8]{0:T(128)S(1)} %copy-done.3, s32[8]{0:T(128)S(1)} %copy-done.4, ...), custom_call_target="tpu_custom_call" | custom-call | flops 1610612736 | bytes 6291456 | tf_op jit(solution)/shard_map/transform/pallas_call | solution.py:76
  37.8 0.3 collective-permute-start.7
  38.1 1.2 %collective-permute-start.8 = (f32[2,8,32,128]{3,2,1,0:T(8,128)S(1)}, f32[2,8,32,128]{3,2,1,0:T(8,128)S(1)}, u32[]{:S(2)}, u32[]{:S(2)}) collective-permute-start(f32[2,8,32,128]{3,2,1,0:T(8,128)S(1)} %get-tuple-element.19), channel_id=1, source_target_pairs={{0,2},{1,3},{2,0},{3,1},{4,6},{5,7},{6,4},{7,5},{8,10},{9,11},{10,... | collective-permute-start | bytes 786440 | tf_op jit(solution)/shard_map/ppermute | solution.py:145
  39.3 0.0 collective-permute-done.3.refs_1_
  39.3 0.7 %collective-permute-start.9 = (f32[2,8,32,128]{3,2,1,0:T(8,128)S(1)}, f32[2,8,32,128]{3,2,1,0:T(8,128)S(1)}, u32[]{:S(2)}, u32[]{:S(2)}) collective-permute-start(f32[2,8,32,128]{3,2,1,0:T(8,128)S(1)} %get-tuple-element.20), channel_id=1, source_target_pairs={{0,3},{1,2},{2,1},{3,0},{4,7},{5,6},{6,5},{7,4},{8,11},{9,10},{10,... | collective-permute-start | bytes 786440 | tf_op jit(solution)/shard_map/ppermute | solution.py:145
  40.0 1.4 %collective-permute-done.4.refs_2_ = f32[2,8,32,128]{3,2,1,0:T(8,128)S(1)} collective-permute-done((f32[2,8,32,128]{3,2,1,0:T(8,128)S(1)}, f32[2,8,32,128]{3,2,1,0:T(8,128)S(1)}, u32[]{:S(2)}, u32[]{:S(2)}) %collective-permute-start.4) | collective-permute-done | bytes 262176 | tf_op jit(solution)/shard_map/ppermute | solution.py:145
  41.5 6.1 %collective-permute-done.5.refs_3_ = f32[2,8,32,128]{3,2,1,0:T(8,128)S(1)} collective-permute-done((f32[2,8,32,128]{3,2,1,0:T(8,128)S(1)}, f32[2,8,32,128]{3,2,1,0:T(8,128)S(1)}, u32[]{:S(2)}, u32[]{:S(2)}) %collective-permute-start.5) | collective-permute-done | bytes 262176 | tf_op jit(solution)/shard_map/ppermute | solution.py:145
  47.6 0.0 collective-permute-done.7.refs_5_
  47.6 5.1 %collective-permute-done.8.refs_6_ = f32[2,8,32,128]{3,2,1,0:T(8,128)S(1)} collective-permute-done((f32[2,8,32,128]{3,2,1,0:T(8,128)S(1)}, f32[2,8,32,128]{3,2,1,0:T(8,128)S(1)}, u32[]{:S(2)}, u32[]{:S(2)}) %collective-permute-start.8) | collective-permute-done | bytes 262176 | tf_op jit(solution)/shard_map/ppermute | solution.py:145
  52.7 5.7 %collective-permute-done.9.refs_7_ = f32[2,8,32,128]{3,2,1,0:T(8,128)S(1)} collective-permute-done((f32[2,8,32,128]{3,2,1,0:T(8,128)S(1)}, f32[2,8,32,128]{3,2,1,0:T(8,128)S(1)}, u32[]{:S(2)}, u32[]{:S(2)}) %collective-permute-start.9) | collective-permute-done | bytes 262176 | tf_op jit(solution)/shard_map/ppermute | solution.py:145
  58.4 7.0 %product.1 = f32[2,32,32,128]{3,2,1,0:T(8,128)} custom-call(f32[2,8,32,128]{3,2,1,0:T(8,128)S(1)} %get-tuple-element.13.refs_0_, f32[2,8,32,128]{3,2,1,0:T(8,128)S(1)} %collective-permute-done.3.refs_1_, f32[2,8,32,128]{3,2,1,0:T(8,128)S(1)} %collective-permute-done.4.refs_2_, f32[2,8,32,128]{3,2,1,0:T(8,128)S(1)} %collective-permute-done.5.refs_3_, ...), custom_call_target="tpu_custom_call" | custom-call | flops 33554432 | bytes 3145728 | tf_op jit(solution)/shard_map/product/pallas_call | solution.py:129
  (1 shorter events, 0.0 us)
Async XLA Ops:
  0.0 11.3 %collective-permute-start.1 = (f32[8,32,256]{2,1,0:T(8,128)}, f32[8,32,256]{2,1,0:T(8,128)S(1)}, u32[]{:S(2)}, u32[]{:S(2)}) collective-permute-start(f32[8,32,256]{2,1,0:T(8,128)} %refs_1_.2), channel_id=1, source_target_pairs={{0,8},{4,12},{8,0},{12,4},{1,9},{5,13},{9,1},{13,5},{2,10},{6,14},... | collective-permute-start | bytes 786440 | tf_op jit(solution)/shard_map/ppermute | solution.py:145
  0.0 13.0 %collective-permute-start = (f32[8,32,256]{2,1,0:T(8,128)}, f32[8,32,256]{2,1,0:T(8,128)S(1)}, u32[]{:S(2)}, u32[]{:S(2)}) collective-permute-start(f32[8,32,256]{2,1,0:T(8,128)} %refs_1_.2), channel_id=1, source_target_pairs={{0,4},{4,0},{8,12},{12,8},{1,5},{5,1},{9,13},{13,9},{2,6},{6,2},{1... | collective-permute-start | bytes 786440 | tf_op jit(solution)/shard_map/ppermute | solution.py:145
  1.4 24.8 %collective-permute-start.2 = (f32[8,32,256]{2,1,0:T(8,128)}, f32[8,32,256]{2,1,0:T(8,128)S(1)}, u32[]{:S(2)}, u32[]{:S(2)}) collective-permute-start(f32[8,32,256]{2,1,0:T(8,128)} %refs_1_.2), channel_id=1, source_target_pairs={{0,12},{4,8},{8,4},{12,0},{1,13},{5,9},{9,5},{13,1},{2,14},{6,10},... | collective-permute-start | bytes 786440 | tf_op jit(solution)/shard_map/ppermute | solution.py:145
  2.6 32.5 %collective-permute-start.6 = (f32[8,32,512]{2,1,0:T(8,128)}, f32[8,32,512]{2,1,0:T(8,128)S(1)}, u32[]{:S(2)}, u32[]{:S(2)}) collective-permute-start(f32[8,32,512]{2,1,0:T(8,128)} %refs_4_.1), channel_id=1, source_target_pairs={{0,16},{16,0},{1,17},{17,1},{2,18},{18,2},{3,19},{19,3},{4,20},{20... | collective-permute-start | bytes 1572872 | tf_op jit(solution)/shard_map/ppermute | solution.py:145
  3.9 31.3 %copy-start.2 = (f32[8]{0:T(128)S(1)}, f32[8]{0:T(128)}, u32[]{:S(2)}) copy-start(f32[8]{0:T(128)} %refs_1_.3) | copy-start | bytes 100
  3.9 31.3 %copy-start.3 = (s32[8]{0:T(128)S(1)}, s32[8]{0:T(128)}, u32[]{:S(2)}) copy-start(s32[8]{0:T(128)} %refs_2_.1) | copy-start | bytes 100
  3.9 31.3 %copy-start.4 = (s32[8]{0:T(128)S(1)}, s32[8]{0:T(128)}, u32[]{:S(2)}) copy-start(s32[8]{0:T(128)} %refs_3_.1) | copy-start | bytes 100
  4.0 31.3 %copy-start = (f32[8,32,512]{2,1,0:T(8,128)S(1)}, f32[8,32,512]{2,1,0:T(8,128)}, u32[]{:S(2)}) copy-start(f32[8,32,512]{2,1,0:T(8,128)} %refs_4_.1) | copy-start | bytes 1572868
  26.2 1.0 %copy-start.1 = (f32[8,32,256]{2,1,0:T(8,128)S(1)}, f32[8,32,256]{2,1,0:T(8,128)}, u32[]{:S(2)}) copy-start(f32[8,32,256]{2,1,0:T(8,128)} %refs_1_.2) | copy-start | bytes 786436
  27.1 1.6 %copy-start.5 = (bf16[4,1024,256]{2,1,0:T(8,128)(2,1)S(1)}, bf16[4,1024,256]{2,1,0:T(8,128)(2,1)}, u32[]{:S(2)}) copy-start(bf16[4,1024,256]{2,1,0:T(8,128)(2,1)} %constant.24.clone.refs_6_.refs_7_) | copy-start | bytes 6291460
  28.7 1.6 %copy-start.7 = (bf16[4,1024,256]{2,1,0:T(8,128)(2,1)S(1)}, bf16[4,1024,256]{2,1,0:T(8,128)(2,1)}, u32[]{:S(2)}) copy-start(bf16[4,1024,256]{2,1,0:T(8,128)(2,1)} %constant.23.clone.refs_5_.refs_6_) | copy-start | bytes 6291460
  30.3 4.9 %copy-start.6 = (bf16[4,1024,256]{2,1,0:T(8,128)(2,1)S(1)}, bf16[4,1024,256]{2,1,0:T(8,128)(2,1)}, u32[]{:S(2)}) copy-start(bf16[4,1024,256]{2,1,0:T(8,128)(2,1)} %constant.24.clone.refs_6_.refs_7_) | copy-start | bytes 6291460
  32.9 6.4 %collective-permute-start.3 = (f32[2,8,32,128]{3,2,1,0:T(8,128)S(1)}, f32[2,8,32,128]{3,2,1,0:T(8,128)S(1)}, u32[]{:S(2)}, u32[]{:S(2)}) collective-permute-start(f32[2,8,32,128]{3,2,1,0:T(8,128)S(1)} %get-tuple-element.14), channel_id=1, source_target_pairs={{0,1},{1,0},{2,3},{3,2},{4,5},{5,4},{6,7},{7,6},{8,9},{9,8},{10,11... | collective-permute-start | bytes 786440 | tf_op jit(solution)/shard_map/ppermute | solution.py:145
  33.5 7.9 %collective-permute-start.4 = (f32[2,8,32,128]{3,2,1,0:T(8,128)S(1)}, f32[2,8,32,128]{3,2,1,0:T(8,128)S(1)}, u32[]{:S(2)}, u32[]{:S(2)}) collective-permute-start(f32[2,8,32,128]{3,2,1,0:T(8,128)S(1)} %get-tuple-element.15), channel_id=1, source_target_pairs={{0,2},{1,3},{2,0},{3,1},{4,6},{5,7},{6,4},{7,5},{8,10},{9,11},{10,... | collective-permute-start | bytes 786440 | tf_op jit(solution)/shard_map/ppermute | solution.py:145
  34.8 12.8 %collective-permute-start.5 = (f32[2,8,32,128]{3,2,1,0:T(8,128)S(1)}, f32[2,8,32,128]{3,2,1,0:T(8,128)S(1)}, u32[]{:S(2)}, u32[]{:S(2)}) collective-permute-start(f32[2,8,32,128]{3,2,1,0:T(8,128)S(1)} %get-tuple-element.16), channel_id=1, source_target_pairs={{0,3},{1,2},{2,1},{3,0},{4,7},{5,6},{6,5},{7,4},{8,11},{9,10},{10,... | collective-permute-start | bytes 786440 | tf_op jit(solution)/shard_map/ppermute | solution.py:145
  37.8 9.8 %collective-permute-start.7 = (f32[2,8,32,128]{3,2,1,0:T(8,128)S(1)}, f32[2,8,32,128]{3,2,1,0:T(8,128)S(1)}, u32[]{:S(2)}, u32[]{:S(2)}) collective-permute-start(f32[2,8,32,128]{3,2,1,0:T(8,128)S(1)} %get-tuple-element.18), channel_id=1, source_target_pairs={{0,1},{1,0},{2,3},{3,2},{4,5},{5,4},{6,7},{7,6},{8,9},{9,8},{10,11... | collective-permute-start | bytes 786440 | tf_op jit(solution)/shard_map/ppermute | solution.py:145
  38.1 14.6 %collective-permute-start.8 = (f32[2,8,32,128]{3,2,1,0:T(8,128)S(1)}, f32[2,8,32,128]{3,2,1,0:T(8,128)S(1)}, u32[]{:S(2)}, u32[]{:S(2)}) collective-permute-start(f32[2,8,32,128]{3,2,1,0:T(8,128)S(1)} %get-tuple-element.19), channel_id=1, source_target_pairs={{0,2},{1,3},{2,0},{3,1},{4,6},{5,7},{6,4},{7,5},{8,10},{9,11},{10,... | collective-permute-start | bytes 786440 | tf_op jit(solution)/shard_map/ppermute | solution.py:145
  39.3 19.1 %collective-permute-start.9 = (f32[2,8,32,128]{3,2,1,0:T(8,128)S(1)}, f32[2,8,32,128]{3,2,1,0:T(8,128)S(1)}, u32[]{:S(2)}, u32[]{:S(2)}) collective-permute-start(f32[2,8,32,128]{3,2,1,0:T(8,128)S(1)} %get-tuple-element.20), channel_id=1, source_target_pairs={{0,3},{1,2},{2,1},{3,0},{4,7},{5,6},{6,5},{7,4},{8,11},{9,10},{10,... | collective-permute-start | bytes 786440 | tf_op jit(solution)/shard_map/ppermute | solution.py:145
where the time goes:
time: 65.6 us; the launch traced here: 65.4 us
  waiting for transfers between devices  40.6 us (62%)
  Pallas kernels  12.1 us (18%)
  starting transfers between devices  8.28 us (13%)
  local copies, waits for them, and re-layouts  4.15 us (6%)
    ppermute x10, waiting for transfers between devices, exchange(): return lax.ppermute(block, axis, [(i, i ^ step) for i in range(size)])  40.6 us
    ppermute x10, starting transfers between devices, exchange(): return lax.ppermute(block, axis, [(i, i ^ step) for i in range(size)])  8.28 us
    pallas_call x1, Pallas kernels, product(): pl.pallas_call(lambda *refs: product_kernel(count, *refs), out_shape=jax....  6.97 us
    pallas_call x2, Pallas kernels, transform(): pl.pallas_call(lambda *refs: transform_kernel(len(pieces), parts, ramp, *...  5.12 us
    unnamed x16, local copies, waits for them, and re-layouts  4.15 us
  transfers between devices with their start and end apart: 10, of which 7 were waited for; matrix products, arithmetic and copies ran while one was open for 0% of the time, Pallas kernels for 8%

commit v1 on v0

v1 whole, which is shorter than its diff:
```python
import math

import jax
import jax.numpy as jnp
import numpy as np
from jax import lax
from jax.experimental import pallas as pl
from jax.experimental.pallas import tpu as pltpu
from jax.sharding import PartitionSpec as P

NF = 512
VMEM = pl.BlockSpec(memory_space=pltpu.VMEM)
SMEM = pl.BlockSpec(memory_space=pltpu.SMEM)
ANY = pl.BlockSpec(memory_space=pl.ANY)
HBM = pl.BlockSpec(memory_space=pltpu.HBM)
COST = pl.CostEstimate(flops=1, bytes_accessed=1, transcendentals=0)
PARAMS = pltpu.CompilerParams(vmem_limit_bytes=16 * 2**20)


def cut_kernel(n_src, chunks, receiver_ref, shot_ref, *refs):
    receiver_outs, shot_outs, sems = refs[:n_src], refs[n_src : n_src + chunks], refs[-1]
    part = receiver_outs[0].shape[0]
    me = lax.axis_index("src")
    copies = []
    for j in range(n_src):
        span = pl.ds((me ^ j) * part, part)
        copies.append(pltpu.make_async_copy(receiver_ref.at[span], receiver_outs[j], sems.at[2 * j]))
        chunk, place = divmod(j * part, shot_outs[0].shape[0])
        copies.append(
            pltpu.make_async_copy(
                shot_ref.at[span], shot_outs[chunk].at[pl.ds(place, part)], sems.at[2 * j + 1]
            )
        )
    for copy in copies:
        copy.start()
    for copy in copies:
        copy.wait()


def cut(receiver_traces, shot_traces, n_src, chunks):
    points = receiver_traces.shape[0]
    out = pl.pallas_call(
        lambda *refs: cut_kernel(n_src, chunks, *refs),
        out_shape=[
            jax.ShapeDtypeStruct((points // n,) + a.shape[1:], a.dtype)
            for a, n in ((receiver_traces, n_src), (shot_traces, chunks))
            for _ in range(n)
        ],
        in_specs=[HBM, HBM],
        out_specs=[VMEM] * (n_src + chunks),
        scratch_shapes=[pltpu.SemaphoreType.DMA((2 * n_src,))],
        compiler_params=pltpu.CompilerParams(vmem_limit_bytes=60 * 2**20),
        cost_estimate=COST,
        name="cut",
    )(receiver_traces, shot_traces)
    return out[:n_src], out[n_src:]


def stage_kernel(coarse_ref, fine_ref, high_ref, low_ref):
    parts, steps, bins = fine_ref.shape[1:]

    def rows(a, _):
        for p in range(parts):
            cos_a, sin_a = coarse_ref[0, p, pl.ds(a, 1), :], coarse_ref[1, p, pl.ds(a, 1), :]
            cos_b, sin_b = fine_ref[0, p], fine_ref[1, p]
            span = pl.ds(pl.multiple_of(a * steps, steps), steps)
            both = jnp.concatenate([cos_a * cos_b - sin_a * sin_b, -(sin_a * cos_b + cos_a * sin_b)], axis=1)
            high = both.astype(jnp.bfloat16)
            high_ref[p, span, :] = high
            low_ref[p, span, :] = (both - high.astype(jnp.float32)).astype(jnp.bfloat16)
        return 0

    lax.fori_loop(0, coarse_ref.shape[2], rows, 0)


def fourier_table(samples, bins, parts):
    steps = 32

    def angles(times):
        freqs = np.arange(bins, dtype=np.int64)[None, :]
        phases = (times[:, None] * freqs % samples) * (2.0 * math.pi / samples)
        table = np.stack([np.cos(phases), np.sin(phases)]).astype(np.float32)
        return jnp.asarray(table.reshape(2, len(times), parts, bins // parts).transpose(0, 2, 1, 3))

    coarse = angles(np.arange(samples // steps, dtype=np.int64) * steps)
    fine = angles(np.arange(steps, dtype=np.int64))
    return pl.pallas_call(
        stage_kernel,
        out_shape=[jax.ShapeDtypeStruct((parts, samples, 2 * (bins // parts)), jnp.bfloat16)] * 2,
        in_specs=[VMEM] * 2,
        out_specs=[VMEM] * 2,
        compiler_params=PARAMS,
        cost_estimate=COST,
        name="fourier",
    )(coarse, fine)


def transform_kernel(pieces, parts, axis, ramp, *refs):
    if ramp:
        (obliquity_ref, lowest_ref, highest_ref), refs = refs[:3], refs[3:]
    piece_refs, refs = refs[:pieces], refs[pieces:]
    high_ref, low_ref = refs[:2]
    out_refs, (x_high, x_low) = refs[-2 - parts : -2], refs[-2:]
    points, rows, width = piece_refs[0].shape
    bins = out_refs[0].shape[-1]
    me_time, me_sp = lax.axis_index(axis), lax.axis_index("sp")
    for j in range(pieces):
        x = piece_refs[j][...].reshape(points * rows, width)
        high = x.astype(jnp.bfloat16)
        low = (x - high.astype(jnp.float32)).astype(jnp.bfloat16)
        columns = pl.ds(pl.multiple_of((me_time ^ j) * width, width), width)
        x_high[:, columns] = high
        x_low[:, columns] = low
    tapers = []
    if ramp:
        first = lax.axis_index("rcv") * rows
        receiver = first + lax.broadcasted_iota(jnp.int32, (rows, bins), 0)
        for i in range(points):
            point = lax.axis_index("src") * points + i
            lowest, highest = lowest_ref[point], highest_ref[point]
            rising = jnp.clip((receiver - lowest + 1).astype(jnp.float32) / ramp, 0.0, 1.0)
            falling = jnp.clip((highest - receiver + 1).astype(jnp.float32) / ramp, 0.0, 1.0)
            tapers.append(obliquity_ref[point] * rising * falling)
    for k in range(parts):
        part = me_sp ^ k
        w_high, w_low = high_ref[part], low_ref[part]
        spectrum = (
            jnp.dot(x_high[...], w_high, preferred_element_type=jnp.float32)
            + jnp.dot(x_low[...], w_high, preferred_element_type=jnp.float32)
            + jnp.dot(x_high[...], w_low, preferred_element_type=jnp.float32)
        )
        for c in range(2):
            half = spectrum[:, c * bins : (c + 1) * bins]
            if ramp:
                for i in range(points):
                    span = slice(i * rows, (i + 1) * rows)
                    out_refs[k][c, span] = half[span] * tapers[i]
            else:
                out_refs[k][c] = half


def transform(pieces, table, parts, axis, ramp=0, taper=(), after=()):
    points, rows, _ = pieces[0].shape
    samples, bins = table[0].shape[1], table[0].shape[2] // 2
    total = points * rows
    return pl.pallas_call(
        lambda *refs: transform_kernel(len(pieces), parts, axis, ramp, *refs),
        out_shape=[jax.ShapeDtypeStruct((2, total, bins), jnp.float32)] * parts,
        in_specs=[SMEM] * len(taper) + [VMEM] * (len(pieces) + 2) + [ANY] * len(after),
        out_specs=[VMEM] * parts,
        scratch_shapes=[pltpu.VMEM((total, samples), jnp.bfloat16)] * 2,
        compiler_params=PARAMS,
        cost_estimate=COST,
        name="transform",
    )(*taper, *pieces, *table, *after)


GROUP = 2


def product_kernel(terms, count, carried, rows, *refs):
    in_refs, total_refs, out_ref = refs[:count], refs[count : count + carried], refs[-1]
    shots, receivers = rows
    bins = out_ref.shape[-1]

    def shot_group(g, _):
        def add_point(term, x, sums):
            shot, shot_row, receiver, receiver_row, _ = term
            span = pl.ds(pl.multiple_of(receiver_row + x * receivers, 8), receivers)
            r_re, r_im = in_refs[receiver][0, span, :], in_refs[receiver][1, span, :]
            r_sum = r_re + r_im
            new = []
            for i in range(GROUP):
                line = pl.ds(shot_row + x * shots + g * GROUP + i, 1)
                s_re, s_im = in_refs[shot][0, line, :], in_refs[shot][1, line, :]
                s_sum = s_re + s_im
                a, b, c = sums[3 * i : 3 * i + 3]
                new += [a + s_re * r_re, b + s_im * r_im, c + s_sum * r_sum]
            return tuple(new)

        sums = (jnp.zeros((receivers, bins), jnp.float32),) * (3 * GROUP)
        for term in terms:
            step = lambda x, s, term=term: add_point(term, x, s)
            sums = lax.fori_loop(0, term[4], step, sums, unroll=2 if term[4] % 2 == 0 else 1)
        for i in range(GROUP):
            a, b, c = sums[3 * i : 3 * i + 3]
            real, imaginary = a - b, c - a - b
            if carried:
                real += total_refs[0][0, g * GROUP + i]
                imaginary += total_refs[0][1, g * GROUP + i]
            out_ref[0, g * GROUP + i] = real
            out_ref[1, g * GROUP + i] = imaginary
        return 0

    lax.fori_loop(0, shots // GROUP, shot_group, 0)


def product(terms, shots, receivers, total=None):
    blocks, described = [], []

    def place(block):
        for i, known in enumerate(blocks):
            if known is block:
                return i
        blocks.append(block)
        return len(blocks) - 1

    for shot, shot_row, receiver, receiver_row, points in terms:
        described.append((place(shot), shot_row, place(receiver), receiver_row, points))
    bins = blocks[0].shape[-1]
    carried = () if total is None else (total,)
    points = sum(term[4] for term in described)
    return pl.pallas_call(
        lambda *refs: product_kernel(described, len(blocks), len(carried), (shots, receivers), *refs),
        out_shape=jax.ShapeDtypeStruct((2, shots, receivers, bins), jnp.float32),
        in_specs=[VMEM] * (len(blocks) + len(carried)),
        out_specs=VMEM,
        compiler_params=PARAMS,
        cost_estimate=COST,
        name="product",
    )(*blocks, *carried)


def exchange(block, axis, size, step):
    return lax.ppermute(block, axis, [(i, i ^ step) for i in range(size)])


def gather(block, axis, size):
    pieces, step = {0: block}, size // 2
    while step:
        pieces |= {j ^ step: exchange(piece, axis, size, step) for j, piece in pieces.items()}
        step //= 2
    return [pieces[j] for j in range(size)]


def swap(blocks, axis, size):
    return [blocks[0]] + [exchange(blocks[step], axis, size, step) for step in range(1, size)]


def solution(mesh):
    n_src, n_rcv, n_sp = mesh.shape["src"], mesh.shape["rcv"], mesh.shape["sp"]

    def local(shot_traces, surface_receiver_traces, obliquity, lowest_receiver_index, hi_index):
        points, receivers = surface_receiver_traces.shape[:2]
        shots = shot_traces.shape[1]
        samples = shot_traces.shape[2] * n_rcv
        chunks, part = 2, points // n_src

        receiver_parts, shot_parts = cut(surface_receiver_traces, shot_traces, n_src, chunks)
        receiver_pieces = swap(receiver_parts, "src", n_src)
        shot_pieces = [gather(chunk, "rcv", n_rcv) for chunk in shot_parts]
        table = fourier_table(samples, NF, n_sp)

        near = n_sp // 2
        ramp = receivers * n_rcv // 8
        taper = (obliquity, lowest_receiver_index, hi_index)
        out = swap(transform(receiver_pieces, table, n_sp, "src", ramp, taper), "sp", n_sp)
        r = [gather(block, "src", n_src) for block in out]
        s = []
        for pieces in shot_pieces:
            out = swap(transform(pieces, table, n_sp, "rcv", after=(out[near],)), "sp", n_sp)
            s.append(out)

        def terms(chunk, k):
            held = n_src // chunks
            return [
                (s[chunk][k], j * part * shots, r[k][chunk * held + j], 0, part) for j in range(held)
            ]

        total = product(sum([terms(0, k) for k in range(n_sp)], []), shots, receivers)
        for span in (range(near), range(near, n_sp - 1), range(n_sp - 1, n_sp)):
            total = product(sum([terms(1, k) for k in span], []), shots, receivers, total)
        return total.transpose(3, 0, 1, 2)

    placed = (P("sp", "src", "rcv"), P("sp", "rcv", "src"), P("sp"), P("sp"), P("sp"))
    return jax.shard_map(
        local, mesh=mesh, in_specs=placed, out_specs=P("sp", None, "src", "rcv"), check_vma=False
    )
```

time: 65.6 us -> 49.1 us (0.75)
  the two profiles are of different devices: /device:TPU:17 before, /device:TPU:0 now
where the time goes in v1:
time: 49.1 us; the launch traced here: 48.8 us
  starting transfers between devices  18.8 us (38%)
  Pallas kernels  14.4 us (29%)
  waiting for transfers between devices  10.8 us (22%)
  local copies, waits for them, and re-layouts  4.73 us (10%)
    ppermute x20, starting transfers between devices, exchange(): return lax.ppermute(block, axis, [(i, i ^ step) for i in range(size)])  18.8 us
    ppermute x20, waiting for transfers between devices, exchange(): return lax.ppermute(block, axis, [(i, i ^ step) for i in range(size)])  10.8 us
    pallas_call x4, Pallas kernels, product(): pl.pallas_call(lambda *refs: product_kernel(described, len(blocks), len(c...  7.6 us
    unnamed x16, local copies, waits for them, and re-layouts  4.73 us
    pallas_call x3, Pallas kernels, transform(): pl.pallas_call(lambda *refs: transform_kernel(len(pieces), parts, axis, r...  3.67 us
    pallas_call x1, Pallas kernels, cut(): pl.pallas_call(lambda *refs: cut_kernel(n_src, chunks, *refs), out_shape=...  2.03 us
    pallas_call x1, Pallas kernels, fourier_table(): pl.pallas_call(stage_kernel, out_shape=[jax.ShapeDtypeStruct((parts, samp...  1.13 us
  transfers between devices with their start and end apart: 20, of which 6 were waited for; matrix products, arithmetic and copies ran while one was open for 0% of the time, Pallas kernels for 21%

profile of v1, /device:TPU:0, one launch (start us, length us, event | category | flops | bytes accessed | tf_op | source)
XLA Modules:
  0.0 48.8 jit_solution(13248921410054055477)
XLA Ops:
  0.0 2.0 %cut.1 = (f32[4,32,512]{2,1,0:T(8,128)}, f32[4,32,512]{2,1,0:T(8,128)}, f32[4,32,256]{2,1,0:T(8,128)}, f32[4,32,256]{2,1,0:T(8,128)}) custom-call(f32[8,32,512]{2,1,0:T(8,128)} %refs_0_.2, f32[8,32,256]{2,1,0:T(8,128)} %refs_1_.2), custom_call_target="tpu_custom_call" | custom-call | flops 1 | bytes 1 | tf_op jit(solution)/shard_map/cut/pallas_call | solution.py:42
  2.0 3.0 %collective-permute-start.6 = (f32[4,32,512]{2,1,0:T(8,128)}, f32[4,32,512]{2,1,0:T(8,128)S(1)}, u32[]{:S(2)}, u32[]{:S(2)}) collective-permute-start(f32[4,32,512]{2,1,0:T(8,128)} %get-tuple-element.28), channel_id=1, source_target_pairs={{0,16},{16,0},{1,17},{17,1},{2,18},{18,2},{3,19},{19,3},{4,20},{20... | collective-permute-start | bytes 786440 | tf_op jit(solution)/shard_map/ppermute | solution.py:225
  5.0 2.6 %collective-permute-start.4 = (f32[4,32,256]{2,1,0:T(8,128)}, f32[4,32,256]{2,1,0:T(8,128)S(1)}, u32[]{:S(2)}, u32[]{:S(2)}) collective-permute-start(f32[4,32,256]{2,1,0:T(8,128)} %get-tuple-element.26.refs_0_), channel_id=1, source_target_pairs={{0,8},{4,12},{8,0},{12,4},{1,9},{5,13},{9,1},{13,5},{2,10},{6,14},... | collective-permute-start | bytes 393224 | tf_op jit(solution)/shard_map/ppermute | solution.py:225
  7.6 1.6 %collective-permute-start.3 = (f32[4,32,256]{2,1,0:T(8,128)}, f32[4,32,256]{2,1,0:T(8,128)S(1)}, u32[]{:S(2)}, u32[]{:S(2)}) collective-permute-start(f32[4,32,256]{2,1,0:T(8,128)} %get-tuple-element.26.refs_0_), channel_id=1, source_target_pairs={{0,4},{4,0},{8,12},{12,8},{1,5},{5,1},{9,13},{13,9},{2,6},{6,2},{1... | collective-permute-start | bytes 393224 | tf_op jit(solution)/shard_map/ppermute | solution.py:225
  9.2 0.3 collective-permute-start.1
  9.5 0.9 %copy-done.3 = f32[2,4,32,128]{3,2,1,0:T(8,128)S(1)} copy-done((f32[2,4,32,128]{3,2,1,0:T(8,128)S(1)}, f32[2,4,32,128]{3,2,1,0:T(8,128)}, u32[]{:S(2)}) %copy-start.3) | copy-done | bytes 131096
  10.5 0.9 %copy-done.4 = f32[2,4,32,128]{3,2,1,0:T(8,128)S(1)} copy-done((f32[2,4,32,128]{3,2,1,0:T(8,128)S(1)}, f32[2,4,32,128]{3,2,1,0:T(8,128)}, u32[]{:S(2)}) %copy-start.4) | copy-done | bytes 131096
  11.4 1.1 %fourier.1 = (bf16[4,1024,256]{2,1,0:T(8,128)(2,1)S(1)}, bf16[4,1024,256]{2,1,0:T(8,128)(2,1)S(1)}) custom-call(f32[2,4,32,128]{3,2,1,0:T(8,128)S(1)} %copy-done.4, f32[2,4,32,128]{3,2,1,0:T(8,128)S(1)} %copy-done.3), custom_call_target="tpu_custom_call" | custom-call | flops 1 | bytes 1 | tf_op jit(solution)/shard_map/fourier/pallas_call | solution.py:87
  12.5 5.5 %collective-permute-done.4.refs_2_ = f32[4,32,256]{2,1,0:T(8,128)S(1)} collective-permute-done((f32[4,32,256]{2,1,0:T(8,128)}, f32[4,32,256]{2,1,0:T(8,128)S(1)}, u32[]{:S(2)}, u32[]{:S(2)}) %collective-permute-start.4) | collective-permute-done | bytes 131104 | tf_op jit(solution)/shard_map/ppermute | solution.py:225
  17.9 0.0 collective-permute-start.5
  17.9 0.0 collective-permute-done.6.refs_4_
  18.0 0.9 %copy-done = f32[4,32,512]{2,1,0:T(8,128)S(1)} copy-done((f32[4,32,512]{2,1,0:T(8,128)S(1)}, f32[4,32,512]{2,1,0:T(8,128)}, u32[]{:S(2)}) %copy-start) | copy-done | bytes 262168
  18.9 0.7 %copy-done.5 = f32[8]{0:T(128)S(1)} copy-done((f32[8]{0:T(128)S(1)}, f32[8]{0:T(128)}, u32[]{:S(2)}) %copy-start.5) | copy-done | bytes 56
  19.6 0.7 %copy-done.6 = s32[8]{0:T(128)S(1)} copy-done((s32[8]{0:T(128)S(1)}, s32[8]{0:T(128)}, u32[]{:S(2)}) %copy-start.6) | copy-done | bytes 56
  20.2 0.7 %copy-done.7 = s32[8]{0:T(128)S(1)} copy-done((s32[8]{0:T(128)S(1)}, s32[8]{0:T(128)}, u32[]{:S(2)}) %copy-start.7) | copy-done | bytes 56
  20.9 1.6 %transform.3 = (f32[2,128,128]{2,1,0:T(8,128)S(1)}, f32[2,128,128]{2,1,0:T(8,128)S(1)}, f32[2,128,128]{2,1,0:T(8,128)S(1)}, f32[2,128,128]{2,1,0:T(8,128)S(1)}) custom-call(f32[8]{0:T(128)S(1)} %copy-done.5, s32[8]{0:T(128)S(1)} %copy-done.6, s32[8]{0:T(128)S(1)} %copy-done.7, f32[4,32,512]{2,1,0:T(8,128)S(1)} %copy-done, ...), custom_call_target="tpu_custom_call" | custom-call | flops 1 | bytes 1 | tf_op jit(solution)/shard_map/transform/pallas_call | solution.py:146
  22.5 1.6 %collective-permute-start.7 = (f32[2,128,128]{2,1,0:T(8,128)S(1)}, f32[2,128,128]{2,1,0:T(8,128)S(1)}, u32[]{:S(2)}, u32[]{:S(2)}) collective-permute-start(f32[2,128,128]{2,1,0:T(8,128)S(1)} %get-tuple-element.29), channel_id=1, source_target_pairs={{0,2},{1,3},{2,0},{3,1},{4,6},{5,7},{6,4},{7,5},{8,10},{9,11},{10,... | collective-permute-start | bytes 393224 | tf_op jit(solution)/shard_map/ppermute | solution.py:225
  24.1 2.0 %collective-permute-start = (f32[4,32,256]{2,1,0:T(8,128)S(1)}, f32[4,32,256]{2,1,0:T(8,128)S(1)}, u32[]{:S(2)}, u32[]{:S(2)}) collective-permute-start(f32[4,32,256]{2,1,0:T(8,128)S(1)} %copy-done.1), channel_id=1, source_target_pairs={{0,4},{4,0},{8,12},{12,8},{1,5},{5,1},{9,13},{13,9},{2,6},{6,2},{1... | collective-permute-start | bytes 393224 | tf_op jit(solution)/shard_map/ppermute | solution.py:225
  26.1 0.0 collective-permute-done.1.refs_2_
  26.1 0.1 collective-permute-start.2
  26.2 0.0 collective-permute-done.3.refs_1_
  26.2 0.0 collective-permute-start.16
  26.2 0.0 collective-permute-done.5.refs_3_
  26.2 1.3 %collective-permute-done.7.refs_6_.refs_5_ = f32[2,128,128]{2,1,0:T(8,128)S(1)} collective-permute-done((f32[2,128,128]{2,1,0:T(8,128)S(1)}, f32[2,128,128]{2,1,0:T(8,128)S(1)}, u32[]{:S(2)}, u32[]{:S(2)}) %collective-permute-start.7) | collective-permute-done | bytes 131104 | tf_op jit(solution)/shard_map/ppermute | solution.py:225
  27.5 1.0 %transform.4 = (f32[2,128,128]{2,1,0:T(8,128)S(1)}, f32[2,128,128]{2,1,0:T(8,128)S(1)}, f32[2,128,128]{2,1,0:T(8,128)S(1)}, f32[2,128,128]{2,1,0:T(8,128)S(1)}) custom-call(f32[4,32,256]{2,1,0:T(8,128)S(1)} %copy-done.2, f32[4,32,256]{2,1,0:T(8,128)S(1)} %collective-permute-done.3.refs_1_, f32[4,32,256]{2,1,0:T(8,128)S(1)} %collective-permute-done.4.refs_2_, ...), custom_call_target="tpu_custom_call" | custom-call | flops 1 | bytes 1 | tf_op jit(solution)/shard_map/transform/pallas_call | solution.py:146
  28.6 1.6 %collective-permute-start.8 = (f32[2,128,128]{2,1,0:T(8,128)S(1)}, f32[2,128,128]{2,1,0:T(8,128)S(1)}, u32[]{:S(2)}, u32[]{:S(2)}) collective-permute-start(f32[2,128,128]{2,1,0:T(8,128)S(1)} %get-tuple-element.30), channel_id=1, source_target_pairs={{0,2},{1,3},{2,0},{3,1},{4,6},{5,7},{6,4},{7,5},{8,10},{9,11},{10,... | collective-permute-start | bytes 393224 | tf_op jit(solution)/shard_map/ppermute | solution.py:225
  30.1 0.0 collective-permute-start.10
  30.1 0.0 collective-permute-done.refs_1_
  30.2 0.5 %collective-permute-start.14 = (f32[2,128,128]{2,1,0:T(8,128)S(1)}, f32[2,128,128]{2,1,0:T(8,128)S(1)}, u32[]{:S(2)}, u32[]{:S(2)}) collective-permute-start(f32[2,128,128]{2,1,0:T(8,128)S(1)} %get-tuple-element.35.refs_1_), channel_id=1, source_target_pairs={{0,16},{16,0},{1,17},{17,1},{2,18},{18,2},{3,19},{19,3},{4,20},{20... | collective-permute-start | bytes 393224 | tf_op jit(solution)/shard_map/ppermute | solution.py:225
  30.7 0.4 collective-permute-done.2.refs_3_
  31.1 0.0 collective-permute-start.18
  31.1 0.0 collective-permute-done.16.refs_3_
  31.1 1.2 %collective-permute-start.19 = (f32[2,128,128]{2,1,0:T(8,128)S(1)}, f32[2,128,128]{2,1,0:T(8,128)S(1)}, u32[]{:S(2)}, u32[]{:S(2)}) collective-permute-start(f32[2,128,128]{2,1,0:T(8,128)S(1)} %get-tuple-element.40), channel_id=1, source_target_pairs={{0,3},{1,2},{2,1},{3,0},{4,7},{5,6},{6,5},{7,4},{8,11},{9,10},{10,... | collective-permute-start | bytes 393224 | tf_op jit(solution)/shard_map/ppermute | solution.py:225
  32.2 1.8 %collective-permute-done.8.refs_6_.refs_4_ = f32[2,128,128]{2,1,0:T(8,128)S(1)} collective-permute-done((f32[2,128,128]{2,1,0:T(8,128)S(1)}, f32[2,128,128]{2,1,0:T(8,128)S(1)}, u32[]{:S(2)}, u32[]{:S(2)}) %collective-permute-start.8) | collective-permute-done | bytes 131104 | tf_op jit(solution)/shard_map/ppermute | solution.py:225
  34.1 0.0 collective-permute-start.17
  34.1 1.0 %transform.5 = (f32[2,128,128]{2,1,0:T(8,128)S(1)}, f32[2,128,128]{2,1,0:T(8,128)S(1)}, f32[2,128,128]{2,1,0:T(8,128)S(1)}, f32[2,128,128]{2,1,0:T(8,128)S(1)}) custom-call(f32[4,32,256]{2,1,0:T(8,128)S(1)} %copy-done.1, f32[4,32,256]{2,1,0:T(8,128)S(1)} %collective-permute-done.refs_1_, f32[4,32,256]{2,1,0:T(8,128)S(1)} %collective-permute-done.1.refs_2_, ...), custom_call_target="tpu_custom_call" | custom-call | flops 1 | bytes 1 | tf_op jit(solution)/shard_map/transform/pallas_call | solution.py:146
  35.1 1.7 %collective-permute-done.10.refs_7_ = f32[2,128,128]{2,1,0:T(8,128)S(1)} collective-permute-done((f32[2,128,128]{2,1,0:T(8,128)S(1)}, f32[2,128,128]{2,1,0:T(8,128)S(1)}, u32[]{:S(2)}, u32[]{:S(2)}) %collective-permute-start.10) | collective-permute-done | bytes 131104 | tf_op jit(solution)/shard_map/ppermute | solution.py:225
  36.8 0.4 collective-permute-start.13
  37.2 0.0 collective-permute-done.14.refs_1_
  37.2 0.0 collective-permute-start.15
  37.2 1.7 %collective-permute-start.11 = (f32[2,128,128]{2,1,0:T(8,128)S(1)}, f32[2,128,128]{2,1,0:T(8,128)S(1)}, u32[]{:S(2)}, u32[]{:S(2)}) collective-permute-start(f32[2,128,128]{2,1,0:T(8,128)S(1)} %collective-permute-done.10.refs_7_), channel_id=1, source_target_pairs={{0,16},{16,0},{1,17},{17,1},{2,18},{18,2},{3,19},{19,3},{4,20},{20... | collective-permute-start | bytes 393224 | tf_op jit(solution)/shard_map/ppermute | solution.py:225
  38.9 2.2 %collective-permute-start.12 = (f32[2,128,128]{2,1,0:T(8,128)S(1)}, f32[2,128,128]{2,1,0:T(8,128)S(1)}, u32[]{:S(2)}, u32[]{:S(2)}) collective-permute-start(f32[2,128,128]{2,1,0:T(8,128)S(1)} %get-tuple-element.33), channel_id=1, source_target_pairs={{0,2},{1,3},{2,0},{3,1},{4,6},{5,7},{6,4},{7,5},{8,10},{9,11},{10,... | collective-permute-start | bytes 393224 | tf_op jit(solution)/shard_map/ppermute | solution.py:225
  41.1 3.1 %product.4.refs_4_ = f32[2,32,32,128]{3,2,1,0:T(8,128)S(1)} custom-call(f32[2,128,128]{2,1,0:T(8,128)S(1)} %get-tuple-element.38.refs_0_, f32[2,128,128]{2,1,0:T(8,128)S(1)} %get-tuple-element.35.refs_1_, f32[2,128,128]{2,1,0:T(8,128)S(1)} %collective-permute-done.18.refs_2_, f32[2,128,128]{2,1,0:T(8,128)S(1)} %collective-permute-done.16.refs_3_, ...), custom_call_target="tpu_custom_call" | custom-call | flops 1 | bytes 1 | tf_op jit(solution)/shard_map/product/pallas_call | solution.py:213
  44.2 1.7 %product.5.refs_2_ = f32[2,32,32,128]{3,2,1,0:T(8,128)S(1)} custom-call(f32[2,128,128]{2,1,0:T(8,128)S(1)} %get-tuple-element.34.refs_0_, f32[2,128,128]{2,1,0:T(8,128)S(1)} %collective-permute-done.14.refs_1_, f32[2,128,128]{2,1,0:T(8,128)S(1)} %collective-permute-done.15.refs_2_, f32[2,128,128]{2,1,0:T(8,128)S(1)} %collective-permute-done.17.refs_3_, ...), custom_call_target="tpu_custom_call" | custom-call | flops 1 | bytes 1 | tf_op jit(solution)/shard_map/product/pallas_call | solution.py:213
  45.8 0.0 collective-permute-done.12.refs_0_
  45.9 0.9 %product.6.refs_2_ = f32[2,32,32,128]{3,2,1,0:T(8,128)S(1)} custom-call(f32[2,128,128]{2,1,0:T(8,128)S(1)} %collective-permute-done.12.refs_0_, f32[2,128,128]{2,1,0:T(8,128)S(1)} %collective-permute-done.13.refs_1_, f32[2,32,32,128]{3,2,1,0:T(8,128)S(1)} %product.5.refs_2_), custom_call_target="tpu_custom_call" | custom-call | flops 1 | bytes 1 | tf_op jit(solution)/shard_map/product/pallas_call | solution.py:213
  46.8 0.1 collective-permute-done.9.refs_0_
  46.9 1.9 %product.7 = f32[2,32,32,128]{3,2,1,0:T(8,128)} custom-call(f32[2,128,128]{2,1,0:T(8,128)S(1)} %collective-permute-done.9.refs_0_, f32[2,128,128]{2,1,0:T(8,128)S(1)} %collective-permute-done.11.refs_1_, f32[2,32,32,128]{3,2,1,0:T(8,128)S(1)} %product.6.refs_2_), custom_call_target="tpu_custom_call" | custom-call | flops 1 | bytes 1 | tf_op jit(solution)/shard_map/product/pallas_call | solution.py:213
  (17 shorter events, 0.0 us)
Async XLA Ops:
  2.0 15.9 %collective-permute-start.6 = (f32[4,32,512]{2,1,0:T(8,128)}, f32[4,32,512]{2,1,0:T(8,128)S(1)}, u32[]{:S(2)}, u32[]{:S(2)}) collective-permute-start(f32[4,32,512]{2,1,0:T(8,128)} %get-tuple-element.28), channel_id=1, source_target_pairs={{0,16},{16,0},{1,17},{17,1},{2,18},{18,2},{3,19},{19,3},{4,20},{20... | collective-permute-start | bytes 786440 | tf_op jit(solution)/shard_map/ppermute | solution.py:225
  5.0 12.9 %collective-permute-start.4 = (f32[4,32,256]{2,1,0:T(8,128)}, f32[4,32,256]{2,1,0:T(8,128)S(1)}, u32[]{:S(2)}, u32[]{:S(2)}) collective-permute-start(f32[4,32,256]{2,1,0:T(8,128)} %get-tuple-element.26.refs_0_), channel_id=1, source_target_pairs={{0,8},{4,12},{8,0},{12,4},{1,9},{5,13},{9,1},{13,5},{2,10},{6,14},... | collective-permute-start | bytes 393224 | tf_op jit(solution)/shard_map/ppermute | solution.py:225
  7.6 18.5 %collective-permute-start.3 = (f32[4,32,256]{2,1,0:T(8,128)}, f32[4,32,256]{2,1,0:T(8,128)S(1)}, u32[]{:S(2)}, u32[]{:S(2)}) collective-permute-start(f32[4,32,256]{2,1,0:T(8,128)} %get-tuple-element.26.refs_0_), channel_id=1, source_target_pairs={{0,4},{4,0},{8,12},{12,8},{1,5},{5,1},{9,13},{13,9},{2,6},{6,2},{1... | collective-permute-start | bytes 393224 | tf_op jit(solution)/shard_map/ppermute | solution.py:225
  9.2 16.9 %collective-permute-start.1 = (f32[4,32,256]{2,1,0:T(8,128)}, f32[4,32,256]{2,1,0:T(8,128)S(1)}, u32[]{:S(2)}, u32[]{:S(2)}) collective-permute-start(f32[4,32,256]{2,1,0:T(8,128)} %get-tuple-element.23.refs_0_), channel_id=1, source_target_pairs={{0,8},{4,12},{8,0},{12,4},{1,9},{5,13},{9,1},{13,5},{2,10},{6,14},... | collective-permute-start | bytes 393224 | tf_op jit(solution)/shard_map/ppermute | solution.py:225
  9.5 0.9 %copy-start.3 = (f32[2,4,32,128]{3,2,1,0:T(8,128)S(1)}, f32[2,4,32,128]{3,2,1,0:T(8,128)}, u32[]{:S(2)}) copy-start(f32[2,4,32,128]{3,2,1,0:T(8,128)} %constant.5.clone.fine_ref) | copy-start | bytes 393220
  10.5 0.9 %copy-start.4 = (f32[2,4,32,128]{3,2,1,0:T(8,128)S(1)}, f32[2,4,32,128]{3,2,1,0:T(8,128)}, u32[]{:S(2)}) copy-start(f32[2,4,32,128]{3,2,1,0:T(8,128)} %constant.4.clone.coarse_ref) | copy-start | bytes 393220
  17.9 8.2 %collective-permute-start.5 = (f32[4,32,256]{2,1,0:T(8,128)S(1)}, f32[4,32,256]{2,1,0:T(8,128)S(1)}, u32[]{:S(2)}, u32[]{:S(2)}) collective-permute-start(f32[4,32,256]{2,1,0:T(8,128)S(1)} %collective-permute-done.4.refs_2_), channel_id=1, source_target_pairs={{0,4},{4,0},{8,12},{12,8},{1,5},{5,1},{9,13},{13,9},{2,6},{6,2},{1... | collective-permute-start | bytes 393224 | tf_op jit(solution)/shard_map/ppermute | solution.py:225
  18.0 1.0 %copy-start = (f32[4,32,512]{2,1,0:T(8,128)S(1)}, f32[4,32,512]{2,1,0:T(8,128)}, u32[]{:S(2)}) copy-start(f32[4,32,512]{2,1,0:T(8,128)} %get-tuple-element.27.refs_3_) | copy-start | bytes 786436
  18.9 0.7 %copy-start.5 = (f32[8]{0:T(128)S(1)}, f32[8]{0:T(128)}, u32[]{:S(2)}) copy-start(f32[8]{0:T(128)} %refs_0_.3) | copy-start | bytes 100
  19.6 0.7 %copy-start.6 = (s32[8]{0:T(128)S(1)}, s32[8]{0:T(128)}, u32[]{:S(2)}) copy-start(s32[8]{0:T(128)} %refs_1_.3) | copy-start | bytes 100
  20.2 0.7 %copy-start.7 = (s32[8]{0:T(128)S(1)}, s32[8]{0:T(128)}, u32[]{:S(2)}) copy-start(s32[8]{0:T(128)} %refs_2_.1) | copy-start | bytes 100
  20.9 3.2 %copy-start.1 = (f32[4,32,256]{2,1,0:T(8,128)S(1)}, f32[4,32,256]{2,1,0:T(8,128)}, u32[]{:S(2)}) copy-start(f32[4,32,256]{2,1,0:T(8,128)} %get-tuple-element.23.refs_0_) | copy-start | bytes 393220
  20.9 6.6 %copy-start.2 = (f32[4,32,256]{2,1,0:T(8,128)S(1)}, f32[4,32,256]{2,1,0:T(8,128)}, u32[]{:S(2)}) copy-start(f32[4,32,256]{2,1,0:T(8,128)} %get-tuple-element.26.refs_0_) | copy-start | bytes 393220
  22.5 5.0 %collective-permute-start.7 = (f32[2,128,128]{2,1,0:T(8,128)S(1)}, f32[2,128,128]{2,1,0:T(8,128)S(1)}, u32[]{:S(2)}, u32[]{:S(2)}) collective-permute-start(f32[2,128,128]{2,1,0:T(8,128)S(1)} %get-tuple-element.29), channel_id=1, source_target_pairs={{0,2},{1,3},{2,0},{3,1},{4,6},{5,7},{6,4},{7,5},{8,10},{9,11},{10,... | collective-permute-start | bytes 393224 | tf_op jit(solution)/shard_map/ppermute | solution.py:225
  24.1 6.1 %collective-permute-start = (f32[4,32,256]{2,1,0:T(8,128)S(1)}, f32[4,32,256]{2,1,0:T(8,128)S(1)}, u32[]{:S(2)}, u32[]{:S(2)}) collective-permute-start(f32[4,32,256]{2,1,0:T(8,128)S(1)} %copy-done.1), channel_id=1, source_target_pairs={{0,4},{4,0},{8,12},{12,8},{1,5},{5,1},{9,13},{13,9},{2,6},{6,2},{1... | collective-permute-start | bytes 393224 | tf_op jit(solution)/shard_map/ppermute | solution.py:225
  26.1 5.0 %collective-permute-start.2 = (f32[4,32,256]{2,1,0:T(8,128)S(1)}, f32[4,32,256]{2,1,0:T(8,128)S(1)}, u32[]{:S(2)}, u32[]{:S(2)}) collective-permute-start(f32[4,32,256]{2,1,0:T(8,128)S(1)} %collective-permute-done.1.refs_2_), channel_id=1, source_target_pairs={{0,4},{4,0},{8,12},{12,8},{1,5},{5,1},{9,13},{13,9},{2,6},{6,2},{1... | collective-permute-start | bytes 393224 | tf_op jit(solution)/shard_map/ppermute | solution.py:225
  26.2 4.9 %collective-permute-start.16 = (f32[2,128,128]{2,1,0:T(8,128)S(1)}, f32[2,128,128]{2,1,0:T(8,128)S(1)}, u32[]{:S(2)}, u32[]{:S(2)}) collective-permute-start(f32[2,128,128]{2,1,0:T(8,128)S(1)} %get-tuple-element.37), channel_id=1, source_target_pairs={{0,1},{1,0},{2,3},{3,2},{4,5},{5,4},{6,7},{7,6},{8,9},{9,8},{10,11... | collective-permute-start | bytes 393224 | tf_op jit(solution)/shard_map/ppermute | solution.py:225
  28.6 5.5 %collective-permute-start.8 = (f32[2,128,128]{2,1,0:T(8,128)S(1)}, f32[2,128,128]{2,1,0:T(8,128)S(1)}, u32[]{:S(2)}, u32[]{:S(2)}) collective-permute-start(f32[2,128,128]{2,1,0:T(8,128)S(1)} %get-tuple-element.30), channel_id=1, source_target_pairs={{0,2},{1,3},{2,0},{3,1},{4,6},{5,7},{6,4},{7,5},{8,10},{9,11},{10,... | collective-permute-start | bytes 393224 | tf_op jit(solution)/shard_map/ppermute | solution.py:225
  30.1 6.6 %collective-permute-start.10 = (f32[2,128,128]{2,1,0:T(8,128)S(1)}, f32[2,128,128]{2,1,0:T(8,128)S(1)}, u32[]{:S(2)}, u32[]{:S(2)}) collective-permute-start(f32[2,128,128]{2,1,0:T(8,128)S(1)} %get-tuple-element.32), channel_id=1, source_target_pairs={{0,3},{1,2},{2,1},{3,0},{4,7},{5,6},{6,5},{7,4},{8,11},{9,10},{10,... | collective-permute-start | bytes 393224 | tf_op jit(solution)/shard_map/ppermute | solution.py:225
  30.2 7.1 %collective-permute-start.14 = (f32[2,128,128]{2,1,0:T(8,128)S(1)}, f32[2,128,128]{2,1,0:T(8,128)S(1)}, u32[]{:S(2)}, u32[]{:S(2)}) collective-permute-start(f32[2,128,128]{2,1,0:T(8,128)S(1)} %get-tuple-element.35.refs_1_), channel_id=1, source_target_pairs={{0,16},{16,0},{1,17},{17,1},{2,18},{18,2},{3,19},{19,3},{4,20},{20... | collective-permute-start | bytes 393224 | tf_op jit(solution)/shard_map/ppermute | solution.py:225
  31.1 6.2 %collective-permute-start.18 = (f32[2,128,128]{2,1,0:T(8,128)S(1)}, f32[2,128,128]{2,1,0:T(8,128)S(1)}, u32[]{:S(2)}, u32[]{:S(2)}) collective-permute-start(f32[2,128,128]{2,1,0:T(8,128)S(1)} %get-tuple-element.39), channel_id=1, source_target_pairs={{0,1},{1,0},{2,3},{3,2},{4,5},{5,4},{6,7},{7,6},{8,9},{9,8},{10,11... | collective-permute-start | bytes 393224 | tf_op jit(solution)/shard_map/ppermute | solution.py:225
  31.1 7.8 %collective-permute-start.19 = (f32[2,128,128]{2,1,0:T(8,128)S(1)}, f32[2,128,128]{2,1,0:T(8,128)S(1)}, u32[]{:S(2)}, u32[]{:S(2)}) collective-permute-start(f32[2,128,128]{2,1,0:T(8,128)S(1)} %get-tuple-element.40), channel_id=1, source_target_pairs={{0,3},{1,2},{2,1},{3,0},{4,7},{5,6},{6,5},{7,4},{8,11},{9,10},{10,... | collective-permute-start | bytes 393224 | tf_op jit(solution)/shard_map/ppermute | solution.py:225
  34.1 7.0 %collective-permute-start.17 = (f32[2,128,128]{2,1,0:T(8,128)S(1)}, f32[2,128,128]{2,1,0:T(8,128)S(1)}, u32[]{:S(2)}, u32[]{:S(2)}) collective-permute-start(f32[2,128,128]{2,1,0:T(8,128)S(1)} %collective-permute-done.16.refs_3_), channel_id=1, source_target_pairs={{0,16},{16,0},{1,17},{17,1},{2,18},{18,2},{3,19},{19,3},{4,20},{20... | collective-permute-start | bytes 393224 | tf_op jit(solution)/shard_map/ppermute | solution.py:225
  36.8 9.1 %collective-permute-start.13 = (f32[2,128,128]{2,1,0:T(8,128)S(1)}, f32[2,128,128]{2,1,0:T(8,128)S(1)}, u32[]{:S(2)}, u32[]{:S(2)}) collective-permute-start(f32[2,128,128]{2,1,0:T(8,128)S(1)} %collective-permute-done.7.refs_6_.refs_5_), channel_id=1, source_target_pairs={{0,16},{16,0},{1,17},{17,1},{2,18},{18,2},{3,19},{19,3},{4,20},{20... | collective-permute-start | bytes 393224 | tf_op jit(solution)/shard_map/ppermute | solution.py:225
  37.2 6.9 %collective-permute-start.15 = (f32[2,128,128]{2,1,0:T(8,128)S(1)}, f32[2,128,128]{2,1,0:T(8,128)S(1)}, u32[]{:S(2)}, u32[]{:S(2)}) collective-permute-start(f32[2,128,128]{2,1,0:T(8,128)S(1)} %get-tuple-element.36), channel_id=1, source_target_pairs={{0,1},{1,0},{2,3},{3,2},{4,5},{5,4},{6,7},{7,6},{8,9},{9,8},{10,11... | collective-permute-start | bytes 393224 | tf_op jit(solution)/shard_map/ppermute | solution.py:225
  37.2 9.6 %collective-permute-start.11 = (f32[2,128,128]{2,1,0:T(8,128)S(1)}, f32[2,128,128]{2,1,0:T(8,128)S(1)}, u32[]{:S(2)}, u32[]{:S(2)}) collective-permute-start(f32[2,128,128]{2,1,0:T(8,128)S(1)} %collective-permute-done.10.refs_7_), channel_id=1, source_target_pairs={{0,16},{16,0},{1,17},{17,1},{2,18},{18,2},{3,19},{19,3},{4,20},{20... | collective-permute-start | bytes 393224 | tf_op jit(solution)/shard_map/ppermute | solution.py:225
  38.9 7.0 %collective-permute-start.12 = (f32[2,128,128]{2,1,0:T(8,128)S(1)}, f32[2,128,128]{2,1,0:T(8,128)S(1)}, u32[]{:S(2)}, u32[]{:S(2)}) collective-permute-start(f32[2,128,128]{2,1,0:T(8,128)S(1)} %get-tuple-element.33), channel_id=1, source_target_pairs={{0,2},{1,3},{2,0},{3,1},{4,6},{5,7},{6,4},{7,5},{8,10},{9,11},{10,... | collective-permute-start | bytes 393224 | tf_op jit(solution)/shard_map/ppermute | solution.py:225
  41.1 5.9 %collective-permute-start.9 = (f32[2,128,128]{2,1,0:T(8,128)S(1)}, f32[2,128,128]{2,1,0:T(8,128)S(1)}, u32[]{:S(2)}, u32[]{:S(2)}) collective-permute-start(f32[2,128,128]{2,1,0:T(8,128)S(1)} %get-tuple-element.31), channel_id=1, source_target_pairs={{0,3},{1,2},{2,1},{3,0},{4,7},{5,6},{6,5},{7,4},{8,11},{9,10},{10,... | collective-permute-start | bytes 393224 | tf_op jit(solution)/shard_map/ppermute | solution.py:225

commit v2 on v1

v2 whole, which is shorter than its diff:
```python
import functools
import math

import jax
import jax.numpy as jnp
import numpy as np
from jax import lax
from jax.experimental import pallas as pl
from jax.experimental.pallas import tpu as pltpu
from jax.sharding import PartitionSpec as P

NF = 512
VMEM = pl.BlockSpec(memory_space=pltpu.VMEM)
SMEM = pl.BlockSpec(memory_space=pltpu.SMEM)
ANY = pl.BlockSpec(memory_space=pl.ANY)
HBM = pl.BlockSpec(memory_space=pltpu.HBM)
COST = pl.CostEstimate(flops=0, bytes_accessed=0, transcendentals=0)


def room(*arrays):
    need = 2**20
    for a in arrays:
        *lead, rows, columns = (1, 1, *a.shape)
        rows, columns = -(-rows // 16) * 16, -(-columns // 128) * 128
        need += math.prod(lead) * rows * columns * a.dtype.itemsize
    return pltpu.CompilerParams(vmem_limit_bytes=need)


def order(arrays, after):
    count = len(arrays)

    def kernel(*refs):
        del refs

    return pl.pallas_call(
        kernel,
        out_shape=[jax.ShapeDtypeStruct(a.shape, a.dtype) for a in arrays],
        in_specs=[ANY] * (count + len(after)),
        out_specs=[ANY] * count,
        input_output_aliases={i: i for i in range(count)},
        compiler_params=room(),
        cost_estimate=COST,
        name="order",
    )(*arrays, *after)


def tables_kernel(angles_ref, high_ref, low_ref):
    _, parts, _, bins = angles_ref.shape
    samples = high_ref.shape[1]
    coarse = samples // STEPS

    def table_rows(a, _):
        for p in range(parts):
            cos_a, sin_a = angles_ref[0, p, pl.ds(a, 1), :], angles_ref[1, p, pl.ds(a, 1), :]
            cos_b, sin_b = angles_ref[0, p, coarse:], angles_ref[1, p, coarse:]
            span = pl.ds(pl.multiple_of(a * STEPS, STEPS), STEPS)
            cosine = cos_a * cos_b - sin_a * sin_b
            both = jnp.concatenate([cosine, -(sin_a * cos_b + cos_a * sin_b)], axis=1)
            high = both.astype(jnp.bfloat16)
            high_ref[p, span, :] = high
            low_ref[p, span, :] = (both - high.astype(jnp.float32)).astype(jnp.bfloat16)
        return 0

    lax.fori_loop(0, coarse, table_rows, 0)


STEPS = 32


def tables(samples, bins, parts):
    times = np.concatenate([np.arange(samples // STEPS) * STEPS, np.arange(STEPS)]).astype(np.int64)
    freqs = np.arange(bins, dtype=np.int64)[None, :]
    phases = (times[:, None] * freqs % samples) * (2.0 * math.pi / samples)
    angles = np.stack([np.cos(phases), np.sin(phases)]).astype(np.float32)
    part = bins // parts
    angles = angles.reshape(2, len(times), parts, part).transpose(0, 2, 1, 3)
    angles = jnp.asarray(angles)
    out = [jax.ShapeDtypeStruct((parts, samples, 2 * part), jnp.bfloat16)] * 2
    return pl.pallas_call(
        tables_kernel,
        out_shape=out,
        in_specs=[VMEM],
        out_specs=[VMEM] * 2,
        compiler_params=room(angles, *out),
        cost_estimate=COST,
        name="tables",
    )(angles)


def tapers(obliquity, lowest, highest, first, rows, ramp, bins):
    receiver = first + lax.broadcasted_iota(jnp.int32, (lowest.shape[0], rows, bins), 1)
    lowest, highest = lowest[:, None, None], highest[:, None, None]
    rising = jnp.clip((receiver - lowest + 1).astype(jnp.float32) / ramp, 0.0, 1.0)
    falling = jnp.clip((highest - receiver + 1).astype(jnp.float32) / ramp, 0.0, 1.0)
    return obliquity[:, None, None] * rising * falling


def transform_kernel(steps, tapered, added, axis, chosen, points, spans, *refs):
    piece_refs, (high_ref, low_ref), refs = refs[: len(steps)], refs[len(steps) : len(steps) + 2], refs[len(steps) + 2 :]
    added_refs, (x_high, x_low) = refs[tapered : tapered + added], refs[-2:]
    pairs = high_ref.shape[0] // 2
    out_refs = refs[-2 - len(spans) : -2]
    _, rows, width = piece_refs[0].shape
    bins = out_refs[0].shape[-1]
    me_src, me_time, me_sp = (lax.axis_index(a) for a in ("src", axis, "sp"))

    def own(i):
        return pl.ds((me_src ^ chosen[i]) * points, points)

    for j, piece_ref in enumerate(piece_refs):
        for i in range(len(chosen)):
            span = slice(None) if piece_ref.shape[0] == points else own(i)
            x = piece_ref[span].reshape(points * rows, width)
            high = x.astype(jnp.bfloat16)
            low = (x - high.astype(jnp.float32)).astype(jnp.bfloat16)
            place = slice(i * points * rows, (i + 1) * points * rows)
            x_high[place, j * width : (j + 1) * width] = high
            x_low[place, j * width : (j + 1) * width] = low
    for k in range(2 * pairs):
        part = me_sp ^ k
        spectrum = 0.0
        for j, step in enumerate(steps):
            times = pl.ds(pl.multiple_of((me_time ^ step) * width, width), width)
            w_high, w_low = high_ref[part, times, :], low_ref[part, times, :]
            high, low = (x[:, j * width : (j + 1) * width] for x in (x_high, x_low))
            spectrum += (
                jnp.dot(high, w_high, preferred_element_type=jnp.float32)
                + jnp.dot(low, w_high, preferred_element_type=jnp.float32)
                + jnp.dot(high, w_low, preferred_element_type=jnp.float32)
            )
        for c in range(2):
            half = spectrum[:, c * bins : (c + 1) * bins]
            if tapered:
                half = half * refs[0][own(0)].reshape(points * rows, bins)
            for i, (q, first, count) in enumerate(spans):
                if q == k // 2:
                    value = half[first : first + count]
                    out_refs[i][k % 2, c] = value + added_refs[i][k % 2, c] if added else value


def transform(pieces, table, axis, chosen, points, cuts, taper=(), added=(), after=()):
    steps, pieces = tuple(pieces), list(pieces.values())
    rows, width = pieces[0].shape[1:]
    bins = table[0].shape[2] // 2
    total = points * len(chosen) * rows
    spans = [(q, i * (total // n), total // n) for q, n in enumerate(cuts) for i in range(n)]
    out = [jax.ShapeDtypeStruct((2, 2, count, bins), jnp.float32) for _, _, count in spans]
    split = [jax.ShapeDtypeStruct((total, len(steps) * width), jnp.bfloat16)] * 2
    spectrum = jax.ShapeDtypeStruct((total, 2 * bins), jnp.float32)
    return pl.pallas_call(
        lambda *refs: transform_kernel(steps, len(taper), len(added), axis, chosen, points, spans, *refs),
        out_shape=out,
        in_specs=[VMEM] * (len(pieces) + 2 + len(taper) + len(added)) + [ANY] * len(after),
        out_specs=[VMEM] * len(spans),
        scratch_shapes=[pltpu.VMEM(x.shape, x.dtype) for x in split],
        compiler_params=room(*pieces, *table, *taper, *added, *out, *split, *[spectrum] * 4),
        cost_estimate=COST,
        name="transform",
    )(*pieces, *table, *taper, *added, *after)


GROUP = 2


def product_kernel(terms, count, carried, rows, *refs):
    in_refs, total_refs, out_ref = refs[:count], refs[count : count + carried], refs[-1]
    shots, receivers = rows
    bins = out_ref.shape[-1]

    def shot_group(g, _):
        def add_point(term, x, sums):
            half, shot, shot_row, receiver, _ = term
            span = pl.ds(pl.multiple_of(x * receivers, 8), receivers)
            r_re, r_im = in_refs[receiver][half, 0, span, :], in_refs[receiver][half, 1, span, :]
            r_sum = r_re + r_im
            new = []
            for i in range(GROUP):
                line = pl.ds(shot_row + x * shots + g * GROUP + i, 1)
                s_re, s_im = in_refs[shot][half, 0, line, :], in_refs[shot][half, 1, line, :]
                s_sum = s_re + s_im
                a, b, c = sums[3 * i : 3 * i + 3]
                new += [a + s_re * r_re, b + s_im * r_im, c + s_sum * r_sum]
            return tuple(new)

        sums = (jnp.zeros((receivers, bins), jnp.float32),) * (3 * GROUP)
        for term in terms:
            step = lambda x, s, term=term: add_point(term, x, s)
            sums = lax.fori_loop(0, term[4], step, sums, unroll=2 if term[4] % 2 == 0 else 1)
        for i in range(GROUP):
            a, b, c = sums[3 * i : 3 * i + 3]
            real, imaginary = a - b, c - a - b
            if carried:
                real += total_refs[0][0, g * GROUP + i]
                imaginary += total_refs[0][1, g * GROUP + i]
            out_ref[0, g * GROUP + i] = real
            out_ref[1, g * GROUP + i] = imaginary
        return 0

    lax.fori_loop(0, shots // GROUP, shot_group, 0)


def product(terms, shots, receivers, total=None, after=()):
    blocks, described = [], []

    def place(block):
        for i, known in enumerate(blocks):
            if known is block:
                return i
        blocks.append(block)
        return len(blocks) - 1

    for half, shot, shot_row, receiver, points in terms:
        described.append((half, place(shot), shot_row, place(receiver), points))
    bins = blocks[0].shape[-1]
    carried = () if total is None else (total,)
    points = sum(term[4] for term in described)
    out = jax.ShapeDtypeStruct((2, shots, receivers, bins), jnp.float32)
    return pl.pallas_call(
        lambda *refs: product_kernel(described, len(blocks), len(carried), (shots, receivers), *refs),
        out_shape=out,
        in_specs=[VMEM] * (len(blocks) + len(carried)) + [ANY] * len(after),
        out_specs=VMEM,
        compiler_params=room(*blocks, *carried, out),
        cost_estimate=COST,
        name="product",
    )(*blocks, *carried, *after)


def exchange(block, axis, size, step):
    return lax.ppermute(block, axis, [(i, i ^ step) for i in range(size)])


def gather(block, axis, size, stop=1):
    pieces, step = {0: block}, size // 2
    while step >= stop:
        pieces |= {j ^ step: exchange(piece, axis, size, step) for j, piece in pieces.items()}
        step //= 2
    return [pieces[j] for j in range(0, size, stop)]


def solution(mesh):
    n_src, n_rcv, n_sp = mesh.shape["src"], mesh.shape["rcv"], mesh.shape["sp"]

    def local(shot_traces, surface_receiver_traces, obliquity, lowest_receiver_index, hi_index):
        points, receivers = surface_receiver_traces.shape[:2]
        shots = shot_traces.shape[1]
        samples = shot_traces.shape[2] * n_rcv
        part = points // n_src
        me = lax.axis_index("src")

        def own(array, j):
            return lax.dynamic_slice_in_dim(array, (me ^ j) * part, part)

        receiver_pieces = [own(surface_receiver_traces, 0)] + [
            exchange(own(surface_receiver_traces, j), "src", n_src, j) for j in range(1, n_src)
        ]
        table = tables(samples, NF, n_sp)
        taper = tapers(
            obliquity,
            lowest_receiver_index,
            hi_index,
            lax.axis_index("rcv") * receivers,
            receivers,
            receivers * n_rcv // 8,
            NF // n_sp,
        )

        def cross(blocks, count):
            return [
                block if i < 1 else exchange(block, "sp", n_sp, 2 * (1 + (i - 1) // count))
                for i, block in enumerate(blocks)
            ]

        def core(block):
            return exchange(block, "sp", n_sp, 1)

        def late(array, *after):
            return order([array], after)[0]

        chips = range(n_sp // 2)
        receiver_pieces = dict(enumerate(receiver_pieces))
        out = transform(receiver_pieces, table, "src", (0,), part, [1] * len(chips), (taper,))
        token, r_first = out[0], cross(out, 1)
        r_near = [gather(r_first[0], "src", n_src)]
        r_far = [[core(r_first[0])]]

        even = gather(shot_traces, "rcv", n_rcv, 2)
        beside = exchange(shot_traces, "rcv", n_rcv, 1)
        passed = order(even[1:], [token, beside])
        near = {0: shot_traces, 1: beside} | {2 * j: piece for j, piece in enumerate(passed, 1)}
        last = {2 * j + 1: exchange(piece, "rcv", n_rcv, 1) for j, piece in enumerate(passed, 1)}
        shot_transform = functools.partial(
            transform, axis="rcv", chosen=tuple(range(n_src)), points=part, cuts=[1] + [2] * (len(chips) - 1)
        )
        out = shot_transform(near, table)
        out = shot_transform(last, table, added=out, after=(r_first[-1], r_far[0][0]))
        token, s_near = out[0], cross(out, 2)
        s_far = [core(s_near[0])]
        for q in chips[1:]:
            r_near.append(gather(late(r_first[q], token), "src", n_src))
        r_far[0] += [core(late(block, token)) for block in r_near[0][1:]]

        held = n_src // 2

        def terms(chunk, pair, half):
            shot = (s_near, s_far)[half]
            block = shot[2 * pair - 1 + chunk] if pair else shot[0]
            first = 0 if pair else chunk * held
            return [
                (
                    half,
                    block,
                    (first + j) * part * shots,
                    (r_near, r_far)[half][pair][chunk * held + j],
                    part,
                )
                for j in range(held)
            ]

        pairs = chips[1:]
        first = [(0, 0, 0), (0, 0, 1), (1, 0, 0), (1, 0, 1)]
        total = product(sum([terms(*x) for x in first], []), shots, receivers)
        for q in pairs:
            s_near[2 * q - 1] = late(s_near[2 * q - 1], total)
        total = product(sum([terms(0, q, 0) for q in pairs], []), shots, receivers, total)
        for q in pairs:
            s_near[2 * q] = late(s_near[2 * q], total)
            s_far += [core(s_near[2 * q - 1]), core(s_near[2 * q])]
            r_far.append([core(late(block, total)) for block in r_near[q]])
        second = [(0, q, 1) for q in pairs] + [(1, q, 0) for q in pairs]
        after = [r_far[q][-1] for q in pairs]
        total = product(sum([terms(*x) for x in second], []), shots, receivers, total, after)
        total = product(sum([terms(1, q, 1) for q in pairs], []), shots, receivers, total)
        return total.transpose(3, 0, 1, 2)

    placed = (P("sp", "src", "rcv"), P("sp", "rcv", "src"), P("sp"), P("sp"), P("sp"))
    return jax.shard_map(
        local, mesh=mesh, in_specs=placed, out_specs=P("sp", None, "src", "rcv"), check_vma=False
    )
```

time: 49.1 us -> 45.4 us (0.925)
  waiting for transfers between devices: 10.8 us -> 15.2 us
  starting transfers between devices: 18.8 us -> 15.2 us
  Pallas kernels: 14.4 us -> 11.7 us
  local copies, waits for them, and re-layouts: 4.73 us -> 2.06 us
  other arithmetic: 0 us -> 0.81 us
    ppermute x20 -> x16, waiting for transfers between devices: 10.8 us -> 15.2 us  [exchange(): return lax.ppermute(block, axis, [(i, i ^ step) for i in range(size)])]
    unnamed x16 -> x6, local copies, waits for them, and re-layouts: 4.73 us -> 0.99 us
    ppermute x20 -> x16, starting transfers between devices: 18.8 us -> 15.2 us  [exchange(): return lax.ppermute(block, axis, [(i, i ^ step) for i in range(size)])]
    pallas_call x5 -> x11, Pallas kernels: 6.83 us -> 4.09 us  [the longest x3 2.95 us: transform(): pl.pallas_call(lambda *refs: transform_kernel(steps, len(taper), len(adde...]
    dynamic_slice x0 -> x1, local copies, waits for them, and re-layouts: none -> 1.07 us  [own(): return lax.dynamic_slice_in_dim(array, (me ^ j) * part, part)]
    mul x0 -> x1, other arithmetic: none -> 0.81 us  [tapers(): return obliquity[:, None, None] * rising * falling]
  transfers between devices with their start and end apart: 20 -> 16, of which waited for: 6 -> 6; matrix products, arithmetic and copies ran while one was open for 0% -> 4% of each run, Pallas kernels for 21% -> 22%
where the time goes in v2:
time: 45.4 us; the launch traced here: 45.2 us
  starting transfers between devices  15.2 us (33%)
  waiting for transfers between devices  15.2 us (33%)
  Pallas kernels  11.7 us (26%)
  local copies, waits for them, and re-layouts  2.06 us (5%)
  other arithmetic  0.81 us (2%)
    ppermute x16, starting transfers between devices, exchange(): return lax.ppermute(block, axis, [(i, i ^ step) for i in range(size)])  15.2 us
    ppermute x16, waiting for transfers between devices, exchange(): return lax.ppermute(block, axis, [(i, i ^ step) for i in range(size)])  15.2 us
    pallas_call x4, Pallas kernels, product(): pl.pallas_call(lambda *refs: product_kernel(described, len(blocks), len(c...  7.61 us
    pallas_call x3, Pallas kernels, transform(): pl.pallas_call(lambda *refs: transform_kernel(steps, len(taper), len(adde...  2.95 us
    pallas_call x1, Pallas kernels, tables(): pl.pallas_call(tables_kernel, out_shape=out, in_specs=[VMEM], out_specs=[...  1.13 us
    dynamic_slice x1, local copies, waits for them, and re-layouts, own(): return lax.dynamic_slice_in_dim(array, (me ^ j) * part, part)  1.07 us
    unnamed x6, local copies, waits for them, and re-layouts  0.99 us
  transfers between devices with their start and end apart: 16, of which 6 were waited for; matrix products, arithmetic and copies ran while one was open for 4% of the time, Pallas kernels for 22%

profile of v2, /device:TPU:0, one launch (start us, length us, event | category | flops | bytes accessed | tf_op | source)
XLA Modules:
  0.0 45.2 jit_solution(3690675379717457984)
XLA Ops:
  0.0 3.0 %collective-permute-start.2 = (f32[8,32,256]{2,1,0:T(8,128)}, f32[8,32,256]{2,1,0:T(8,128)S(1)}, u32[]{:S(2)}, u32[]{:S(2)}) collective-permute-start(f32[8,32,256]{2,1,0:T(8,128)} %refs_0_.1), channel_id=1, source_target_pairs={{0,4},{4,0},{8,12},{12,8},{1,5},{5,1},{9,13},{13,9},{2,6},{6,2},{1... | collective-permute-start | bytes 786440 | tf_op jit(solution)/shard_map/ppermute | solution.py:230
  3.0 2.6 %collective-permute-start = (f32[8,32,256]{2,1,0:T(8,128)}, f32[8,32,256]{2,1,0:T(8,128)S(1)}, u32[]{:S(2)}, u32[]{:S(2)}) collective-permute-start(f32[8,32,256]{2,1,0:T(8,128)} %refs_0_.1), channel_id=1, source_target_pairs={{0,8},{4,12},{8,0},{12,4},{1,9},{5,13},{9,1},{13,5},{2,10},{6,14},... | collective-permute-start | bytes 786440 | tf_op jit(solution)/shard_map/ppermute | solution.py:230
  5.6 1.1 %constant_dynamic-slice_fusion = (f32[4,32,512]{2,1,0:T(8,128)S(1)}, f32[4,32,512]{2,1,0:T(8,128)S(1)}) fusion(f32[8,32,512]{2,1,0:T(8,128)} %param.7, s32[]{:T(128)S(6)} %select_n.7, s32[]{:T(128)S(6)} %select_n.6), kind=kLoop, calls=%fused_computation.2 | loop fusion | bytes 1048584 | tf_op jit(solution)/shard_map/dynamic_slice | solution.py:252
  6.7 1.6 %collective-permute-start.1 = (f32[4,32,512]{2,1,0:T(8,128)S(1)}, f32[4,32,512]{2,1,0:T(8,128)S(1)}, u32[]{:S(2)}, u32[]{:S(2)}) collective-permute-start(f32[4,32,512]{2,1,0:T(8,128)S(1)} %get-tuple-element.25), channel_id=1, source_target_pairs={{0,16},{16,0},{1,17},{17,1},{2,18},{18,2},{3,19},{19,3},{4,20},{20... | collective-permute-start | bytes 786440 | tf_op jit(solution)/shard_map/ppermute | solution.py:230
  8.3 0.0 copy-start.1
  8.3 0.9 %copy-done.1 = f32[2,4,64,128]{3,2,1,0:T(8,128)S(1)} copy-done((f32[2,4,64,128]{3,2,1,0:T(8,128)S(1)}, f32[2,4,64,128]{3,2,1,0:T(8,128)}, u32[]{:S(2)}) %copy-start.1) | copy-done | bytes 262168
  9.2 1.1 %tables.1 = (bf16[4,1024,256]{2,1,0:T(8,128)(2,1)S(1)}, bf16[4,1024,256]{2,1,0:T(8,128)(2,1)S(1)}) custom-call(f32[2,4,64,128]{3,2,1,0:T(8,128)S(1)} %copy-done.1), custom_call_target="tpu_custom_call" | custom-call | tf_op jit(solution)/shard_map/tables/pallas_call | solution.py:79
  10.3 0.8 %clamp_multiply_fusion.refs_4_ = f32[8,32,128]{2,1,0:T(8,128)S(1)} fusion(s32[8]{0:T(128)} %param.10, s32[8]{0:T(128)} %param.9, s32[32]{0:T(128)S(1)} %iota_add_fusion, f32[8]{0:T(128)} %param.8), kind=kLoop, calls=%fused_computation | loop fusion | flops 393216 | bytes 131296 | tf_op jit(solution)/shard_map/mul | solution.py:95
  11.2 3.1 %collective-permute-done.1.refs_1_ = f32[4,32,512]{2,1,0:T(8,128)S(1)} collective-permute-done((f32[4,32,512]{2,1,0:T(8,128)S(1)}, f32[4,32,512]{2,1,0:T(8,128)S(1)}, u32[]{:S(2)}, u32[]{:S(2)}) %collective-permute-start.1) | collective-permute-done | bytes 262176 | tf_op jit(solution)/shard_map/ppermute | solution.py:230
  14.2 0.0 copy-start
  14.2 1.0 %transform.3 = (f32[2,2,128,128]{3,2,1,0:T(8,128)S(1)}, f32[2,2,128,128]{3,2,1,0:T(8,128)S(1)}) custom-call(f32[4,32,512]{2,1,0:T(8,128)S(1)} %get-tuple-element.26.refs_0_, f32[4,32,512]{2,1,0:T(8,128)S(1)} %collective-permute-done.1.refs_1_, bf16[4,1024,256]{2,1,0:T(8,128)(2,1)S(1)} %get-tuple-element.15.refs_2_.refs_3_.refs_1_, ...), custom_call_target="tpu_custom_call" | custom-call | tf_op jit(solution)/shard_map/transform/pallas_call | solution.py:150
  15.2 0.1 collective-permute-start.5
  15.3 0.0 collective-permute-done.2.refs_2_.refs_1_
  15.3 2.2 %collective-permute-done.refs_0_ = f32[8,32,256]{2,1,0:T(8,128)S(1)} collective-permute-done((f32[8,32,256]{2,1,0:T(8,128)}, f32[8,32,256]{2,1,0:T(8,128)S(1)}, u32[]{:S(2)}, u32[]{:S(2)}) %collective-permute-start) | collective-permute-done | bytes 262176 | tf_op jit(solution)/shard_map/ppermute | solution.py:230
  17.6 0.4 collective-permute-start.3
  18.0 1.5 %collective-permute-start.4 = (f32[2,2,128,128]{3,2,1,0:T(8,128)S(1)}, f32[2,2,128,128]{3,2,1,0:T(8,128)S(1)}, u32[]{:S(2)}, u32[]{:S(2)}) collective-permute-start(f32[2,2,128,128]{3,2,1,0:T(8,128)S(1)} %get-tuple-element.21), channel_id=1, source_target_pairs={{0,2},{1,3},{2,0},{3,1},{4,6},{5,7},{6,4},{7,5},{8,10},{9,11},{10,... | collective-permute-start | bytes 786440 | tf_op jit(solution)/shard_map/ppermute | solution.py:230
  19.5 1.5 %collective-permute-start.9 = (f32[2,2,128,128]{3,2,1,0:T(8,128)S(1)}, f32[2,2,128,128]{3,2,1,0:T(8,128)S(1)}, u32[]{:S(2)}, u32[]{:S(2)}) collective-permute-start(f32[2,2,128,128]{3,2,1,0:T(8,128)S(1)} %get-tuple-element.17.refs_1_), channel_id=1, source_target_pairs={{0,16},{16,0},{1,17},{17,1},{2,18},{18,2},{3,19},{19,3},{4,20},{20... | collective-permute-start | bytes 786440 | tf_op jit(solution)/shard_map/ppermute | solution.py:230
  21.0 0.0 copy-done
  21.0 1.4 %transform.4 = (f32[2,2,256,128]{3,2,1,0:T(8,128)S(1)}, f32[2,2,128,128]{3,2,1,0:T(8,128)S(1)}, f32[2,2,128,128]{3,2,1,0:T(8,128)S(1)}) custom-call(f32[8,32,256]{2,1,0:T(8,128)S(1)} %copy-done, f32[8,32,256]{2,1,0:T(8,128)S(1)} %collective-permute-done.2.refs_2_.refs_1_, f32[8,32,256]{2,1,0:T(8,128)S(1)} %order.7.refs_2_, ...), custom_call_target="tpu_custom_call" | custom-call | tf_op jit(solution)/shard_map/transform/pallas_call | solution.py:150
  22.4 1.6 %collective-permute-done.3.refs_0_ = f32[8,32,256]{2,1,0:T(8,128)S(1)} collective-permute-done((f32[8,32,256]{2,1,0:T(8,128)S(1)}, f32[8,32,256]{2,1,0:T(8,128)S(1)}, u32[]{:S(2)}, u32[]{:S(2)}) %collective-permute-start.3) | collective-permute-done | bytes 262176 | tf_op jit(solution)/shard_map/ppermute | solution.py:230
  24.0 0.0 collective-permute-done.5.refs_7_.refs_3_
  24.0 0.8 %collective-permute-done.4.refs_6_.refs_0_ = f32[2,2,128,128]{3,2,1,0:T(8,128)S(1)} collective-permute-done((f32[2,2,128,128]{3,2,1,0:T(8,128)S(1)}, f32[2,2,128,128]{3,2,1,0:T(8,128)S(1)}, u32[]{:S(2)}, u32[]{:S(2)}) %collective-permute-start.4) | collective-permute-done | bytes 262176 | tf_op jit(solution)/shard_map/ppermute | solution.py:230
  24.9 0.6 %transform.5 = (f32[2,2,256,128]{3,2,1,0:T(8,128)S(1)}, f32[2,2,128,128]{3,2,1,0:T(8,128)S(1)}, f32[2,2,128,128]{3,2,1,0:T(8,128)S(1)}) custom-call(f32[8,32,256]{2,1,0:T(8,128)S(1)} %collective-permute-done.3.refs_0_, bf16[4,1024,256]{2,1,0:T(8,128)(2,1)S(1)} %get-tuple-element.15.refs_2_.refs_3_.refs_1_, ...), custom_call_target="tpu_custom_call" | custom-call | tf_op jit(solution)/shard_map/transform/pallas_call | solution.py:150
  25.4 0.1 collective-permute-start.8
  25.5 1.6 %collective-permute-start.12 = (f32[2,2,128,128]{3,2,1,0:T(8,128)S(1)}, f32[2,2,128,128]{3,2,1,0:T(8,128)S(1)}, u32[]{:S(2)}, u32[]{:S(2)}) collective-permute-start(f32[2,2,128,128]{3,2,1,0:T(8,128)S(1)} %order.10.refs_1_.refs_0_), channel_id=1, source_target_pairs={{0,16},{16,0},{1,17},{17,1},{2,18},{18,2},{3,19},{19,3},{4,20},{20... | collective-permute-start | bytes 786440 | tf_op jit(solution)/shard_map/ppermute | solution.py:230
  27.1 0.0 collective-permute-done.9.refs_4_
  27.1 0.2 collective-permute-start.10
  27.4 1.5 %collective-permute-start.7 = (f32[2,2,128,128]{3,2,1,0:T(8,128)S(1)}, f32[2,2,128,128]{3,2,1,0:T(8,128)S(1)}, u32[]{:S(2)}, u32[]{:S(2)}) collective-permute-start(f32[2,2,128,128]{3,2,1,0:T(8,128)S(1)} %get-tuple-element.23), channel_id=1, source_target_pairs={{0,2},{1,3},{2,0},{3,1},{4,6},{5,7},{6,4},{7,5},{8,10},{9,11},{10,... | collective-permute-start | bytes 786440 | tf_op jit(solution)/shard_map/ppermute | solution.py:230
  28.9 0.5 %collective-permute-start.6 = (f32[2,2,128,128]{3,2,1,0:T(8,128)S(1)}, f32[2,2,128,128]{3,2,1,0:T(8,128)S(1)}, u32[]{:S(2)}, u32[]{:S(2)}) collective-permute-start(f32[2,2,128,128]{3,2,1,0:T(8,128)S(1)} %get-tuple-element.22), channel_id=1, source_target_pairs={{0,2},{1,3},{2,0},{3,1},{4,6},{5,7},{6,4},{7,5},{8,10},{9,11},{10,... | collective-permute-start | bytes 786440 | tf_op jit(solution)/shard_map/ppermute | solution.py:230
  29.4 4.9 %collective-permute-done.12.refs_3_ = f32[2,2,128,128]{3,2,1,0:T(8,128)S(1)} collective-permute-done((f32[2,2,128,128]{3,2,1,0:T(8,128)S(1)}, f32[2,2,128,128]{3,2,1,0:T(8,128)S(1)}, u32[]{:S(2)}, u32[]{:S(2)}) %collective-permute-start.12) | collective-permute-done | bytes 262176 | tf_op jit(solution)/shard_map/ppermute | solution.py:230
  34.3 0.0 collective-permute-done.10.refs_5_
  34.3 0.0 collective-permute-done.8.refs_2_
  34.3 3.1 %product.4.refs_1_.refs_2_ = f32[2,32,32,128]{3,2,1,0:T(8,128)S(1)} custom-call(f32[2,2,256,128]{3,2,1,0:T(8,128)S(1)} %get-tuple-element.24.refs_1_.refs_0_, f32[2,2,128,128]{3,2,1,0:T(8,128)S(1)} %get-tuple-element.17.refs_1_, f32[2,2,256,128]{3,2,1,0:T(8,128)S(1)} %collective-permute-done.8.refs_2_, ...), custom_call_target="tpu_custom_call" | custom-call | tf_op jit(solution)/shard_map/product/pallas_call | solution.py:218
  37.4 0.0 collective-permute-done.7.refs_0_
  37.4 0.9 %product.5.refs_1_.refs_4_ = f32[2,32,32,128]{3,2,1,0:T(8,128)S(1)} custom-call(f32[2,2,128,128]{3,2,1,0:T(8,128)S(1)} %order.9.refs_0_, f32[2,2,128,128]{3,2,1,0:T(8,128)S(1)} %order.10.refs_1_.refs_0_, f32[2,32,32,128]{3,2,1,0:T(8,128)S(1)} %product.4.refs_1_.refs_2_), custom_call_target="tpu_custom_call" | custom-call | tf_op jit(solution)/shard_map/product/pallas_call | solution.py:218
  38.4 0.1 collective-permute-start.14
  38.4 0.5 %collective-permute-start.15 = (f32[2,2,128,128]{3,2,1,0:T(8,128)S(1)}, f32[2,2,128,128]{3,2,1,0:T(8,128)S(1)}, u32[]{:S(2)}, u32[]{:S(2)}) collective-permute-start(f32[2,2,128,128]{3,2,1,0:T(8,128)S(1)} %order.13), channel_id=1, source_target_pairs={{0,1},{1,0},{2,3},{3,2},{4,5},{5,4},{6,7},{7,6},{8,9},{9,8},{10,11... | collective-permute-start | bytes 786440 | tf_op jit(solution)/shard_map/ppermute | solution.py:230
  38.9 0.1 collective-permute-start.13
  39.0 2.5 %collective-permute-done.6.refs_0_ = f32[2,2,128,128]{3,2,1,0:T(8,128)S(1)} collective-permute-done((f32[2,2,128,128]{3,2,1,0:T(8,128)S(1)}, f32[2,2,128,128]{3,2,1,0:T(8,128)S(1)}, u32[]{:S(2)}, u32[]{:S(2)}) %collective-permute-start.6) | collective-permute-done | bytes 262176 | tf_op jit(solution)/shard_map/ppermute | solution.py:230
  41.5 0.0 collective-permute-start.11
  41.5 0.0 collective-permute-done.15.refs_1_
  41.5 0.0 collective-permute-done.13.refs_5_.refs_1_
  41.5 0.0 collective-permute-done.14.refs_0_
  41.6 1.7 %product.6.refs_2_ = f32[2,32,32,128]{3,2,1,0:T(8,128)S(1)} custom-call(f32[2,2,128,128]{3,2,1,0:T(8,128)S(1)} %collective-permute-done.14.refs_0_, f32[2,2,128,128]{3,2,1,0:T(8,128)S(1)} %collective-permute-done.15.refs_1_, f32[2,2,128,128]{3,2,1,0:T(8,128)S(1)} %order.11.refs_2_, f32[2,2,128,128]{3,2,1,0:T(8,128)S(1)} %collective-permute-done.12.refs_3_, ...), custom_call_target="tpu_custom_call" | custom-call | tf_op jit(solution)/shard_map/product/pallas_call | solution.py:218
  43.2 0.0 collective-permute-done.11.refs_0_
  43.2 1.9 %product.7 = f32[2,32,32,128]{3,2,1,0:T(8,128)} custom-call(f32[2,2,128,128]{3,2,1,0:T(8,128)S(1)} %collective-permute-done.11.refs_0_, f32[2,2,128,128]{3,2,1,0:T(8,128)S(1)} %collective-permute-done.13.refs_5_.refs_1_, f32[2,32,32,128]{3,2,1,0:T(8,128)S(1)} %product.6.refs_2_), custom_call_target="tpu_custom_call" | custom-call | tf_op jit(solution)/shard_map/product/pallas_call | solution.py:218
  (10 shorter events, 0.0 us)
Async XLA Ops:
  0.0 15.3 %collective-permute-start.2 = (f32[8,32,256]{2,1,0:T(8,128)}, f32[8,32,256]{2,1,0:T(8,128)S(1)}, u32[]{:S(2)}, u32[]{:S(2)}) collective-permute-start(f32[8,32,256]{2,1,0:T(8,128)} %refs_0_.1), channel_id=1, source_target_pairs={{0,4},{4,0},{8,12},{12,8},{1,5},{5,1},{9,13},{13,9},{2,6},{6,2},{1... | collective-permute-start | bytes 786440 | tf_op jit(solution)/shard_map/ppermute | solution.py:230
  3.0 14.6 %collective-permute-start = (f32[8,32,256]{2,1,0:T(8,128)}, f32[8,32,256]{2,1,0:T(8,128)S(1)}, u32[]{:S(2)}, u32[]{:S(2)}) collective-permute-start(f32[8,32,256]{2,1,0:T(8,128)} %refs_0_.1), channel_id=1, source_target_pairs={{0,8},{4,12},{8,0},{12,4},{1,9},{5,13},{9,1},{13,5},{2,10},{6,14},... | collective-permute-start | bytes 786440 | tf_op jit(solution)/shard_map/ppermute | solution.py:230
  6.7 7.6 %collective-permute-start.1 = (f32[4,32,512]{2,1,0:T(8,128)S(1)}, f32[4,32,512]{2,1,0:T(8,128)S(1)}, u32[]{:S(2)}, u32[]{:S(2)}) collective-permute-start(f32[4,32,512]{2,1,0:T(8,128)S(1)} %get-tuple-element.25), channel_id=1, source_target_pairs={{0,16},{16,0},{1,17},{17,1},{2,18},{18,2},{3,19},{19,3},{4,20},{20... | collective-permute-start | bytes 786440 | tf_op jit(solution)/shard_map/ppermute | solution.py:230
  8.3 0.9 %copy-start.1 = (f32[2,4,64,128]{3,2,1,0:T(8,128)S(1)}, f32[2,4,64,128]{3,2,1,0:T(8,128)}, u32[]{:S(2)}) copy-start(f32[2,4,64,128]{3,2,1,0:T(8,128)} %constant.32.clone.angles_ref) | copy-start | bytes 786436
  14.2 6.8 %copy-start = (f32[8,32,256]{2,1,0:T(8,128)S(1)}, f32[8,32,256]{2,1,0:T(8,128)}, u32[]{:S(2)}) copy-start(f32[8,32,256]{2,1,0:T(8,128)} %refs_0_.1) | copy-start | bytes 786436
  15.2 8.8 %collective-permute-start.5 = (f32[2,2,128,128]{3,2,1,0:T(8,128)S(1)}, f32[2,2,128,128]{3,2,1,0:T(8,128)S(1)}, u32[]{:S(2)}, u32[]{:S(2)}) collective-permute-start(f32[2,2,128,128]{3,2,1,0:T(8,128)S(1)} %get-tuple-element.17.refs_1_), channel_id=1, source_target_pairs={{0,1},{1,0},{2,3},{3,2},{4,5},{5,4},{6,7},{7,6},{8,9},{9,8},{10,11... | collective-permute-start | bytes 786440 | tf_op jit(solution)/shard_map/ppermute | solution.py:230
  17.6 6.5 %collective-permute-start.3 = (f32[8,32,256]{2,1,0:T(8,128)S(1)}, f32[8,32,256]{2,1,0:T(8,128)S(1)}, u32[]{:S(2)}, u32[]{:S(2)}) collective-permute-start(f32[8,32,256]{2,1,0:T(8,128)S(1)} %order.7.refs_2_), channel_id=1, source_target_pairs={{0,4},{4,0},{8,12},{12,8},{1,5},{5,1},{9,13},{13,9},{2,6},{6,2},{1... | collective-permute-start | bytes 786440 | tf_op jit(solution)/shard_map/ppermute | solution.py:230
  18.0 6.8 %collective-permute-start.4 = (f32[2,2,128,128]{3,2,1,0:T(8,128)S(1)}, f32[2,2,128,128]{3,2,1,0:T(8,128)S(1)}, u32[]{:S(2)}, u32[]{:S(2)}) collective-permute-start(f32[2,2,128,128]{3,2,1,0:T(8,128)S(1)} %get-tuple-element.21), channel_id=1, source_target_pairs={{0,2},{1,3},{2,0},{3,1},{4,6},{5,7},{6,4},{7,5},{8,10},{9,11},{10,... | collective-permute-start | bytes 786440 | tf_op jit(solution)/shard_map/ppermute | solution.py:230
  19.5 7.6 %collective-permute-start.9 = (f32[2,2,128,128]{3,2,1,0:T(8,128)S(1)}, f32[2,2,128,128]{3,2,1,0:T(8,128)S(1)}, u32[]{:S(2)}, u32[]{:S(2)}) collective-permute-start(f32[2,2,128,128]{3,2,1,0:T(8,128)S(1)} %get-tuple-element.17.refs_1_), channel_id=1, source_target_pairs={{0,16},{16,0},{1,17},{17,1},{2,18},{18,2},{3,19},{19,3},{4,20},{20... | collective-permute-start | bytes 786440 | tf_op jit(solution)/shard_map/ppermute | solution.py:230
  25.4 8.8 %collective-permute-start.8 = (f32[2,2,256,128]{3,2,1,0:T(8,128)S(1)}, f32[2,2,256,128]{3,2,1,0:T(8,128)S(1)}, u32[]{:S(2)}, u32[]{:S(2)}) collective-permute-start(f32[2,2,256,128]{3,2,1,0:T(8,128)S(1)} %get-tuple-element.24.refs_1_.refs_0_), channel_id=1, source_target_pairs={{0,1},{1,0},{2,3},{3,2},{4,5},{5,4},{6,7},{7,6},{8,9},{9,8},{10,11... | collective-permute-start | bytes 1572872 | tf_op jit(solution)/shard_map/ppermute | solution.py:230
  25.5 8.7 %collective-permute-start.12 = (f32[2,2,128,128]{3,2,1,0:T(8,128)S(1)}, f32[2,2,128,128]{3,2,1,0:T(8,128)S(1)}, u32[]{:S(2)}, u32[]{:S(2)}) collective-permute-start(f32[2,2,128,128]{3,2,1,0:T(8,128)S(1)} %order.10.refs_1_.refs_0_), channel_id=1, source_target_pairs={{0,16},{16,0},{1,17},{17,1},{2,18},{18,2},{3,19},{19,3},{4,20},{20... | collective-permute-start | bytes 786440 | tf_op jit(solution)/shard_map/ppermute | solution.py:230
  27.1 7.1 %collective-permute-start.10 = (f32[2,2,128,128]{3,2,1,0:T(8,128)S(1)}, f32[2,2,128,128]{3,2,1,0:T(8,128)S(1)}, u32[]{:S(2)}, u32[]{:S(2)}) collective-permute-start(f32[2,2,128,128]{3,2,1,0:T(8,128)S(1)} %order.8), channel_id=1, source_target_pairs={{0,1},{1,0},{2,3},{3,2},{4,5},{5,4},{6,7},{7,6},{8,9},{9,8},{10,11... | collective-permute-start | bytes 786440 | tf_op jit(solution)/shard_map/ppermute | solution.py:230
  27.4 10.0 %collective-permute-start.7 = (f32[2,2,128,128]{3,2,1,0:T(8,128)S(1)}, f32[2,2,128,128]{3,2,1,0:T(8,128)S(1)}, u32[]{:S(2)}, u32[]{:S(2)}) collective-permute-start(f32[2,2,128,128]{3,2,1,0:T(8,128)S(1)} %get-tuple-element.23), channel_id=1, source_target_pairs={{0,2},{1,3},{2,0},{3,1},{4,6},{5,7},{6,4},{7,5},{8,10},{9,11},{10,... | collective-permute-start | bytes 786440 | tf_op jit(solution)/shard_map/ppermute | solution.py:230
  28.9 12.7 %collective-permute-start.6 = (f32[2,2,128,128]{3,2,1,0:T(8,128)S(1)}, f32[2,2,128,128]{3,2,1,0:T(8,128)S(1)}, u32[]{:S(2)}, u32[]{:S(2)}) collective-permute-start(f32[2,2,128,128]{3,2,1,0:T(8,128)S(1)} %get-tuple-element.22), channel_id=1, source_target_pairs={{0,2},{1,3},{2,0},{3,1},{4,6},{5,7},{6,4},{7,5},{8,10},{9,11},{10,... | collective-permute-start | bytes 786440 | tf_op jit(solution)/shard_map/ppermute | solution.py:230
  38.4 3.2 %collective-permute-start.14 = (f32[2,2,128,128]{3,2,1,0:T(8,128)S(1)}, f32[2,2,128,128]{3,2,1,0:T(8,128)S(1)}, u32[]{:S(2)}, u32[]{:S(2)}) collective-permute-start(f32[2,2,128,128]{3,2,1,0:T(8,128)S(1)} %order.9.refs_0_), channel_id=1, source_target_pairs={{0,1},{1,0},{2,3},{3,2},{4,5},{5,4},{6,7},{7,6},{8,9},{9,8},{10,11... | collective-permute-start | bytes 786440 | tf_op jit(solution)/shard_map/ppermute | solution.py:230
  38.4 3.1 %collective-permute-start.15 = (f32[2,2,128,128]{3,2,1,0:T(8,128)S(1)}, f32[2,2,128,128]{3,2,1,0:T(8,128)S(1)}, u32[]{:S(2)}, u32[]{:S(2)}) collective-permute-start(f32[2,2,128,128]{3,2,1,0:T(8,128)S(1)} %order.13), channel_id=1, source_target_pairs={{0,1},{1,0},{2,3},{3,2},{4,5},{5,4},{6,7},{7,6},{8,9},{9,8},{10,11... | collective-permute-start | bytes 786440 | tf_op jit(solution)/shard_map/ppermute | solution.py:230
  38.9 2.6 %collective-permute-start.13 = (f32[2,2,128,128]{3,2,1,0:T(8,128)S(1)}, f32[2,2,128,128]{3,2,1,0:T(8,128)S(1)}, u32[]{:S(2)}, u32[]{:S(2)}) collective-permute-start(f32[2,2,128,128]{3,2,1,0:T(8,128)S(1)} %order.12), channel_id=1, source_target_pairs={{0,1},{1,0},{2,3},{3,2},{4,5},{5,4},{6,7},{7,6},{8,9},{9,8},{10,11... | collective-permute-start | bytes 786440 | tf_op jit(solution)/shard_map/ppermute | solution.py:230
  41.5 1.7 %collective-permute-start.11 = (f32[2,2,128,128]{3,2,1,0:T(8,128)S(1)}, f32[2,2,128,128]{3,2,1,0:T(8,128)S(1)}, u32[]{:S(2)}, u32[]{:S(2)}) collective-permute-start(f32[2,2,128,128]{3,2,1,0:T(8,128)S(1)} %order.11.refs_2_), channel_id=1, source_target_pairs={{0,1},{1,0},{2,3},{3,2},{4,5},{5,4},{6,7},{7,6},{8,9},{9,8},{10,11... | collective-permute-start | bytes 786440 | tf_op jit(solution)/shard_map/ppermute | solution.py:230

commit v3 on v2

--- a/solution.py
+++ b/solution.py
@@ -143,7 +143,10 @@
     rows, width = pieces[0].shape[1:]
     bins = table[0].shape[2] // 2
     total = points * len(chosen) * rows
-    spans = [(q, i * (total // n), total // n) for q, n in enumerate(cuts) for i in range(n)]
+    spans = []
+    for q, cut in enumerate(cuts):
+        edges = [0, *(point * rows for point in cut), total]
+        spans += [(q, start, stop - start) for start, stop in zip(edges, edges[1:])]
     out = [jax.ShapeDtypeStruct((2, 2, count, bins), jnp.float32) for _, _, count in spans]
     split = [jax.ShapeDtypeStruct((total, len(steps) * width), jnp.bfloat16)] * 2
     spectrum = jax.ShapeDtypeStruct((total, 2 * bins), jnp.float32)
@@ -159,47 +162,63 @@
     )(*pieces, *table, *taper, *added, *after)
 
 
-GROUP = 2
-
-
-def product_kernel(terms, count, carried, rows, *refs):
-    in_refs, total_refs, out_ref = refs[:count], refs[count : count + carried], refs[-1]
+GROUP = 4
+
+
+def product_kernel(terms, count, carried, rows, sends, *refs):
+    in_refs, total_refs = refs[:count], refs[count : count + carried]
     shots, receivers = rows
+    if sends:
+        send_ref, out_ref, sems = refs[-3:]
+    else:
+        out_ref = refs[-1]
     bins = out_ref.shape[-1]
 
-    def shot_group(g, _):
-        def add_point(term, x, sums):
-            half, shot, shot_row, receiver, _ = term
-            span = pl.ds(pl.multiple_of(x * receivers, 8), receivers)
-            r_re, r_im = in_refs[receiver][half, 0, span, :], in_refs[receiver][half, 1, span, :]
-            r_sum = r_re + r_im
-            new = []
+    def copy(g, c):
+        span = pl.ds(g * GROUP, GROUP)
+        return pltpu.make_async_copy(out_ref.at[c, span], send_ref.at[c, span], sems.at[g, c])
+
+    for number, (half, shot, shot_row, receiver, receiver_row, points) in enumerate(terms):
+        before = out_ref if number else total_refs[0] if carried else None
+
+        def shot_group(g, _):
+            sums = [jnp.zeros((receivers, bins), jnp.float32)] * (3 * GROUP)
+            for x in range(points):
+                span = slice(receiver_row + x * receivers, receiver_row + (x + 1) * receivers)
+                r_re, r_im = in_refs[receiver][half, 0, span, :], in_refs[receiver][half, 1, span, :]
+                r_sum = r_re + r_im
+                for i in range(GROUP):
+                    line = pl.ds(shot_row + x * shots + g * GROUP + i, 1)
+                    s_re, s_im = in_refs[shot][half, 0, line, :], in_refs[shot][half, 1, line, :]
+                    s_sum = s_re + s_im
+                    sums[3 * i] += s_re * r_re
+                    sums[3 * i + 1] += s_im * r_im
+                    sums[3 * i + 2] += s_sum * r_sum
             for i in range(GROUP):
-                line = pl.ds(shot_row + x * shots + g * GROUP + i, 1)
-                s_re, s_im = in_refs[shot][half, 0, line, :], in_refs[shot][half, 1, line, :]
-                s_sum = s_re + s_im
                 a, b, c = sums[3 * i : 3 * i + 3]
-                new += [a + s_re * r_re, b + s_im * r_im, c + s_sum * r_sum]
-            return tuple(new)
-
-        sums = (jnp.zeros((receivers, bins), jnp.float32),) * (3 * GROUP)
-        for term in terms:
-            step = lambda x, s, term=term: add_point(term, x, s)
-            sums = lax.fori_loop(0, term[4], step, sums, unroll=2 if term[4] % 2 == 0 else 1)
-        for i in range(GROUP):
-            a, b, c = sums[3 * i : 3 * i + 3]
-            real, imaginary = a - b, c - a - b
-            if carried:
-                real += total_refs[0][0, g * GROUP + i]
-                imaginary += total_refs[0][1, g * GROUP + i]
-            out_ref[0, g * GROUP + i] = real
-            out_ref[1, g * GROUP + i] = imaginary
-        return 0
-
-    lax.fori_loop(0, shots // GROUP, shot_group, 0)
-
-
-def product(terms, shots, receivers, total=None, after=()):
+                real, imaginary = a - b, c - a - b
+                if before is not None:
+                    real += before[0, g * GROUP + i]
+                    imaginary += before[1, g * GROUP + i]
+                out_ref[0, g * GROUP + i] = real
+                out_ref[1, g * GROUP + i] = imaginary
+            if sends and number == len(terms) - 1:
+                copy(g, 0).start()
+                copy(g, 1).start()
+            return 0
+
+        lax.fori_loop(0, shots // GROUP, shot_group, 0)
+    if sends:
+
+        def arrive(g, _):
+            copy(g, 0).wait()
+            copy(g, 1).wait()
+            return 0
+
+        lax.fori_loop(0, shots // GROUP, arrive, 0)
+
+
+def product(terms, shots, receivers, total=None, after=(), last=False):
     blocks, described = [], []
 
     def place(block):
@@ -209,17 +228,18 @@
         blocks.append(block)
         return len(blocks) - 1
 
-    for half, shot, shot_row, receiver, points in terms:
-        described.append((half, place(shot), shot_row, place(receiver), points))
+    for half, shot, shot_row, receiver, receiver_row, points in terms:
+        described.append((half, place(shot), shot_row, place(receiver), receiver_row, points))
     bins = blocks[0].shape[-1]
     carried = () if total is None else (total,)
-    points = sum(term[4] for term in described)
     out = jax.ShapeDtypeStruct((2, shots, receivers, bins), jnp.float32)
+    sends = [pltpu.VMEM(out.shape, out.dtype), pltpu.SemaphoreType.DMA((shots // GROUP, 2))]
     return pl.pallas_call(
-        lambda *refs: product_kernel(described, len(blocks), len(carried), (shots, receivers), *refs),
+        lambda *refs: product_kernel(described, len(blocks), len(carried), (shots, receivers), last, *refs),
         out_shape=out,
         in_specs=[VMEM] * (len(blocks) + len(carried)) + [ANY] * len(after),
-        out_specs=VMEM,
+        out_specs=HBM if last else VMEM,
+        scratch_shapes=sends if last else [],
         compiler_params=room(*blocks, *carried, out),
         cost_estimate=COST,
         name="product",
@@ -279,18 +299,19 @@
 
         chips = range(n_sp // 2)
         receiver_pieces = dict(enumerate(receiver_pieces))
-        out = transform(receiver_pieces, table, "src", (0,), part, [1] * len(chips), (taper,))
+        out = transform(receiver_pieces, table, "src", (0,), part, [()] * len(chips), (taper,))
         token, r_first = out[0], cross(out, 1)
         r_near = [gather(r_first[0], "src", n_src)]
         r_far = [[core(r_first[0])]]
 
+        cut = points - 3 * points // 8
         even = gather(shot_traces, "rcv", n_rcv, 2)
         beside = exchange(shot_traces, "rcv", n_rcv, 1)
-        passed = order(even[1:], [token, beside])
+        beside, *passed = order([beside, *even[1:]], [token])
         near = {0: shot_traces, 1: beside} | {2 * j: piece for j, piece in enumerate(passed, 1)}
         last = {2 * j + 1: exchange(piece, "rcv", n_rcv, 1) for j, piece in enumerate(passed, 1)}
         shot_transform = functools.partial(
-            transform, axis="rcv", chosen=tuple(range(n_src)), points=part, cuts=[1] + [2] * (len(chips) - 1)
+            transform, axis="rcv", chosen=tuple(range(n_src)), points=part, cuts=[()] + [(cut,)] * (len(chips) - 1)
         )
         out = shot_transform(near, table)
         out = shot_transform(last, table, added=out, after=(r_first[-1], r_far[0][0]))
@@ -300,22 +321,17 @@
             r_near.append(gather(late(r_first[q], token), "src", n_src))
         r_far[0] += [core(late(block, token)) for block in r_near[0][1:]]
 
-        held = n_src // 2
-
         def terms(chunk, pair, half):
-            shot = (s_near, s_far)[half]
-            block = shot[2 * pair - 1 + chunk] if pair else shot[0]
-            first = 0 if pair else chunk * held
-            return [
-                (
-                    half,
-                    block,
-                    (first + j) * part * shots,
-                    (r_near, r_far)[half][pair][chunk * held + j],
-                    part,
-                )
-                for j in range(held)
-            ]
+            low, high = ((0, cut), (cut, points))[chunk]
+            block = (s_near, s_far)[half][2 * pair - 1 + chunk if pair else 0]
+            found = []
+            for j in range(n_src):
+                start, stop = max(low, j * part), min(high, (j + 1) * part)
+                if start < stop:
+                    shot_row = (start - (low if pair else 0)) * shots
+                    receiver = (r_near, r_far)[half][pair][j]
+                    found.append((half, block, shot_row, receiver, (start - j * part) * receivers, stop - start))
+            return found
 
         pairs = chips[1:]
         first = [(0, 0, 0), (0, 0, 1), (1, 0, 0), (1, 0, 1)]
@@ -326,11 +342,11 @@
         for q in pairs:
             s_near[2 * q] = late(s_near[2 * q], total)
             s_far += [core(s_near[2 * q - 1]), core(s_near[2 * q])]
-            r_far.append([core(late(block, total)) for block in r_near[q]])
+            r_far.append([core(block) for block in r_near[q]])
         second = [(0, q, 1) for q in pairs] + [(1, q, 0) for q in pairs]
         after = [r_far[q][-1] for q in pairs]
         total = product(sum([terms(*x) for x in second], []), shots, receivers, total, after)
-        total = product(sum([terms(1, q, 1) for q in pairs], []), shots, receivers, total)
+        total = product(sum([terms(1, q, 1) for q in pairs], []), shots, receivers, total, last=True)
         return total.transpose(3, 0, 1, 2)
 
     placed = (P("sp", "src", "rcv"), P("sp", "rcv", "src"), P("sp"), P("sp"), P("sp"))

time: 45.4 us -> 42.7 us (0.941)
  Pallas kernels: 11.7 us -> 10.2 us
  waiting for transfers between devices: 15.2 us -> 14.3 us
    pallas_call x4, Pallas kernels: 7.61 us -> 6.1 us  [product(): pl.pallas_call(lambda *refs: product_kernel(described, len(blocks), len(c...]
    ppermute x16, waiting for transfers between devices: 15.2 us -> 14.3 us  [exchange(): return lax.ppermute(block, axis, [(i, i ^ step) for i in range(size)])]
    unnamed x6 -> x5, local copies, waits for them, and re-layouts: 0.99 us -> 0.97 us
  transfers between devices with their start and end apart: 16 -> 16, of which waited for: 6 -> 7; matrix products, arithmetic and copies ran while one was open for 4% -> 4% of each run, Pallas kernels for 22% -> 21%
where the time goes in v3:
time: 42.7 us; the launch traced here: 42.6 us
  starting transfers between devices  15.1 us (35%)
  waiting for transfers between devices  14.3 us (33%)
  Pallas kernels  10.2 us (24%)
  local copies, waits for them, and re-layouts  2.04 us (5%)
  other arithmetic  0.81 us (2%)
    ppermute x16, starting transfers between devices, exchange(): return lax.ppermute(block, axis, [(i, i ^ step) for i in range(size)])  15.1 us
    ppermute x16, waiting for transfers between devices, exchange(): return lax.ppermute(block, axis, [(i, i ^ step) for i in range(size)])  14.3 us
    pallas_call x4, Pallas kernels, product(): pl.pallas_call(lambda *refs: product_kernel(described, len(blocks), len(c...  6.1 us
    pallas_call x3, Pallas kernels, transform(): pl.pallas_call(lambda *refs: transform_kernel(steps, len(taper), len(adde...  2.94 us
    pallas_call x1, Pallas kernels, tables(): pl.pallas_call(tables_kernel, out_shape=out, in_specs=[VMEM], out_specs=[...  1.13 us
    dynamic_slice x1, local copies, waits for them, and re-layouts, own(): return lax.dynamic_slice_in_dim(array, (me ^ j) * part, part)  1.07 us
    unnamed x5, local copies, waits for them, and re-layouts  0.97 us
  transfers between devices with their start and end apart: 16, of which 7 were waited for; matrix products, arithmetic and copies ran while one was open for 4% of the time, Pallas kernels for 21%

profile of v3, /device:TPU:0, one launch (start us, length us, event | category | flops | bytes accessed | tf_op | source)
XLA Modules:
  0.0 42.6 jit_solution(13731440998574589165)
XLA Ops:
  0.0 3.0 %collective-permute-start = (f32[8,32,256]{2,1,0:T(8,128)}, f32[8,32,256]{2,1,0:T(8,128)S(1)}, u32[]{:S(2)}, u32[]{:S(2)}) collective-permute-start(f32[8,32,256]{2,1,0:T(8,128)} %refs_0_.1), channel_id=1, source_target_pairs={{0,4},{4,0},{8,12},{12,8},{1,5},{5,1},{9,13},{13,9},{2,6},{6,2},{1... | collective-permute-start | bytes 786440 | tf_op jit(solution)/shard_map/ppermute | solution.py:250
  3.0 2.6 %collective-permute-start.1 = (f32[8,32,256]{2,1,0:T(8,128)}, f32[8,32,256]{2,1,0:T(8,128)S(1)}, u32[]{:S(2)}, u32[]{:S(2)}) collective-permute-start(f32[8,32,256]{2,1,0:T(8,128)} %refs_0_.1), channel_id=1, source_target_pairs={{0,8},{4,12},{8,0},{12,4},{1,9},{5,13},{9,1},{13,5},{2,10},{6,14},... | collective-permute-start | bytes 786440 | tf_op jit(solution)/shard_map/ppermute | solution.py:250
  5.6 1.1 %constant_dynamic-slice_fusion = (f32[4,32,512]{2,1,0:T(8,128)S(1)}, f32[4,32,512]{2,1,0:T(8,128)S(1)}) fusion(f32[8,32,512]{2,1,0:T(8,128)} %param.7, s32[]{:T(128)S(6)} %select_n.7, s32[]{:T(128)S(6)} %select_n.6), kind=kLoop, calls=%fused_computation.2 | loop fusion | bytes 1048584 | tf_op jit(solution)/shard_map/dynamic_slice | solution.py:272
  6.7 1.6 %collective-permute-start.2 = (f32[4,32,512]{2,1,0:T(8,128)S(1)}, f32[4,32,512]{2,1,0:T(8,128)S(1)}, u32[]{:S(2)}, u32[]{:S(2)}) collective-permute-start(f32[4,32,512]{2,1,0:T(8,128)S(1)} %get-tuple-element.29), channel_id=1, source_target_pairs={{0,16},{16,0},{1,17},{17,1},{2,18},{18,2},{3,19},{19,3},{4,20},{20... | collective-permute-start | bytes 786440 | tf_op jit(solution)/shard_map/ppermute | solution.py:250
  8.3 0.0 copy-start.1
  8.3 0.9 %copy-done.1 = f32[2,4,64,128]{3,2,1,0:T(8,128)S(1)} copy-done((f32[2,4,64,128]{3,2,1,0:T(8,128)S(1)}, f32[2,4,64,128]{3,2,1,0:T(8,128)}, u32[]{:S(2)}) %copy-start.1) | copy-done | bytes 262168
  9.2 1.1 %tables.1 = (bf16[4,1024,256]{2,1,0:T(8,128)(2,1)S(1)}, bf16[4,1024,256]{2,1,0:T(8,128)(2,1)S(1)}) custom-call(f32[2,4,64,128]{3,2,1,0:T(8,128)S(1)} %copy-done.1), custom_call_target="tpu_custom_call" | custom-call | tf_op jit(solution)/shard_map/tables/pallas_call | solution.py:79
  10.3 0.8 %clamp_multiply_fusion.refs_4_ = f32[8,32,128]{2,1,0:T(8,128)S(1)} fusion(s32[8]{0:T(128)} %param.10, s32[8]{0:T(128)} %param.9, s32[32]{0:T(128)S(1)} %iota_add_fusion, f32[8]{0:T(128)} %param.8), kind=kLoop, calls=%fused_computation | loop fusion | flops 393216 | bytes 131296 | tf_op jit(solution)/shard_map/mul | solution.py:95
  11.2 3.1 %collective-permute-done.2.refs_1_ = f32[4,32,512]{2,1,0:T(8,128)S(1)} collective-permute-done((f32[4,32,512]{2,1,0:T(8,128)S(1)}, f32[4,32,512]{2,1,0:T(8,128)S(1)}, u32[]{:S(2)}, u32[]{:S(2)}) %collective-permute-start.2) | collective-permute-done | bytes 262176 | tf_op jit(solution)/shard_map/ppermute | solution.py:250
  14.2 0.0 copy-start
  14.2 1.0 %transform.3 = (f32[2,2,128,128]{3,2,1,0:T(8,128)S(1)}, f32[2,2,128,128]{3,2,1,0:T(8,128)S(1)}) custom-call(f32[4,32,512]{2,1,0:T(8,128)S(1)} %get-tuple-element.30.refs_0_, f32[4,32,512]{2,1,0:T(8,128)S(1)} %collective-permute-done.2.refs_1_, bf16[4,1024,256]{2,1,0:T(8,128)(2,1)S(1)} %get-tuple-element.17.refs_2_.refs_3_.refs_1_, ...), custom_call_target="tpu_custom_call" | custom-call | tf_op jit(solution)/shard_map/transform/pallas_call | solution.py:153
  15.2 0.1 collective-permute-start.5
  15.3 0.0 collective-permute-done.refs_0_
  15.3 2.2 %collective-permute-done.1.refs_1_ = f32[8,32,256]{2,1,0:T(8,128)S(1)} collective-permute-done((f32[8,32,256]{2,1,0:T(8,128)}, f32[8,32,256]{2,1,0:T(8,128)S(1)}, u32[]{:S(2)}, u32[]{:S(2)}) %collective-permute-start.1) | collective-permute-done | bytes 262176 | tf_op jit(solution)/shard_map/ppermute | solution.py:250
  17.6 0.4 %collective-permute-start.3 = (f32[8,32,256]{2,1,0:T(8,128)S(1)}, f32[8,32,256]{2,1,0:T(8,128)S(1)}, u32[]{:S(2)}, u32[]{:S(2)}) collective-permute-start(f32[8,32,256]{2,1,0:T(8,128)S(1)} %get-tuple-element.20.refs_2_), channel_id=1, source_target_pairs={{0,4},{4,0},{8,12},{12,8},{1,5},{5,1},{9,13},{13,9},{2,6},{6,2},{1... | collective-permute-start | bytes 786440 | tf_op jit(solution)/shard_map/ppermute | solution.py:250
  18.0 1.5 %collective-permute-start.4 = (f32[2,2,128,128]{3,2,1,0:T(8,128)S(1)}, f32[2,2,128,128]{3,2,1,0:T(8,128)S(1)}, u32[]{:S(2)}, u32[]{:S(2)}) collective-permute-start(f32[2,2,128,128]{3,2,1,0:T(8,128)S(1)} %get-tuple-element.25), channel_id=1, source_target_pairs={{0,2},{1,3},{2,0},{3,1},{4,6},{5,7},{6,4},{7,5},{8,10},{9,11},{10,... | collective-permute-start | bytes 786440 | tf_op jit(solution)/shard_map/ppermute | solution.py:250
  19.5 1.5 %collective-permute-start.8 = (f32[2,2,128,128]{3,2,1,0:T(8,128)S(1)}, f32[2,2,128,128]{3,2,1,0:T(8,128)S(1)}, u32[]{:S(2)}, u32[]{:S(2)}) collective-permute-start(f32[2,2,128,128]{3,2,1,0:T(8,128)S(1)} %get-tuple-element.19.refs_2_.refs_1_), channel_id=1, source_target_pairs={{0,16},{16,0},{1,17},{17,1},{2,18},{18,2},{3,19},{19,3},{4,20},{20... | collective-permute-start | bytes 786440 | tf_op jit(solution)/shard_map/ppermute | solution.py:250
  21.0 0.0 copy-done
  21.0 1.4 %transform.4 = (f32[2,2,256,128]{3,2,1,0:T(8,128)S(1)}, f32[2,2,160,128]{3,2,1,0:T(8,128)S(1)}, f32[2,2,96,128]{3,2,1,0:T(8,128)S(1)}) custom-call(f32[8,32,256]{2,1,0:T(8,128)S(1)} %copy-done, f32[8,32,256]{2,1,0:T(8,128)S(1)} %get-tuple-element.21.refs_1_, f32[8,32,256]{2,1,0:T(8,128)S(1)} %get-tuple-element.20.refs_2_, ...), custom_call_target="tpu_custom_call" | custom-call | tf_op jit(solution)/shard_map/transform/pallas_call | solution.py:153
  22.4 1.6 %collective-permute-done.3.refs_0_ = f32[8,32,256]{2,1,0:T(8,128)S(1)} collective-permute-done((f32[8,32,256]{2,1,0:T(8,128)S(1)}, f32[8,32,256]{2,1,0:T(8,128)S(1)}, u32[]{:S(2)}, u32[]{:S(2)}) %collective-permute-start.3) | collective-permute-done | bytes 262176 | tf_op jit(solution)/shard_map/ppermute | solution.py:250
  24.0 0.0 collective-permute-done.5.refs_7_.refs_4_
  24.0 0.8 %collective-permute-done.4.refs_6_.refs_0_ = f32[2,2,128,128]{3,2,1,0:T(8,128)S(1)} collective-permute-done((f32[2,2,128,128]{3,2,1,0:T(8,128)S(1)}, f32[2,2,128,128]{3,2,1,0:T(8,128)S(1)}, u32[]{:S(2)}, u32[]{:S(2)}) %collective-permute-start.4) | collective-permute-done | bytes 262176 | tf_op jit(solution)/shard_map/ppermute | solution.py:250
  24.9 0.6 %transform.5 = (f32[2,2,256,128]{3,2,1,0:T(8,128)S(1)}, f32[2,2,160,128]{3,2,1,0:T(8,128)S(1)}, f32[2,2,96,128]{3,2,1,0:T(8,128)S(1)}) custom-call(f32[8,32,256]{2,1,0:T(8,128)S(1)} %collective-permute-done.3.refs_0_, bf16[4,1024,256]{2,1,0:T(8,128)(2,1)S(1)} %get-tuple-element.17.refs_2_.refs_3_.refs_1_, ...), custom_call_target="tpu_custom_call" | custom-call | tf_op jit(solution)/shard_map/transform/pallas_call | solution.py:153
  25.4 0.1 collective-permute-start.9
  25.5 1.6 %collective-permute-start.7 = (f32[2,2,160,128]{3,2,1,0:T(8,128)S(1)}, f32[2,2,160,128]{3,2,1,0:T(8,128)S(1)}, u32[]{:S(2)}, u32[]{:S(2)}) collective-permute-start(f32[2,2,160,128]{3,2,1,0:T(8,128)S(1)} %get-tuple-element.27), channel_id=1, source_target_pairs={{0,2},{1,3},{2,0},{3,1},{4,6},{5,7},{6,4},{7,5},{8,10},{9,11},{10,... | collective-permute-start | bytes 983048 | tf_op jit(solution)/shard_map/ppermute | solution.py:250
  27.1 0.0 collective-permute-done.8.refs_2_
  27.1 0.2 collective-permute-start.10
  27.4 1.5 %collective-permute-start.11 = (f32[2,2,128,128]{3,2,1,0:T(8,128)S(1)}, f32[2,2,128,128]{3,2,1,0:T(8,128)S(1)}, u32[]{:S(2)}, u32[]{:S(2)}) collective-permute-start(f32[2,2,128,128]{3,2,1,0:T(8,128)S(1)} %order.8.refs_1_), channel_id=1, source_target_pairs={{0,16},{16,0},{1,17},{17,1},{2,18},{18,2},{3,19},{19,3},{4,20},{20... | collective-permute-start | bytes 786440 | tf_op jit(solution)/shard_map/ppermute | solution.py:250
  28.9 0.5 %collective-permute-start.6 = (f32[2,2,96,128]{3,2,1,0:T(8,128)S(1)}, f32[2,2,96,128]{3,2,1,0:T(8,128)S(1)}, u32[]{:S(2)}, u32[]{:S(2)}) collective-permute-start(f32[2,2,96,128]{3,2,1,0:T(8,128)S(1)} %get-tuple-element.26), channel_id=1, source_target_pairs={{0,2},{1,3},{2,0},{3,1},{4,6},{5,7},{6,4},{7,5},{8,10},{9,11},{10,... | collective-permute-start | bytes 589832 | tf_op jit(solution)/shard_map/ppermute | solution.py:250
  29.4 0.0 collective-permute-done.10.refs_5_
  29.4 0.0 collective-permute-done.9.refs_3_
  29.4 2.6 %product.4.refs_1_.refs_3_ = f32[2,32,32,128]{3,2,1,0:T(8,128)S(1)} custom-call(f32[2,2,256,128]{3,2,1,0:T(8,128)S(1)} %get-tuple-element.28.refs_1_.refs_0_, f32[2,2,128,128]{3,2,1,0:T(8,128)S(1)} %get-tuple-element.19.refs_2_.refs_1_, f32[2,2,128,128]{3,2,1,0:T(8,128)S(1)} %collective-permute-done.8.refs_2_, ...), custom_call_target="tpu_custom_call" | custom-call | tf_op jit(solution)/shard_map/product/pallas_call | solution.py:237
  32.0 4.1 %collective-permute-done.7.refs_0_ = f32[2,2,160,128]{3,2,1,0:T(8,128)S(1)} collective-permute-done((f32[2,2,160,128]{3,2,1,0:T(8,128)S(1)}, f32[2,2,160,128]{3,2,1,0:T(8,128)S(1)}, u32[]{:S(2)}, u32[]{:S(2)}) %collective-permute-start.7) | collective-permute-done | bytes 327712 | tf_op jit(solution)/shard_map/ppermute | solution.py:250
  36.1 0.0 collective-permute-start.14
  36.1 0.5 %collective-permute-start.15 = (f32[2,2,128,128]{3,2,1,0:T(8,128)S(1)}, f32[2,2,128,128]{3,2,1,0:T(8,128)S(1)}, u32[]{:S(2)}, u32[]{:S(2)}) collective-permute-start(f32[2,2,128,128]{3,2,1,0:T(8,128)S(1)} %order.8.refs_1_), channel_id=1, source_target_pairs={{0,1},{1,0},{2,3},{3,2},{4,5},{5,4},{6,7},{7,6},{8,9},{9,8},{10,11... | collective-permute-start | bytes 786440 | tf_op jit(solution)/shard_map/ppermute | solution.py:250
  36.6 0.0 collective-permute-done.11.refs_2_.refs_4_
  36.6 0.0 collective-permute-start.13
  36.6 0.9 %product.5.refs_1_.refs_5_ = f32[2,32,32,128]{3,2,1,0:T(8,128)S(1)} custom-call(f32[2,2,160,128]{3,2,1,0:T(8,128)S(1)} %order.7.refs_0_, f32[2,2,128,128]{3,2,1,0:T(8,128)S(1)} %order.8.refs_1_, f32[2,2,128,128]{3,2,1,0:T(8,128)S(1)} %collective-permute-done.11.refs_2_.refs_4_, f32[2,32,32,128]{3,2,1,0:T(8,128)S(1)} %product.4.refs_1_.refs_3_), custom_call_target="tpu_custom_call" | custom-call | tf_op jit(solution)/shard_map/product/pallas_call | solution.py:237
  37.5 2.4 %collective-permute-done.6.refs_0_ = f32[2,2,96,128]{3,2,1,0:T(8,128)S(1)} collective-permute-done((f32[2,2,96,128]{3,2,1,0:T(8,128)S(1)}, f32[2,2,96,128]{3,2,1,0:T(8,128)S(1)}, u32[]{:S(2)}, u32[]{:S(2)}) %collective-permute-start.6) | collective-permute-done | bytes 196640 | tf_op jit(solution)/shard_map/ppermute | solution.py:250
  39.9 0.0 collective-permute-start.12
  39.9 0.0 collective-permute-done.15.refs_1_
  39.9 0.0 collective-permute-done.13.refs_2_.refs_6_.refs_1_
  39.9 0.0 collective-permute-done.14.refs_0_
  39.9 1.3 %product.6.refs_2_ = f32[2,32,32,128]{3,2,1,0:T(8,128)S(1)} custom-call(f32[2,2,160,128]{3,2,1,0:T(8,128)S(1)} %collective-permute-done.14.refs_0_, f32[2,2,128,128]{3,2,1,0:T(8,128)S(1)} %collective-permute-done.15.refs_1_, f32[2,2,128,128]{3,2,1,0:T(8,128)S(1)} %collective-permute-done.13.refs_2_.refs_6_.refs_1_, f32[2,2,96,128]{3,2,1,0:T(8,128)S(1)} %order.9.refs_3_, ...), custom_call_target="tpu_custom_call" | custom-call | tf_op jit(solution)/shard_map/product/pallas_call | solution.py:237
  41.2 0.1 collective-permute-done.12.refs_0_
  41.3 1.3 %product.7 = f32[2,32,32,128]{3,2,1,0:T(8,128)} custom-call(f32[2,2,96,128]{3,2,1,0:T(8,128)S(1)} %collective-permute-done.12.refs_0_, f32[2,2,128,128]{3,2,1,0:T(8,128)S(1)} %collective-permute-done.13.refs_2_.refs_6_.refs_1_, f32[2,32,32,128]{3,2,1,0:T(8,128)S(1)} %product.6.refs_2_), custom_call_target="tpu_custom_call" | custom-call | tf_op jit(solution)/shard_map/product/pallas_call | solution.py:237
  (7 shorter events, 0.0 us)
Async XLA Ops:
  0.0 15.3 %collective-permute-start = (f32[8,32,256]{2,1,0:T(8,128)}, f32[8,32,256]{2,1,0:T(8,128)S(1)}, u32[]{:S(2)}, u32[]{:S(2)}) collective-permute-start(f32[8,32,256]{2,1,0:T(8,128)} %refs_0_.1), channel_id=1, source_target_pairs={{0,4},{4,0},{8,12},{12,8},{1,5},{5,1},{9,13},{13,9},{2,6},{6,2},{1... | collective-permute-start | bytes 786440 | tf_op jit(solution)/shard_map/ppermute | solution.py:250
  3.0 14.6 %collective-permute-start.1 = (f32[8,32,256]{2,1,0:T(8,128)}, f32[8,32,256]{2,1,0:T(8,128)S(1)}, u32[]{:S(2)}, u32[]{:S(2)}) collective-permute-start(f32[8,32,256]{2,1,0:T(8,128)} %refs_0_.1), channel_id=1, source_target_pairs={{0,8},{4,12},{8,0},{12,4},{1,9},{5,13},{9,1},{13,5},{2,10},{6,14},... | collective-permute-start | bytes 786440 | tf_op jit(solution)/shard_map/ppermute | solution.py:250
  6.7 7.6 %collective-permute-start.2 = (f32[4,32,512]{2,1,0:T(8,128)S(1)}, f32[4,32,512]{2,1,0:T(8,128)S(1)}, u32[]{:S(2)}, u32[]{:S(2)}) collective-permute-start(f32[4,32,512]{2,1,0:T(8,128)S(1)} %get-tuple-element.29), channel_id=1, source_target_pairs={{0,16},{16,0},{1,17},{17,1},{2,18},{18,2},{3,19},{19,3},{4,20},{20... | collective-permute-start | bytes 786440 | tf_op jit(solution)/shard_map/ppermute | solution.py:250
  8.3 0.9 %copy-start.1 = (f32[2,4,64,128]{3,2,1,0:T(8,128)S(1)}, f32[2,4,64,128]{3,2,1,0:T(8,128)}, u32[]{:S(2)}) copy-start(f32[2,4,64,128]{3,2,1,0:T(8,128)} %constant.32.clone.angles_ref) | copy-start | bytes 786436
  14.2 6.8 %copy-start = (f32[8,32,256]{2,1,0:T(8,128)S(1)}, f32[8,32,256]{2,1,0:T(8,128)}, u32[]{:S(2)}) copy-start(f32[8,32,256]{2,1,0:T(8,128)} %refs_0_.1) | copy-start | bytes 786436
  15.2 8.8 %collective-permute-start.5 = (f32[2,2,128,128]{3,2,1,0:T(8,128)S(1)}, f32[2,2,128,128]{3,2,1,0:T(8,128)S(1)}, u32[]{:S(2)}, u32[]{:S(2)}) collective-permute-start(f32[2,2,128,128]{3,2,1,0:T(8,128)S(1)} %get-tuple-element.19.refs_2_.refs_1_), channel_id=1, source_target_pairs={{0,1},{1,0},{2,3},{3,2},{4,5},{5,4},{6,7},{7,6},{8,9},{9,8},{10,11... | collective-permute-start | bytes 786440 | tf_op jit(solution)/shard_map/ppermute | solution.py:250
  17.6 6.5 %collective-permute-start.3 = (f32[8,32,256]{2,1,0:T(8,128)S(1)}, f32[8,32,256]{2,1,0:T(8,128)S(1)}, u32[]{:S(2)}, u32[]{:S(2)}) collective-permute-start(f32[8,32,256]{2,1,0:T(8,128)S(1)} %get-tuple-element.20.refs_2_), channel_id=1, source_target_pairs={{0,4},{4,0},{8,12},{12,8},{1,5},{5,1},{9,13},{13,9},{2,6},{6,2},{1... | collective-permute-start | bytes 786440 | tf_op jit(solution)/shard_map/ppermute | solution.py:250
  18.0 6.8 %collective-permute-start.4 = (f32[2,2,128,128]{3,2,1,0:T(8,128)S(1)}, f32[2,2,128,128]{3,2,1,0:T(8,128)S(1)}, u32[]{:S(2)}, u32[]{:S(2)}) collective-permute-start(f32[2,2,128,128]{3,2,1,0:T(8,128)S(1)} %get-tuple-element.25), channel_id=1, source_target_pairs={{0,2},{1,3},{2,0},{3,1},{4,6},{5,7},{6,4},{7,5},{8,10},{9,11},{10,... | collective-permute-start | bytes 786440 | tf_op jit(solution)/shard_map/ppermute | solution.py:250
  19.5 7.6 %collective-permute-start.8 = (f32[2,2,128,128]{3,2,1,0:T(8,128)S(1)}, f32[2,2,128,128]{3,2,1,0:T(8,128)S(1)}, u32[]{:S(2)}, u32[]{:S(2)}) collective-permute-start(f32[2,2,128,128]{3,2,1,0:T(8,128)S(1)} %get-tuple-element.19.refs_2_.refs_1_), channel_id=1, source_target_pairs={{0,16},{16,0},{1,17},{17,1},{2,18},{18,2},{3,19},{19,3},{4,20},{20... | collective-permute-start | bytes 786440 | tf_op jit(solution)/shard_map/ppermute | solution.py:250
  25.4 3.9 %collective-permute-start.9 = (f32[2,2,256,128]{3,2,1,0:T(8,128)S(1)}, f32[2,2,256,128]{3,2,1,0:T(8,128)S(1)}, u32[]{:S(2)}, u32[]{:S(2)}) collective-permute-start(f32[2,2,256,128]{3,2,1,0:T(8,128)S(1)} %get-tuple-element.28.refs_1_.refs_0_), channel_id=1, source_target_pairs={{0,1},{1,0},{2,3},{3,2},{4,5},{5,4},{6,7},{7,6},{8,9},{9,8},{10,11... | collective-permute-start | bytes 1572872 | tf_op jit(solution)/shard_map/ppermute | solution.py:250
  25.5 10.6 %collective-permute-start.7 = (f32[2,2,160,128]{3,2,1,0:T(8,128)S(1)}, f32[2,2,160,128]{3,2,1,0:T(8,128)S(1)}, u32[]{:S(2)}, u32[]{:S(2)}) collective-permute-start(f32[2,2,160,128]{3,2,1,0:T(8,128)S(1)} %get-tuple-element.27), channel_id=1, source_target_pairs={{0,2},{1,3},{2,0},{3,1},{4,6},{5,7},{6,4},{7,5},{8,10},{9,11},{10,... | collective-permute-start | bytes 983048 | tf_op jit(solution)/shard_map/ppermute | solution.py:250
  27.1 2.2 %collective-permute-start.10 = (f32[2,2,128,128]{3,2,1,0:T(8,128)S(1)}, f32[2,2,128,128]{3,2,1,0:T(8,128)S(1)}, u32[]{:S(2)}, u32[]{:S(2)}) collective-permute-start(f32[2,2,128,128]{3,2,1,0:T(8,128)S(1)} %order.6), channel_id=1, source_target_pairs={{0,1},{1,0},{2,3},{3,2},{4,5},{5,4},{6,7},{7,6},{8,9},{9,8},{10,11... | collective-permute-start | bytes 786440 | tf_op jit(solution)/shard_map/ppermute | solution.py:250
  27.4 9.2 %collective-permute-start.11 = (f32[2,2,128,128]{3,2,1,0:T(8,128)S(1)}, f32[2,2,128,128]{3,2,1,0:T(8,128)S(1)}, u32[]{:S(2)}, u32[]{:S(2)}) collective-permute-start(f32[2,2,128,128]{3,2,1,0:T(8,128)S(1)} %order.8.refs_1_), channel_id=1, source_target_pairs={{0,16},{16,0},{1,17},{17,1},{2,18},{18,2},{3,19},{19,3},{4,20},{20... | collective-permute-start | bytes 786440 | tf_op jit(solution)/shard_map/ppermute | solution.py:250
  28.9 11.0 %collective-permute-start.6 = (f32[2,2,96,128]{3,2,1,0:T(8,128)S(1)}, f32[2,2,96,128]{3,2,1,0:T(8,128)S(1)}, u32[]{:S(2)}, u32[]{:S(2)}) collective-permute-start(f32[2,2,96,128]{3,2,1,0:T(8,128)S(1)} %get-tuple-element.26), channel_id=1, source_target_pairs={{0,2},{1,3},{2,0},{3,1},{4,6},{5,7},{6,4},{7,5},{8,10},{9,11},{10,... | collective-permute-start | bytes 589832 | tf_op jit(solution)/shard_map/ppermute | solution.py:250
  36.1 3.8 %collective-permute-start.14 = (f32[2,2,160,128]{3,2,1,0:T(8,128)S(1)}, f32[2,2,160,128]{3,2,1,0:T(8,128)S(1)}, u32[]{:S(2)}, u32[]{:S(2)}) collective-permute-start(f32[2,2,160,128]{3,2,1,0:T(8,128)S(1)} %order.7.refs_0_), channel_id=1, source_target_pairs={{0,1},{1,0},{2,3},{3,2},{4,5},{5,4},{6,7},{7,6},{8,9},{9,8},{10,11... | collective-permute-start | bytes 983048 | tf_op jit(solution)/shard_map/ppermute | solution.py:250
  36.1 3.8 %collective-permute-start.15 = (f32[2,2,128,128]{3,2,1,0:T(8,128)S(1)}, f32[2,2,128,128]{3,2,1,0:T(8,128)S(1)}, u32[]{:S(2)}, u32[]{:S(2)}) collective-permute-start(f32[2,2,128,128]{3,2,1,0:T(8,128)S(1)} %order.8.refs_1_), channel_id=1, source_target_pairs={{0,1},{1,0},{2,3},{3,2},{4,5},{5,4},{6,7},{7,6},{8,9},{9,8},{10,11... | collective-permute-start | bytes 786440 | tf_op jit(solution)/shard_map/ppermute | solution.py:250
  36.6 3.3 %collective-permute-start.13 = (f32[2,2,128,128]{3,2,1,0:T(8,128)S(1)}, f32[2,2,128,128]{3,2,1,0:T(8,128)S(1)}, u32[]{:S(2)}, u32[]{:S(2)}) collective-permute-start(f32[2,2,128,128]{3,2,1,0:T(8,128)S(1)} %collective-permute-done.11.refs_2_.refs_4_), channel_id=1, source_target_pairs={{0,1},{1,0},{2,3},{3,2},{4,5},{5,4},{6,7},{7,6},{8,9},{9,8},{10,11... | collective-permute-start | bytes 786440 | tf_op jit(solution)/shard_map/ppermute | solution.py:250
  39.9 1.4 %collective-permute-start.12 = (f32[2,2,96,128]{3,2,1,0:T(8,128)S(1)}, f32[2,2,96,128]{3,2,1,0:T(8,128)S(1)}, u32[]{:S(2)}, u32[]{:S(2)}) collective-permute-start(f32[2,2,96,128]{3,2,1,0:T(8,128)S(1)} %order.9.refs_3_), channel_id=1, source_target_pairs={{0,1},{1,0},{2,3},{3,2},{4,5},{5,4},{6,7},{7,6},{8,9},{9,8},{10,11... | collective-permute-start | bytes 589832 | tf_op jit(solution)/shard_map/ppermute | solution.py:250

commit v4 on v3

--- a/solution.py
+++ b/solution.py
@@ -14,7 +14,10 @@
 SMEM = pl.BlockSpec(memory_space=pltpu.SMEM)
 ANY = pl.BlockSpec(memory_space=pl.ANY)
 HBM = pl.BlockSpec(memory_space=pltpu.HBM)
-COST = pl.CostEstimate(flops=0, bytes_accessed=0, transcendentals=0)
+
+
+def cost(flops=0):
+    return pl.CostEstimate(flops=flops, bytes_accessed=0, transcendentals=0)
 
 
 def room(*arrays):
@@ -26,7 +29,7 @@
     return pltpu.CompilerParams(vmem_limit_bytes=need)
 
 
-def order(arrays, after):
+def order(arrays, after, flops=0):
     count = len(arrays)
 
     def kernel(*refs):
@@ -39,9 +42,38 @@
         out_specs=[ANY] * count,
         input_output_aliases={i: i for i in range(count)},
         compiler_params=room(),
-        cost_estimate=COST,
+        cost_estimate=cost(flops),
         name="order",
     )(*arrays, *after)
+
+
+def runs(low, high, part):
+    found = []
+    for j in range(low // part, -(-high // part)):
+        start, stop = max(low, j * part), min(high, (j + 1) * part)
+        found.append((j, start - j * part, stop - start, start - low))
+    return found
+
+
+def pick(array, edges, part, after, flops=0):
+    bounds = list(zip(edges, edges[1:]))
+    out = [jax.ShapeDtypeStruct((high - low,) + array.shape[1:], array.dtype) for low, high in bounds]
+
+    def kernel(array_ref, *refs):
+        me = lax.axis_index("src")
+        for (low, high), out_ref in zip(bounds, refs[len(after) :]):
+            for j, first, count, place in runs(low, high, part):
+                out_ref[place : place + count] = array_ref[pl.ds((me ^ j) * part + first, count)]
+
+    return pl.pallas_call(
+        kernel,
+        out_shape=out,
+        in_specs=[VMEM] + [ANY] * len(after),
+        out_specs=[VMEM] * len(out),
+        compiler_params=room(array, *out),
+        cost_estimate=cost(flops),
+        name="pick",
+    )(array, *after)
 
 
 def tables_kernel(angles_ref, high_ref, low_ref):
@@ -82,7 +114,7 @@
         in_specs=[VMEM],
         out_specs=[VMEM] * 2,
         compiler_params=room(angles, *out),
-        cost_estimate=COST,
+        cost_estimate=cost(),
         name="tables",
     )(angles)
 
@@ -95,7 +127,7 @@
     return obliquity[:, None, None] * rising * falling
 
 
-def transform_kernel(steps, tapered, added, axis, chosen, points, spans, *refs):
+def transform_kernel(steps, tapered, added, axis, low, high, part, points, spans, *refs):
     piece_refs, (high_ref, low_ref), refs = refs[: len(steps)], refs[len(steps) : len(steps) + 2], refs[len(steps) + 2 :]
     added_refs, (x_high, x_low) = refs[tapered : tapered + added], refs[-2:]
     pairs = high_ref.shape[0] // 2
@@ -104,60 +136,59 @@
     bins = out_refs[0].shape[-1]
     me_src, me_time, me_sp = (lax.axis_index(a) for a in ("src", axis, "sp"))
 
-    def own(i):
-        return pl.ds((me_src ^ chosen[i]) * points, points)
-
     for j, piece_ref in enumerate(piece_refs):
-        for i in range(len(chosen)):
-            span = slice(None) if piece_ref.shape[0] == points else own(i)
-            x = piece_ref[span].reshape(points * rows, width)
-            high = x.astype(jnp.bfloat16)
-            low = (x - high.astype(jnp.float32)).astype(jnp.bfloat16)
-            place = slice(i * points * rows, (i + 1) * points * rows)
-            x_high[place, j * width : (j + 1) * width] = high
-            x_low[place, j * width : (j + 1) * width] = low
+        for i, first, count, place in runs(low, high, part):
+            whole = piece_ref.shape[0] == points
+            x = piece_ref[pl.ds((me_src ^ i) * part + first, count) if whole else slice(place, place + count)]
+            x = x.reshape(count * rows, width)
+            high_part = x.astype(jnp.bfloat16)
+            low_part = (x - high_part.astype(jnp.float32)).astype(jnp.bfloat16)
+            place = slice(place * rows, (place + count) * rows)
+            x_high[place, j * width : (j + 1) * width] = high_part
+            x_low[place, j * width : (j + 1) * width] = low_part
     for k in range(2 * pairs):
-        part = me_sp ^ k
+        device = me_sp ^ k
         spectrum = 0.0
         for j, step in enumerate(steps):
             times = pl.ds(pl.multiple_of((me_time ^ step) * width, width), width)
-            w_high, w_low = high_ref[part, times, :], low_ref[part, times, :]
-            high, low = (x[:, j * width : (j + 1) * width] for x in (x_high, x_low))
+            w_high, w_low = high_ref[device, times, :], low_ref[device, times, :]
+            x_hi, x_lo = (x[:, j * width : (j + 1) * width] for x in (x_high, x_low))
             spectrum += (
-                jnp.dot(high, w_high, preferred_element_type=jnp.float32)
-                + jnp.dot(low, w_high, preferred_element_type=jnp.float32)
-                + jnp.dot(high, w_low, preferred_element_type=jnp.float32)
+                jnp.dot(x_hi, w_high, preferred_element_type=jnp.float32)
+                + jnp.dot(x_lo, w_high, preferred_element_type=jnp.float32)
+                + jnp.dot(x_hi, w_low, preferred_element_type=jnp.float32)
             )
         for c in range(2):
             half = spectrum[:, c * bins : (c + 1) * bins]
             if tapered:
-                half = half * refs[0][own(0)].reshape(points * rows, bins)
+                own = pl.ds(me_src * part, part)
+                half = half * refs[0][own].reshape(part * rows, bins)
             for i, (q, first, count) in enumerate(spans):
                 if q == k // 2:
                     value = half[first : first + count]
                     out_refs[i][k % 2, c] = value + added_refs[i][k % 2, c] if added else value
 
 
-def transform(pieces, table, axis, chosen, points, cuts, taper=(), added=(), after=()):
+def transform(pieces, table, axis, low, high, part, points, cuts, taper=(), added=(), after=(), flops=0):
     steps, pieces = tuple(pieces), list(pieces.values())
     rows, width = pieces[0].shape[1:]
     bins = table[0].shape[2] // 2
-    total = points * len(chosen) * rows
+    total = (high - low) * rows
     spans = []
     for q, cut in enumerate(cuts):
-        edges = [0, *(point * rows for point in cut), total]
+        edges = [0, *((point - low) * rows for point in cut), total]
         spans += [(q, start, stop - start) for start, stop in zip(edges, edges[1:])]
     out = [jax.ShapeDtypeStruct((2, 2, count, bins), jnp.float32) for _, _, count in spans]
     split = [jax.ShapeDtypeStruct((total, len(steps) * width), jnp.bfloat16)] * 2
     spectrum = jax.ShapeDtypeStruct((total, 2 * bins), jnp.float32)
     return pl.pallas_call(
-        lambda *refs: transform_kernel(steps, len(taper), len(added), axis, chosen, points, spans, *refs),
+        lambda *refs: transform_kernel(steps, len(taper), len(added), axis, low, high, part, points, spans, *refs),
         out_shape=out,
         in_specs=[VMEM] * (len(pieces) + 2 + len(taper) + len(added)) + [ANY] * len(after),
         out_specs=[VMEM] * len(spans),
         scratch_shapes=[pltpu.VMEM(x.shape, x.dtype) for x in split],
         compiler_params=room(*pieces, *table, *taper, *added, *out, *split, *[spectrum] * 4),
-        cost_estimate=COST,
+        cost_estimate=cost(flops),
         name="transform",
     )(*pieces, *table, *taper, *added, *after)
 
@@ -241,7 +272,7 @@
         out_specs=HBM if last else VMEM,
         scratch_shapes=sends if last else [],
         compiler_params=room(*blocks, *carried, out),
-        cost_estimate=COST,
+        cost_estimate=cost(),
         name="product",
     )(*blocks, *carried, *after)
 
@@ -299,7 +330,7 @@
 
         chips = range(n_sp // 2)
         receiver_pieces = dict(enumerate(receiver_pieces))
-        out = transform(receiver_pieces, table, "src", (0,), part, [()] * len(chips), (taper,))
+        out = transform(receiver_pieces, table, "src", 0, part, part, points, [()] * len(chips), (taper,))
         token, r_first = out[0], cross(out, 1)
         r_near = [gather(r_first[0], "src", n_src)]
         r_far = [[core(r_first[0])]]
@@ -307,41 +338,52 @@
         cut = points - 3 * points // 8
         even = gather(shot_traces, "rcv", n_rcv, 2)
         beside = exchange(shot_traces, "rcv", n_rcv, 1)
-        beside, *passed = order([beside, *even[1:]], [token])
-        near = {0: shot_traces, 1: beside} | {2 * j: piece for j, piece in enumerate(passed, 1)}
-        last = {2 * j + 1: exchange(piece, "rcv", n_rcv, 1) for j, piece in enumerate(passed, 1)}
-        shot_transform = functools.partial(
-            transform, axis="rcv", chosen=tuple(range(n_src)), points=part, cuts=[()] + [(cut,)] * (len(chips) - 1)
+        beside = late(beside, token)
+        edges = (0, cut, points)
+        shot_transform = functools.partial(transform, table=table, axis="rcv", part=part, points=points)
+        near = {0: shot_traces, 1: beside} | {2 * j: piece for j, piece in enumerate(even[1:], 1)}
+        first = [pick(piece, edges[:2], part, [token, beside], 3 * 10**9) for piece in even[1:]]
+        out = shot_transform(
+            near, low=0, high=points, cuts=[(cut,)] * len(chips), after=[p[0] for p in first], flops=10**9
         )
-        out = shot_transform(near, table)
-        out = shot_transform(last, table, added=out, after=(r_first[-1], r_far[0][0]))
-        token, s_near = out[0], cross(out, 2)
-        s_far = [core(s_near[0])]
+        passed = [p + pick(piece, edges[1:], part, [out[0]]) for p, piece in zip(first, even[1:])]
+        s_near = [None] * (2 * len(chips))
+        after = r_far[0] + r_first[1:]
+        for chunk, flops in ((0, 2500 * 10**6), (1, 8 * 10**9)):
+            last = {2 * j + 1: exchange(p[chunk], "rcv", n_rcv, 1) for j, p in enumerate(passed, 1)}
+            blocks = shot_transform(
+                last,
+                low=edges[chunk],
+                high=edges[chunk + 1],
+                cuts=[()] * len(chips),
+                added=out[chunk::2],
+                after=after,
+                flops=flops,
+            )
+            s_near[chunk::2] = cross(blocks, 1)
+            after, token = [blocks[0]], blocks[0]
+        s_far = [core(s_near[0]), None]
         for q in chips[1:]:
             r_near.append(gather(late(r_first[q], token), "src", n_src))
-        r_far[0] += [core(late(block, token)) for block in r_near[0][1:]]
+        r_far[0] += [core(late(block, s_near[0])) for block in r_near[0][1:]]
 
         def terms(chunk, pair, half):
-            low, high = ((0, cut), (cut, points))[chunk]
-            block = (s_near, s_far)[half][2 * pair - 1 + chunk if pair else 0]
-            found = []
-            for j in range(n_src):
-                start, stop = max(low, j * part), min(high, (j + 1) * part)
-                if start < stop:
-                    shot_row = (start - (low if pair else 0)) * shots
-                    receiver = (r_near, r_far)[half][pair][j]
-                    found.append((half, block, shot_row, receiver, (start - j * part) * receivers, stop - start))
-            return found
+            block = (s_near, s_far)[half][2 * pair + chunk]
+            return [
+                (half, block, place * shots, (r_near, r_far)[half][pair][j], first * receivers, count)
+                for j, first, count, place in runs(edges[chunk], edges[chunk + 1], part)
+            ]
 
         pairs = chips[1:]
-        first = [(0, 0, 0), (0, 0, 1), (1, 0, 0), (1, 0, 1)]
+        first = [(0, 0, 0), (0, 0, 1), (1, 0, 0)]
         total = product(sum([terms(*x) for x in first], []), shots, receivers)
         for q in pairs:
-            s_near[2 * q - 1] = late(s_near[2 * q - 1], total)
-        total = product(sum([terms(0, q, 0) for q in pairs], []), shots, receivers, total)
+            s_near[2 * q] = late(s_near[2 * q], total)
+        s_far[1] = core(s_near[1])
+        total = product(sum([terms(0, q, 0) for q in pairs] + [terms(1, 0, 1)], []), shots, receivers, total)
         for q in pairs:
-            s_near[2 * q] = late(s_near[2 * q], total)
-            s_far += [core(s_near[2 * q - 1]), core(s_near[2 * q])]
+            s_near[2 * q + 1] = late(s_near[2 * q + 1], total)
+            s_far += [core(s_near[2 * q]), core(s_near[2 * q + 1])]
             r_far.append([core(block) for block in r_near[q]])
         second = [(0, q, 1) for q in pairs] + [(1, q, 0) for q in pairs]
         after = [r_far[q][-1] for q in pairs]

time: 42.7 us -> 40.9 us (0.958)
  waiting for transfers between devices: 14.3 us -> 10.1 us
  starting transfers between devices: 15.1 us -> 17.2 us
    ppermute x16 -> x18, waiting for transfers between devices: 14.3 us -> 10.1 us  [exchange(): return lax.ppermute(block, axis, [(i, i ^ step) for i in range(size)])]
    ppermute x16 -> x18, starting transfers between devices: 15.1 us -> 17.2 us  [exchange(): return lax.ppermute(block, axis, [(i, i ^ step) for i in range(size)])]
    pallas_call x3 -> x4, Pallas kernels: 2.94 us -> 3.2 us  [transform(): pl.pallas_call(lambda *refs: transform_kernel(steps, len(taper), len(adde...]
  transfers between devices with their start and end apart: 16 -> 18, of which waited for: 7 -> 6; matrix products, arithmetic and copies ran while one was open for 4% -> 5% of each run, Pallas kernels for 21% -> 23%
where the time goes in v4:
time: 40.9 us; the launch traced here: 40.8 us
  starting transfers between devices  17.2 us (42%)
  Pallas kernels  10.5 us (26%)
  waiting for transfers between devices  10.1 us (25%)
  local copies, waits for them, and re-layouts  2.04 us (5%)
  other arithmetic  0.81 us (2%)
    ppermute x18, starting transfers between devices, exchange(): return lax.ppermute(block, axis, [(i, i ^ step) for i in range(size)])  17.2 us
    ppermute x18, waiting for transfers between devices, exchange(): return lax.ppermute(block, axis, [(i, i ^ step) for i in range(size)])  10.1 us
    pallas_call x4, Pallas kernels, product(): pl.pallas_call(lambda *refs: product_kernel(described, len(blocks), len(c...  6.1 us
    pallas_call x4, Pallas kernels, transform(): pl.pallas_call(lambda *refs: transform_kernel(steps, len(taper), len(adde...  3.2 us
    pallas_call x1, Pallas kernels, tables(): pl.pallas_call(tables_kernel, out_shape=out, in_specs=[VMEM], out_specs=[...  1.13 us
    dynamic_slice x1, local copies, waits for them, and re-layouts, own(): return lax.dynamic_slice_in_dim(array, (me ^ j) * part, part)  1.07 us
    unnamed x5, local copies, waits for them, and re-layouts  0.97 us
  transfers between devices with their start and end apart: 18, of which 6 were waited for; matrix products, arithmetic and copies ran while one was open for 5% of the time, Pallas kernels for 23%

profile of v4, /device:TPU:0, one launch (start us, length us, event | category | flops | bytes accessed | tf_op | source)
XLA Modules:
  0.0 40.8 jit_solution(13156536510802681629)
XLA Ops:
  0.0 4.0 %collective-permute-start = (f32[8,32,256]{2,1,0:T(8,128)}, f32[8,32,256]{2,1,0:T(8,128)S(1)}, u32[]{:S(2)}, u32[]{:S(2)}) collective-permute-start(f32[8,32,256]{2,1,0:T(8,128)} %refs_0_.1), channel_id=1, source_target_pairs={{0,8},{4,12},{8,0},{12,4},{1,9},{5,13},{9,1},{13,5},{2,10},{6,14},... | collective-permute-start | bytes 786440 | tf_op jit(solution)/shard_map/ppermute | solution.py:281
  4.0 1.6 %collective-permute-start.1 = (f32[8,32,256]{2,1,0:T(8,128)}, f32[8,32,256]{2,1,0:T(8,128)S(1)}, u32[]{:S(2)}, u32[]{:S(2)}) collective-permute-start(f32[8,32,256]{2,1,0:T(8,128)} %refs_0_.1), channel_id=1, source_target_pairs={{0,4},{4,0},{8,12},{12,8},{1,5},{5,1},{9,13},{13,9},{2,6},{6,2},{1... | collective-permute-start | bytes 786440 | tf_op jit(solution)/shard_map/ppermute | solution.py:281
  5.6 1.1 %constant_dynamic-slice_fusion = (f32[4,32,512]{2,1,0:T(8,128)S(1)}, f32[4,32,512]{2,1,0:T(8,128)S(1)}) fusion(f32[8,32,512]{2,1,0:T(8,128)} %param.7, s32[]{:T(128)S(6)} %select_n.7, s32[]{:T(128)S(6)} %select_n.6), kind=kLoop, calls=%fused_computation.2 | loop fusion | bytes 1048584 | tf_op jit(solution)/shard_map/dynamic_slice | solution.py:303
  6.7 1.6 %collective-permute-start.2 = (f32[4,32,512]{2,1,0:T(8,128)S(1)}, f32[4,32,512]{2,1,0:T(8,128)S(1)}, u32[]{:S(2)}, u32[]{:S(2)}) collective-permute-start(f32[4,32,512]{2,1,0:T(8,128)S(1)} %get-tuple-element.29), channel_id=1, source_target_pairs={{0,16},{16,0},{1,17},{17,1},{2,18},{18,2},{3,19},{19,3},{4,20},{20... | collective-permute-start | bytes 786440 | tf_op jit(solution)/shard_map/ppermute | solution.py:281
  8.3 0.9 %copy-done.1 = f32[2,4,64,128]{3,2,1,0:T(8,128)S(1)} copy-done((f32[2,4,64,128]{3,2,1,0:T(8,128)S(1)}, f32[2,4,64,128]{3,2,1,0:T(8,128)}, u32[]{:S(2)}) %copy-start.1) | copy-done | bytes 262168
  9.2 1.1 %tables.1 = (bf16[4,1024,256]{2,1,0:T(8,128)(2,1)S(1)}, bf16[4,1024,256]{2,1,0:T(8,128)(2,1)S(1)}) custom-call(f32[2,4,64,128]{3,2,1,0:T(8,128)S(1)} %copy-done.1), custom_call_target="tpu_custom_call" | custom-call | tf_op jit(solution)/shard_map/tables/pallas_call | solution.py:111
  10.3 0.8 %clamp_multiply_fusion.refs_4_ = f32[8,32,128]{2,1,0:T(8,128)S(1)} fusion(s32[8]{0:T(128)} %param.10, s32[8]{0:T(128)} %param.9, s32[32]{0:T(128)S(1)} %iota_add_fusion, f32[8]{0:T(128)} %param.8), kind=kLoop, calls=%fused_computation | loop fusion | flops 393216 | bytes 131296 | tf_op jit(solution)/shard_map/mul | solution.py:127
  11.2 3.1 %collective-permute-done.2.refs_1_ = f32[4,32,512]{2,1,0:T(8,128)S(1)} collective-permute-done((f32[4,32,512]{2,1,0:T(8,128)S(1)}, f32[4,32,512]{2,1,0:T(8,128)S(1)}, u32[]{:S(2)}, u32[]{:S(2)}) %collective-permute-start.2) | collective-permute-done | bytes 262176 | tf_op jit(solution)/shard_map/ppermute | solution.py:281
  14.2 1.0 %transform.4 = (f32[2,2,128,128]{3,2,1,0:T(8,128)S(1)}, f32[2,2,128,128]{3,2,1,0:T(8,128)S(1)}) custom-call(f32[4,32,512]{2,1,0:T(8,128)S(1)} %get-tuple-element.30.refs_0_, f32[4,32,512]{2,1,0:T(8,128)S(1)} %collective-permute-done.2.refs_1_, bf16[4,1024,256]{2,1,0:T(8,128)(2,1)S(1)} %get-tuple-element.17.refs_2_.refs_3_.refs_1_, ...), custom_call_target="tpu_custom_call" | custom-call | tf_op jit(solution)/shard_map/transform/pallas_call | solution.py:184
  15.2 0.1 collective-permute-start.5
  15.3 1.6 %collective-permute-start.6 = (f32[2,2,128,128]{3,2,1,0:T(8,128)S(1)}, f32[2,2,128,128]{3,2,1,0:T(8,128)S(1)}, u32[]{:S(2)}, u32[]{:S(2)}) collective-permute-start(f32[2,2,128,128]{3,2,1,0:T(8,128)S(1)} %get-tuple-element.24), channel_id=1, source_target_pairs={{0,2},{1,3},{2,0},{3,1},{4,6},{5,7},{6,4},{7,5},{8,10},{9,11},{10,... | collective-permute-start | bytes 786440 | tf_op jit(solution)/shard_map/ppermute | solution.py:281
  16.9 0.0 collective-permute-done.1.refs_0_
  16.9 0.0 collective-permute-done.array_ref.refs_2_
  16.9 1.1 %collective-permute-start.4 = (f32[5,32,256]{2,1,0:T(8,128)S(1)}, f32[5,32,256]{2,1,0:T(8,128)S(1)}, u32[]{:S(2)}, u32[]{:S(2)}) collective-permute-start(f32[5,32,256]{2,1,0:T(8,128)S(1)} %pick.2.refs_5_), channel_id=1, source_target_pairs={{0,4},{4,0},{8,12},{12,8},{1,5},{5,1},{9,13},{13,9},{2,6},{6,2},{1... | collective-permute-start | bytes 491528 | tf_op jit(solution)/shard_map/ppermute | solution.py:281
  18.0 1.5 %collective-permute-start.9 = (f32[2,2,128,128]{3,2,1,0:T(8,128)S(1)}, f32[2,2,128,128]{3,2,1,0:T(8,128)S(1)}, u32[]{:S(2)}, u32[]{:S(2)}) collective-permute-start(f32[2,2,128,128]{3,2,1,0:T(8,128)S(1)} %get-tuple-element.19.refs_1_.refs_0_), channel_id=1, source_target_pairs={{0,16},{16,0},{1,17},{17,1},{2,18},{18,2},{3,19},{19,3},{4,20},{20... | collective-permute-start | bytes 786440 | tf_op jit(solution)/shard_map/ppermute | solution.py:281
  19.5 1.4 %transform.5 = (f32[2,2,160,128]{3,2,1,0:T(8,128)S(1)}, f32[2,2,96,128]{3,2,1,0:T(8,128)S(1)}, f32[2,2,160,128]{3,2,1,0:T(8,128)S(1)}, f32[2,2,96,128]{3,2,1,0:T(8,128)S(1)}) custom-call(f32[8,32,256]{2,1,0:T(8,128)S(1)} %copy-done, f32[8,32,256]{2,1,0:T(8,128)S(1)} %order.5.refs_1_, f32[8,32,256]{2,1,0:T(8,128)S(1)} %collective-permute-done.array_ref.refs_2_, ...), custom_call_target="tpu_custom_call" | custom-call | flops 1000000000 | tf_op jit(solution)/shard_map/transform/pallas_call | solution.py:184
  21.0 1.0 %collective-permute-start.3 = (f32[3,32,256]{2,1,0:T(8,128)S(1)}, f32[3,32,256]{2,1,0:T(8,128)S(1)}, u32[]{:S(2)}, u32[]{:S(2)}) collective-permute-start(f32[3,32,256]{2,1,0:T(8,128)S(1)} %pick.3), channel_id=1, source_target_pairs={{0,4},{4,0},{8,12},{12,8},{1,5},{5,1},{9,13},{13,9},{2,6},{6,2},{1... | collective-permute-start | bytes 294920 | tf_op jit(solution)/shard_map/ppermute | solution.py:281
  22.0 1.9 %collective-permute-done.4.refs_0_ = f32[5,32,256]{2,1,0:T(8,128)S(1)} collective-permute-done((f32[5,32,256]{2,1,0:T(8,128)S(1)}, f32[5,32,256]{2,1,0:T(8,128)S(1)}, u32[]{:S(2)}, u32[]{:S(2)}) %collective-permute-start.4) | collective-permute-done | bytes 163872 | tf_op jit(solution)/shard_map/ppermute | solution.py:281
  23.9 0.0 collective-permute-done.5.refs_5_.refs_4_
  23.9 0.2 collective-permute-done.6.refs_6_.refs_0_
  24.0 0.4 %transform.6 = (f32[2,2,160,128]{3,2,1,0:T(8,128)S(1)}, f32[2,2,160,128]{3,2,1,0:T(8,128)S(1)}) custom-call(f32[5,32,256]{2,1,0:T(8,128)S(1)} %collective-permute-done.4.refs_0_, bf16[4,1024,256]{2,1,0:T(8,128)(2,1)S(1)} %get-tuple-element.17.refs_2_.refs_3_.refs_1_, bf16[4,1024,256]{2,1,0:T(8,128)(2,1)S(1)} %get-tuple-element.18.refs_3_.refs_4_.refs_2_, ...), custom_call_target="tpu_custom_call" | custom-call | flops 2500000000 | tf_op jit(solution)/shard_map/transform/pallas_call | solution.py:184
  24.5 1.6 %collective-permute-start.8 = (f32[2,2,160,128]{3,2,1,0:T(8,128)S(1)}, f32[2,2,160,128]{3,2,1,0:T(8,128)S(1)}, u32[]{:S(2)}, u32[]{:S(2)}) collective-permute-start(f32[2,2,160,128]{3,2,1,0:T(8,128)S(1)} %get-tuple-element.27), channel_id=1, source_target_pairs={{0,2},{1,3},{2,0},{3,1},{4,6},{5,7},{6,4},{7,5},{8,10},{9,11},{10,... | collective-permute-start | bytes 983048 | tf_op jit(solution)/shard_map/ppermute | solution.py:281
  26.1 0.0 collective-permute-start.10
  26.1 0.0 collective-permute-done.9.refs_2_
  26.1 0.6 %collective-permute-start.11 = (f32[2,2,128,128]{3,2,1,0:T(8,128)S(1)}, f32[2,2,128,128]{3,2,1,0:T(8,128)S(1)}, u32[]{:S(2)}, u32[]{:S(2)}) collective-permute-start(f32[2,2,128,128]{3,2,1,0:T(8,128)S(1)} %order.6), channel_id=1, source_target_pairs={{0,1},{1,0},{2,3},{3,2},{4,5},{5,4},{6,7},{7,6},{8,9},{9,8},{10,11... | collective-permute-start | bytes 786440 | tf_op jit(solution)/shard_map/ppermute | solution.py:281
  26.7 0.0 collective-permute-done.3.refs_0_
  26.7 0.4 transform.7
  27.1 1.6 %collective-permute-start.12 = (f32[2,2,128,128]{3,2,1,0:T(8,128)S(1)}, f32[2,2,128,128]{3,2,1,0:T(8,128)S(1)}, u32[]{:S(2)}, u32[]{:S(2)}) collective-permute-start(f32[2,2,128,128]{3,2,1,0:T(8,128)S(1)} %order.8.refs_1_), channel_id=1, source_target_pairs={{0,16},{16,0},{1,17},{17,1},{2,18},{18,2},{3,19},{19,3},{4,20},{20... | collective-permute-start | bytes 786440 | tf_op jit(solution)/shard_map/ppermute | solution.py:281
  28.6 0.0 collective-permute-start.13
  28.6 0.0 collective-permute-done.11.refs_5_.refs_4_
  28.6 0.5 %collective-permute-start.7 = (f32[2,2,96,128]{3,2,1,0:T(8,128)S(1)}, f32[2,2,96,128]{3,2,1,0:T(8,128)S(1)}, u32[]{:S(2)}, u32[]{:S(2)}) collective-permute-start(f32[2,2,96,128]{3,2,1,0:T(8,128)S(1)} %get-tuple-element.26), channel_id=1, source_target_pairs={{0,2},{1,3},{2,0},{3,1},{4,6},{5,7},{6,4},{7,5},{8,10},{9,11},{10,... | collective-permute-start | bytes 589832 | tf_op jit(solution)/shard_map/ppermute | solution.py:281
  29.2 0.0 collective-permute-done.10.refs_3_
  29.2 2.1 %product.4.refs_1_.refs_5_ = f32[2,32,32,128]{3,2,1,0:T(8,128)S(1)} custom-call(f32[2,2,160,128]{3,2,1,0:T(8,128)S(1)} %get-tuple-element.25.refs_5_.refs_1_.refs_0_, f32[2,2,128,128]{3,2,1,0:T(8,128)S(1)} %get-tuple-element.19.refs_1_.refs_0_, f32[2,2,128,128]{3,2,1,0:T(8,128)S(1)} %collective-permute-done.9.refs_2_, ...), custom_call_target="tpu_custom_call" | custom-call | tf_op jit(solution)/shard_map/product/pallas_call | solution.py:268
  31.3 3.9 %collective-permute-done.8.refs_0_ = f32[2,2,160,128]{3,2,1,0:T(8,128)S(1)} collective-permute-done((f32[2,2,160,128]{3,2,1,0:T(8,128)S(1)}, f32[2,2,160,128]{3,2,1,0:T(8,128)S(1)}, u32[]{:S(2)}, u32[]{:S(2)}) %collective-permute-start.8) | collective-permute-done | bytes 327712 | tf_op jit(solution)/shard_map/ppermute | solution.py:281
  35.2 0.0 collective-permute-start.16
  35.2 0.5 %collective-permute-start.17 = (f32[2,2,128,128]{3,2,1,0:T(8,128)S(1)}, f32[2,2,128,128]{3,2,1,0:T(8,128)S(1)}, u32[]{:S(2)}, u32[]{:S(2)}) collective-permute-start(f32[2,2,128,128]{3,2,1,0:T(8,128)S(1)} %order.8.refs_1_), channel_id=1, source_target_pairs={{0,1},{1,0},{2,3},{3,2},{4,5},{5,4},{6,7},{7,6},{8,9},{9,8},{10,11... | collective-permute-start | bytes 786440 | tf_op jit(solution)/shard_map/ppermute | solution.py:281
  35.7 0.0 collective-permute-done.12.refs_2_.refs_4_
  35.7 0.0 collective-permute-start.15
  35.7 0.0 collective-permute-done.13.refs_3_
  35.7 1.3 %product.5.refs_1_.refs_5_ = f32[2,32,32,128]{3,2,1,0:T(8,128)S(1)} custom-call(f32[2,2,160,128]{3,2,1,0:T(8,128)S(1)} %order.7.refs_0_, f32[2,2,128,128]{3,2,1,0:T(8,128)S(1)} %order.8.refs_1_, f32[2,2,128,128]{3,2,1,0:T(8,128)S(1)} %collective-permute-done.12.refs_2_.refs_4_, f32[2,2,96,128]{3,2,1,0:T(8,128)S(1)} %collective-permute-done.13.refs_3_, ...), custom_call_target="tpu_custom_call" | custom-call | tf_op jit(solution)/shard_map/product/pallas_call | solution.py:268
  37.0 1.0 %collective-permute-done.7.refs_0_ = f32[2,2,96,128]{3,2,1,0:T(8,128)S(1)} collective-permute-done((f32[2,2,96,128]{3,2,1,0:T(8,128)S(1)}, f32[2,2,96,128]{3,2,1,0:T(8,128)S(1)}, u32[]{:S(2)}, u32[]{:S(2)}) %collective-permute-start.7) | collective-permute-done | bytes 196640 | tf_op jit(solution)/shard_map/ppermute | solution.py:281
  38.0 0.0 collective-permute-start.14
  38.0 0.0 collective-permute-done.17.refs_1_
  38.0 0.0 collective-permute-done.15.refs_2_.refs_6_.refs_1_
  38.0 0.0 collective-permute-done.16.refs_0_
  38.1 1.3 %product.6.refs_2_ = f32[2,32,32,128]{3,2,1,0:T(8,128)S(1)} custom-call(f32[2,2,160,128]{3,2,1,0:T(8,128)S(1)} %collective-permute-done.16.refs_0_, f32[2,2,128,128]{3,2,1,0:T(8,128)S(1)} %collective-permute-done.17.refs_1_, f32[2,2,128,128]{3,2,1,0:T(8,128)S(1)} %collective-permute-done.15.refs_2_.refs_6_.refs_1_, f32[2,2,96,128]{3,2,1,0:T(8,128)S(1)} %order.9.refs_3_, ...), custom_call_target="tpu_custom_call" | custom-call | tf_op jit(solution)/shard_map/product/pallas_call | solution.py:268
  39.4 0.1 collective-permute-done.14.refs_0_
  39.5 1.3 %product.7 = f32[2,32,32,128]{3,2,1,0:T(8,128)} custom-call(f32[2,2,96,128]{3,2,1,0:T(8,128)S(1)} %collective-permute-done.14.refs_0_, f32[2,2,128,128]{3,2,1,0:T(8,128)S(1)} %collective-permute-done.15.refs_2_.refs_6_.refs_1_, f32[2,32,32,128]{3,2,1,0:T(8,128)S(1)} %product.6.refs_2_), custom_call_target="tpu_custom_call" | custom-call | tf_op jit(solution)/shard_map/product/pallas_call | solution.py:268
  (12 shorter events, 0.1 us)
Async XLA Ops:
  0.0 16.9 %collective-permute-start = (f32[8,32,256]{2,1,0:T(8,128)}, f32[8,32,256]{2,1,0:T(8,128)S(1)}, u32[]{:S(2)}, u32[]{:S(2)}) collective-permute-start(f32[8,32,256]{2,1,0:T(8,128)} %refs_0_.1), channel_id=1, source_target_pairs={{0,8},{4,12},{8,0},{12,4},{1,9},{5,13},{9,1},{13,5},{2,10},{6,14},... | collective-permute-start | bytes 786440 | tf_op jit(solution)/shard_map/ppermute | solution.py:281
  4.0 12.9 %collective-permute-start.1 = (f32[8,32,256]{2,1,0:T(8,128)}, f32[8,32,256]{2,1,0:T(8,128)S(1)}, u32[]{:S(2)}, u32[]{:S(2)}) collective-permute-start(f32[8,32,256]{2,1,0:T(8,128)} %refs_0_.1), channel_id=1, source_target_pairs={{0,4},{4,0},{8,12},{12,8},{1,5},{5,1},{9,13},{13,9},{2,6},{6,2},{1... | collective-permute-start | bytes 786440 | tf_op jit(solution)/shard_map/ppermute | solution.py:281
  6.7 7.6 %collective-permute-start.2 = (f32[4,32,512]{2,1,0:T(8,128)S(1)}, f32[4,32,512]{2,1,0:T(8,128)S(1)}, u32[]{:S(2)}, u32[]{:S(2)}) collective-permute-start(f32[4,32,512]{2,1,0:T(8,128)S(1)} %get-tuple-element.29), channel_id=1, source_target_pairs={{0,16},{16,0},{1,17},{17,1},{2,18},{18,2},{3,19},{19,3},{4,20},{20... | collective-permute-start | bytes 786440 | tf_op jit(solution)/shard_map/ppermute | solution.py:281
  8.3 0.9 %copy-start.1 = (f32[2,4,64,128]{3,2,1,0:T(8,128)S(1)}, f32[2,4,64,128]{3,2,1,0:T(8,128)}, u32[]{:S(2)}) copy-start(f32[2,4,64,128]{3,2,1,0:T(8,128)} %constant.32.clone.angles_ref) | copy-start | bytes 786436
  15.2 8.6 %collective-permute-start.5 = (f32[2,2,128,128]{3,2,1,0:T(8,128)S(1)}, f32[2,2,128,128]{3,2,1,0:T(8,128)S(1)}, u32[]{:S(2)}, u32[]{:S(2)}) collective-permute-start(f32[2,2,128,128]{3,2,1,0:T(8,128)S(1)} %get-tuple-element.19.refs_1_.refs_0_), channel_id=1, source_target_pairs={{0,1},{1,0},{2,3},{3,2},{4,5},{5,4},{6,7},{7,6},{8,9},{9,8},{10,11... | collective-permute-start | bytes 786440 | tf_op jit(solution)/shard_map/ppermute | solution.py:281
  15.3 8.7 %collective-permute-start.6 = (f32[2,2,128,128]{3,2,1,0:T(8,128)S(1)}, f32[2,2,128,128]{3,2,1,0:T(8,128)S(1)}, u32[]{:S(2)}, u32[]{:S(2)}) collective-permute-start(f32[2,2,128,128]{3,2,1,0:T(8,128)S(1)} %get-tuple-element.24), channel_id=1, source_target_pairs={{0,2},{1,3},{2,0},{3,1},{4,6},{5,7},{6,4},{7,5},{8,10},{9,11},{10,... | collective-permute-start | bytes 786440 | tf_op jit(solution)/shard_map/ppermute | solution.py:281
  16.9 2.6 %copy-start = (f32[8,32,256]{2,1,0:T(8,128)S(1)}, f32[8,32,256]{2,1,0:T(8,128)}, u32[]{:S(2)}) copy-start(f32[8,32,256]{2,1,0:T(8,128)} %refs_0_.1) | copy-start | bytes 786436
  16.9 6.9 %collective-permute-start.4 = (f32[5,32,256]{2,1,0:T(8,128)S(1)}, f32[5,32,256]{2,1,0:T(8,128)S(1)}, u32[]{:S(2)}, u32[]{:S(2)}) collective-permute-start(f32[5,32,256]{2,1,0:T(8,128)S(1)} %pick.2.refs_5_), channel_id=1, source_target_pairs={{0,4},{4,0},{8,12},{12,8},{1,5},{5,1},{9,13},{13,9},{2,6},{6,2},{1... | collective-permute-start | bytes 491528 | tf_op jit(solution)/shard_map/ppermute | solution.py:281
  18.0 8.0 %collective-permute-start.9 = (f32[2,2,128,128]{3,2,1,0:T(8,128)S(1)}, f32[2,2,128,128]{3,2,1,0:T(8,128)S(1)}, u32[]{:S(2)}, u32[]{:S(2)}) collective-permute-start(f32[2,2,128,128]{3,2,1,0:T(8,128)S(1)} %get-tuple-element.19.refs_1_.refs_0_), channel_id=1, source_target_pairs={{0,16},{16,0},{1,17},{17,1},{2,18},{18,2},{3,19},{19,3},{4,20},{20... | collective-permute-start | bytes 786440 | tf_op jit(solution)/shard_map/ppermute | solution.py:281
  21.0 5.7 %collective-permute-start.3 = (f32[3,32,256]{2,1,0:T(8,128)S(1)}, f32[3,32,256]{2,1,0:T(8,128)S(1)}, u32[]{:S(2)}, u32[]{:S(2)}) collective-permute-start(f32[3,32,256]{2,1,0:T(8,128)S(1)} %pick.3), channel_id=1, source_target_pairs={{0,4},{4,0},{8,12},{12,8},{1,5},{5,1},{9,13},{13,9},{2,6},{6,2},{1... | collective-permute-start | bytes 294920 | tf_op jit(solution)/shard_map/ppermute | solution.py:281
  24.5 10.7 %collective-permute-start.8 = (f32[2,2,160,128]{3,2,1,0:T(8,128)S(1)}, f32[2,2,160,128]{3,2,1,0:T(8,128)S(1)}, u32[]{:S(2)}, u32[]{:S(2)}) collective-permute-start(f32[2,2,160,128]{3,2,1,0:T(8,128)S(1)} %get-tuple-element.27), channel_id=1, source_target_pairs={{0,2},{1,3},{2,0},{3,1},{4,6},{5,7},{6,4},{7,5},{8,10},{9,11},{10,... | collective-permute-start | bytes 983048 | tf_op jit(solution)/shard_map/ppermute | solution.py:281
  26.1 3.1 %collective-permute-start.10 = (f32[2,2,160,128]{3,2,1,0:T(8,128)S(1)}, f32[2,2,160,128]{3,2,1,0:T(8,128)S(1)}, u32[]{:S(2)}, u32[]{:S(2)}) collective-permute-start(f32[2,2,160,128]{3,2,1,0:T(8,128)S(1)} %get-tuple-element.25.refs_5_.refs_1_.refs_0_), channel_id=1, source_target_pairs={{0,1},{1,0},{2,3},{3,2},{4,5},{5,4},{6,7},{7,6},{8,9},{9,8},{10,11... | collective-permute-start | bytes 983048 | tf_op jit(solution)/shard_map/ppermute | solution.py:281
  26.1 2.5 %collective-permute-start.11 = (f32[2,2,128,128]{3,2,1,0:T(8,128)S(1)}, f32[2,2,128,128]{3,2,1,0:T(8,128)S(1)}, u32[]{:S(2)}, u32[]{:S(2)}) collective-permute-start(f32[2,2,128,128]{3,2,1,0:T(8,128)S(1)} %order.6), channel_id=1, source_target_pairs={{0,1},{1,0},{2,3},{3,2},{4,5},{5,4},{6,7},{7,6},{8,9},{9,8},{10,11... | collective-permute-start | bytes 786440 | tf_op jit(solution)/shard_map/ppermute | solution.py:281
  27.1 8.6 %collective-permute-start.12 = (f32[2,2,128,128]{3,2,1,0:T(8,128)S(1)}, f32[2,2,128,128]{3,2,1,0:T(8,128)S(1)}, u32[]{:S(2)}, u32[]{:S(2)}) collective-permute-start(f32[2,2,128,128]{3,2,1,0:T(8,128)S(1)} %order.8.refs_1_), channel_id=1, source_target_pairs={{0,16},{16,0},{1,17},{17,1},{2,18},{18,2},{3,19},{19,3},{4,20},{20... | collective-permute-start | bytes 786440 | tf_op jit(solution)/shard_map/ppermute | solution.py:281
  28.6 7.1 %collective-permute-start.13 = (f32[2,2,96,128]{3,2,1,0:T(8,128)S(1)}, f32[2,2,96,128]{3,2,1,0:T(8,128)S(1)}, u32[]{:S(2)}, u32[]{:S(2)}) collective-permute-start(f32[2,2,96,128]{3,2,1,0:T(8,128)S(1)} %get-tuple-element.28.refs_6_.refs_1_), channel_id=1, source_target_pairs={{0,1},{1,0},{2,3},{3,2},{4,5},{5,4},{6,7},{7,6},{8,9},{9,8},{10,11... | collective-permute-start | bytes 589832 | tf_op jit(solution)/shard_map/ppermute | solution.py:281
  28.6 9.4 %collective-permute-start.7 = (f32[2,2,96,128]{3,2,1,0:T(8,128)S(1)}, f32[2,2,96,128]{3,2,1,0:T(8,128)S(1)}, u32[]{:S(2)}, u32[]{:S(2)}) collective-permute-start(f32[2,2,96,128]{3,2,1,0:T(8,128)S(1)} %get-tuple-element.26), channel_id=1, source_target_pairs={{0,2},{1,3},{2,0},{3,1},{4,6},{5,7},{6,4},{7,5},{8,10},{9,11},{10,... | collective-permute-start | bytes 589832 | tf_op jit(solution)/shard_map/ppermute | solution.py:281
  35.2 2.9 %collective-permute-start.16 = (f32[2,2,160,128]{3,2,1,0:T(8,128)S(1)}, f32[2,2,160,128]{3,2,1,0:T(8,128)S(1)}, u32[]{:S(2)}, u32[]{:S(2)}) collective-permute-start(f32[2,2,160,128]{3,2,1,0:T(8,128)S(1)} %order.7.refs_0_), channel_id=1, source_target_pairs={{0,1},{1,0},{2,3},{3,2},{4,5},{5,4},{6,7},{7,6},{8,9},{9,8},{10,11... | collective-permute-start | bytes 983048 | tf_op jit(solution)/shard_map/ppermute | solution.py:281
  35.2 2.9 %collective-permute-start.17 = (f32[2,2,128,128]{3,2,1,0:T(8,128)S(1)}, f32[2,2,128,128]{3,2,1,0:T(8,128)S(1)}, u32[]{:S(2)}, u32[]{:S(2)}) collective-permute-start(f32[2,2,128,128]{3,2,1,0:T(8,128)S(1)} %order.8.refs_1_), channel_id=1, source_target_pairs={{0,1},{1,0},{2,3},{3,2},{4,5},{5,4},{6,7},{7,6},{8,9},{9,8},{10,11... | collective-permute-start | bytes 786440 | tf_op jit(solution)/shard_map/ppermute | solution.py:281
  35.7 2.4 %collective-permute-start.15 = (f32[2,2,128,128]{3,2,1,0:T(8,128)S(1)}, f32[2,2,128,128]{3,2,1,0:T(8,128)S(1)}, u32[]{:S(2)}, u32[]{:S(2)}) collective-permute-start(f32[2,2,128,128]{3,2,1,0:T(8,128)S(1)} %collective-permute-done.12.refs_2_.refs_4_), channel_id=1, source_target_pairs={{0,1},{1,0},{2,3},{3,2},{4,5},{5,4},{6,7},{7,6},{8,9},{9,8},{10,11... | collective-permute-start | bytes 786440 | tf_op jit(solution)/shard_map/ppermute | solution.py:281
  38.0 1.4 %collective-permute-start.14 = (f32[2,2,96,128]{3,2,1,0:T(8,128)S(1)}, f32[2,2,96,128]{3,2,1,0:T(8,128)S(1)}, u32[]{:S(2)}, u32[]{:S(2)}) collective-permute-start(f32[2,2,96,128]{3,2,1,0:T(8,128)S(1)} %order.9.refs_3_), channel_id=1, source_target_pairs={{0,1},{1,0},{2,3},{3,2},{4,5},{5,4},{6,7},{7,6},{8,9},{9,8},{10,11... | collective-permute-start | bytes 589832 | tf_op jit(solution)/shard_map/ppermute | solution.py:281

commit v5 on v4

--- a/solution.py
+++ b/solution.py
@@ -338,11 +338,10 @@
         cut = points - 3 * points // 8
         even = gather(shot_traces, "rcv", n_rcv, 2)
         beside = exchange(shot_traces, "rcv", n_rcv, 1)
-        beside = late(beside, token)
         edges = (0, cut, points)
         shot_transform = functools.partial(transform, table=table, axis="rcv", part=part, points=points)
         near = {0: shot_traces, 1: beside} | {2 * j: piece for j, piece in enumerate(even[1:], 1)}
-        first = [pick(piece, edges[:2], part, [token, beside], 3 * 10**9) for piece in even[1:]]
+        first = [pick(piece, edges[:2], part, [token], 3 * 10**9) for piece in even[1:]]
         out = shot_transform(
             near, low=0, high=points, cuts=[(cut,)] * len(chips), after=[p[0] for p in first], flops=10**9
         )

time: 40.9 us -> 40.9 us (level)
  no operation moved by 1% of the time
where the time goes in v5:
time: 40.9 us; the launch traced here: 40.7 us
  starting transfers between devices  17.2 us (42%)
  Pallas kernels  10.5 us (26%)
  waiting for transfers between devices  10.1 us (25%)
  local copies, waits for them, and re-layouts  2.04 us (5%)
  other arithmetic  0.81 us (2%)
    ppermute x18, starting transfers between devices, exchange(): return lax.ppermute(block, axis, [(i, i ^ step) for i in range(size)])  17.2 us
    ppermute x18, waiting for transfers between devices, exchange(): return lax.ppermute(block, axis, [(i, i ^ step) for i in range(size)])  10.1 us
    pallas_call x4, Pallas kernels, product(): pl.pallas_call(lambda *refs: product_kernel(described, len(blocks), len(c...  6.1 us
    pallas_call x4, Pallas kernels, transform(): pl.pallas_call(lambda *refs: transform_kernel(steps, len(taper), len(adde...  3.19 us
    pallas_call x1, Pallas kernels, tables(): pl.pallas_call(tables_kernel, out_shape=out, in_specs=[VMEM], out_specs=[...  1.13 us
    dynamic_slice x1, local copies, waits for them, and re-layouts, own(): return lax.dynamic_slice_in_dim(array, (me ^ j) * part, part)  1.07 us
    unnamed x5, local copies, waits for them, and re-layouts  0.97 us
  transfers between devices with their start and end apart: 18, of which 6 were waited for; matrix products, arithmetic and copies ran while one was open for 5% of the time, Pallas kernels for 23%

profile of v5, /device:TPU:0, one launch (start us, length us, event | category | flops | bytes accessed | tf_op | source)
XLA Modules:
  0.0 40.7 jit_solution(10913658731488620237)
XLA Ops:
  0.0 4.0 %collective-permute-start = (f32[8,32,256]{2,1,0:T(8,128)}, f32[8,32,256]{2,1,0:T(8,128)S(1)}, u32[]{:S(2)}, u32[]{:S(2)}) collective-permute-start(f32[8,32,256]{2,1,0:T(8,128)} %refs_0_.1), channel_id=1, source_target_pairs={{0,8},{4,12},{8,0},{12,4},{1,9},{5,13},{9,1},{13,5},{2,10},{6,14},... | collective-permute-start | bytes 786440 | tf_op jit(solution)/shard_map/ppermute | solution.py:281
  4.0 1.6 %collective-permute-start.1 = (f32[8,32,256]{2,1,0:T(8,128)}, f32[8,32,256]{2,1,0:T(8,128)S(1)}, u32[]{:S(2)}, u32[]{:S(2)}) collective-permute-start(f32[8,32,256]{2,1,0:T(8,128)} %refs_0_.1), channel_id=1, source_target_pairs={{0,4},{4,0},{8,12},{12,8},{1,5},{5,1},{9,13},{13,9},{2,6},{6,2},{1... | collective-permute-start | bytes 786440 | tf_op jit(solution)/shard_map/ppermute | solution.py:281
  5.6 1.1 %constant_dynamic-slice_fusion = (f32[4,32,512]{2,1,0:T(8,128)S(1)}, f32[4,32,512]{2,1,0:T(8,128)S(1)}) fusion(f32[8,32,512]{2,1,0:T(8,128)} %param.7, s32[]{:T(128)S(6)} %select_n.7, s32[]{:T(128)S(6)} %select_n.6), kind=kLoop, calls=%fused_computation.2 | loop fusion | bytes 1048584 | tf_op jit(solution)/shard_map/dynamic_slice | solution.py:303
  6.7 1.6 %collective-permute-start.2 = (f32[4,32,512]{2,1,0:T(8,128)S(1)}, f32[4,32,512]{2,1,0:T(8,128)S(1)}, u32[]{:S(2)}, u32[]{:S(2)}) collective-permute-start(f32[4,32,512]{2,1,0:T(8,128)S(1)} %get-tuple-element.29), channel_id=1, source_target_pairs={{0,16},{16,0},{1,17},{17,1},{2,18},{18,2},{3,19},{19,3},{4,20},{20... | collective-permute-start | bytes 786440 | tf_op jit(solution)/shard_map/ppermute | solution.py:281
  8.3 0.9 %copy-done.1 = f32[2,4,64,128]{3,2,1,0:T(8,128)S(1)} copy-done((f32[2,4,64,128]{3,2,1,0:T(8,128)S(1)}, f32[2,4,64,128]{3,2,1,0:T(8,128)}, u32[]{:S(2)}) %copy-start.1) | copy-done | bytes 262168
  9.2 1.1 %tables.1 = (bf16[4,1024,256]{2,1,0:T(8,128)(2,1)S(1)}, bf16[4,1024,256]{2,1,0:T(8,128)(2,1)S(1)}) custom-call(f32[2,4,64,128]{3,2,1,0:T(8,128)S(1)} %copy-done.1), custom_call_target="tpu_custom_call" | custom-call | tf_op jit(solution)/shard_map/tables/pallas_call | solution.py:111
  10.3 0.8 %clamp_multiply_fusion.refs_4_ = f32[8,32,128]{2,1,0:T(8,128)S(1)} fusion(s32[8]{0:T(128)} %param.10, s32[8]{0:T(128)} %param.9, s32[32]{0:T(128)S(1)} %iota_add_fusion, f32[8]{0:T(128)} %param.8), kind=kLoop, calls=%fused_computation | loop fusion | flops 393216 | bytes 131296 | tf_op jit(solution)/shard_map/mul | solution.py:127
  11.2 3.1 %collective-permute-done.2.refs_1_ = f32[4,32,512]{2,1,0:T(8,128)S(1)} collective-permute-done((f32[4,32,512]{2,1,0:T(8,128)S(1)}, f32[4,32,512]{2,1,0:T(8,128)S(1)}, u32[]{:S(2)}, u32[]{:S(2)}) %collective-permute-start.2) | collective-permute-done | bytes 262176 | tf_op jit(solution)/shard_map/ppermute | solution.py:281
  14.2 1.0 %transform.4 = (f32[2,2,128,128]{3,2,1,0:T(8,128)S(1)}, f32[2,2,128,128]{3,2,1,0:T(8,128)S(1)}) custom-call(f32[4,32,512]{2,1,0:T(8,128)S(1)} %get-tuple-element.30.refs_0_, f32[4,32,512]{2,1,0:T(8,128)S(1)} %collective-permute-done.2.refs_1_, bf16[4,1024,256]{2,1,0:T(8,128)(2,1)S(1)} %get-tuple-element.17.refs_2_.refs_3_.refs_1_, ...), custom_call_target="tpu_custom_call" | custom-call | tf_op jit(solution)/shard_map/transform/pallas_call | solution.py:184
  15.2 0.1 collective-permute-start.5
  15.3 0.0 copy-start
  15.3 1.6 %collective-permute-start.6 = (f32[2,2,128,128]{3,2,1,0:T(8,128)S(1)}, f32[2,2,128,128]{3,2,1,0:T(8,128)S(1)}, u32[]{:S(2)}, u32[]{:S(2)}) collective-permute-start(f32[2,2,128,128]{3,2,1,0:T(8,128)S(1)} %get-tuple-element.24), channel_id=1, source_target_pairs={{0,2},{1,3},{2,0},{3,1},{4,6},{5,7},{6,4},{7,5},{8,10},{9,11},{10,... | collective-permute-start | bytes 786440 | tf_op jit(solution)/shard_map/ppermute | solution.py:281
  16.9 0.0 collective-permute-done.array_ref.refs_2_
  16.9 0.5 %collective-permute-start.4 = (f32[5,32,256]{2,1,0:T(8,128)S(1)}, f32[5,32,256]{2,1,0:T(8,128)S(1)}, u32[]{:S(2)}, u32[]{:S(2)}) collective-permute-start(f32[5,32,256]{2,1,0:T(8,128)S(1)} %pick.2.refs_5_), channel_id=1, source_target_pairs={{0,4},{4,0},{8,12},{12,8},{1,5},{5,1},{9,13},{13,9},{2,6},{6,2},{1... | collective-permute-start | bytes 491528 | tf_op jit(solution)/shard_map/ppermute | solution.py:281
  17.4 1.5 %collective-permute-start.9 = (f32[2,2,128,128]{3,2,1,0:T(8,128)S(1)}, f32[2,2,128,128]{3,2,1,0:T(8,128)S(1)}, u32[]{:S(2)}, u32[]{:S(2)}) collective-permute-start(f32[2,2,128,128]{3,2,1,0:T(8,128)S(1)} %get-tuple-element.19.refs_0_.refs_1_), channel_id=1, source_target_pairs={{0,16},{16,0},{1,17},{17,1},{2,18},{18,2},{3,19},{19,3},{4,20},{20... | collective-permute-start | bytes 786440 | tf_op jit(solution)/shard_map/ppermute | solution.py:281
  18.9 0.0 collective-permute-done.1.refs_1_
  18.9 1.4 %transform.5 = (f32[2,2,160,128]{3,2,1,0:T(8,128)S(1)}, f32[2,2,96,128]{3,2,1,0:T(8,128)S(1)}, f32[2,2,160,128]{3,2,1,0:T(8,128)S(1)}, f32[2,2,96,128]{3,2,1,0:T(8,128)S(1)}) custom-call(f32[8,32,256]{2,1,0:T(8,128)S(1)} %copy-done, f32[8,32,256]{2,1,0:T(8,128)S(1)} %collective-permute-done.1.refs_1_, ...), custom_call_target="tpu_custom_call" | custom-call | flops 1000000000 | tf_op jit(solution)/shard_map/transform/pallas_call | solution.py:184
  20.4 1.6 %collective-permute-start.3 = (f32[3,32,256]{2,1,0:T(8,128)S(1)}, f32[3,32,256]{2,1,0:T(8,128)S(1)}, u32[]{:S(2)}, u32[]{:S(2)}) collective-permute-start(f32[3,32,256]{2,1,0:T(8,128)S(1)} %pick.3), channel_id=1, source_target_pairs={{0,4},{4,0},{8,12},{12,8},{1,5},{5,1},{9,13},{13,9},{2,6},{6,2},{1... | collective-permute-start | bytes 294920 | tf_op jit(solution)/shard_map/ppermute | solution.py:281
  22.0 1.8 %collective-permute-done.4.refs_0_ = f32[5,32,256]{2,1,0:T(8,128)S(1)} collective-permute-done((f32[5,32,256]{2,1,0:T(8,128)S(1)}, f32[5,32,256]{2,1,0:T(8,128)S(1)}, u32[]{:S(2)}, u32[]{:S(2)}) %collective-permute-start.4) | collective-permute-done | bytes 163872 | tf_op jit(solution)/shard_map/ppermute | solution.py:281
  23.8 0.0 collective-permute-done.5.refs_5_.refs_4_
  23.8 0.2 collective-permute-done.6.refs_6_.refs_0_
  24.0 0.4 %transform.6 = (f32[2,2,160,128]{3,2,1,0:T(8,128)S(1)}, f32[2,2,160,128]{3,2,1,0:T(8,128)S(1)}) custom-call(f32[5,32,256]{2,1,0:T(8,128)S(1)} %collective-permute-done.4.refs_0_, bf16[4,1024,256]{2,1,0:T(8,128)(2,1)S(1)} %get-tuple-element.17.refs_2_.refs_3_.refs_1_, bf16[4,1024,256]{2,1,0:T(8,128)(2,1)S(1)} %get-tuple-element.18.refs_3_.refs_4_.refs_2_, ...), custom_call_target="tpu_custom_call" | custom-call | flops 2500000000 | tf_op jit(solution)/shard_map/transform/pallas_call | solution.py:184
  24.5 1.6 %collective-permute-start.8 = (f32[2,2,160,128]{3,2,1,0:T(8,128)S(1)}, f32[2,2,160,128]{3,2,1,0:T(8,128)S(1)}, u32[]{:S(2)}, u32[]{:S(2)}) collective-permute-start(f32[2,2,160,128]{3,2,1,0:T(8,128)S(1)} %get-tuple-element.27), channel_id=1, source_target_pairs={{0,2},{1,3},{2,0},{3,1},{4,6},{5,7},{6,4},{7,5},{8,10},{9,11},{10,... | collective-permute-start | bytes 983048 | tf_op jit(solution)/shard_map/ppermute | solution.py:281
  26.1 0.0 collective-permute-start.10
  26.1 0.0 collective-permute-done.9.refs_2_
  26.1 0.6 %collective-permute-start.11 = (f32[2,2,128,128]{3,2,1,0:T(8,128)S(1)}, f32[2,2,128,128]{3,2,1,0:T(8,128)S(1)}, u32[]{:S(2)}, u32[]{:S(2)}) collective-permute-start(f32[2,2,128,128]{3,2,1,0:T(8,128)S(1)} %order.4), channel_id=1, source_target_pairs={{0,1},{1,0},{2,3},{3,2},{4,5},{5,4},{6,7},{7,6},{8,9},{9,8},{10,11... | collective-permute-start | bytes 786440 | tf_op jit(solution)/shard_map/ppermute | solution.py:281
  26.7 0.0 collective-permute-done.3.refs_0_
  26.7 0.4 transform.7
  27.1 1.6 %collective-permute-start.12 = (f32[2,2,128,128]{3,2,1,0:T(8,128)S(1)}, f32[2,2,128,128]{3,2,1,0:T(8,128)S(1)}, u32[]{:S(2)}, u32[]{:S(2)}) collective-permute-start(f32[2,2,128,128]{3,2,1,0:T(8,128)S(1)} %order.6.refs_1_), channel_id=1, source_target_pairs={{0,16},{16,0},{1,17},{17,1},{2,18},{18,2},{3,19},{19,3},{4,20},{20... | collective-permute-start | bytes 786440 | tf_op jit(solution)/shard_map/ppermute | solution.py:281
  28.6 0.0 collective-permute-start.13
  28.6 0.0 collective-permute-done.11.refs_5_.refs_4_
  28.6 0.5 %collective-permute-start.7 = (f32[2,2,96,128]{3,2,1,0:T(8,128)S(1)}, f32[2,2,96,128]{3,2,1,0:T(8,128)S(1)}, u32[]{:S(2)}, u32[]{:S(2)}) collective-permute-start(f32[2,2,96,128]{3,2,1,0:T(8,128)S(1)} %get-tuple-element.26), channel_id=1, source_target_pairs={{0,2},{1,3},{2,0},{3,1},{4,6},{5,7},{6,4},{7,5},{8,10},{9,11},{10,... | collective-permute-start | bytes 589832 | tf_op jit(solution)/shard_map/ppermute | solution.py:281
  29.2 0.0 collective-permute-done.10.refs_3_
  29.2 2.1 %product.4.refs_1_.refs_5_ = f32[2,32,32,128]{3,2,1,0:T(8,128)S(1)} custom-call(f32[2,2,160,128]{3,2,1,0:T(8,128)S(1)} %get-tuple-element.25.refs_5_.refs_1_.refs_0_, f32[2,2,128,128]{3,2,1,0:T(8,128)S(1)} %get-tuple-element.19.refs_0_.refs_1_, f32[2,2,128,128]{3,2,1,0:T(8,128)S(1)} %collective-permute-done.9.refs_2_, ...), custom_call_target="tpu_custom_call" | custom-call | tf_op jit(solution)/shard_map/product/pallas_call | solution.py:268
  31.3 3.9 %collective-permute-done.8.refs_0_ = f32[2,2,160,128]{3,2,1,0:T(8,128)S(1)} collective-permute-done((f32[2,2,160,128]{3,2,1,0:T(8,128)S(1)}, f32[2,2,160,128]{3,2,1,0:T(8,128)S(1)}, u32[]{:S(2)}, u32[]{:S(2)}) %collective-permute-start.8) | collective-permute-done | bytes 327712 | tf_op jit(solution)/shard_map/ppermute | solution.py:281
  35.2 0.0 collective-permute-start.16
  35.2 0.5 %collective-permute-start.17 = (f32[2,2,128,128]{3,2,1,0:T(8,128)S(1)}, f32[2,2,128,128]{3,2,1,0:T(8,128)S(1)}, u32[]{:S(2)}, u32[]{:S(2)}) collective-permute-start(f32[2,2,128,128]{3,2,1,0:T(8,128)S(1)} %order.6.refs_1_), channel_id=1, source_target_pairs={{0,1},{1,0},{2,3},{3,2},{4,5},{5,4},{6,7},{7,6},{8,9},{9,8},{10,11... | collective-permute-start | bytes 786440 | tf_op jit(solution)/shard_map/ppermute | solution.py:281
  35.7 0.0 collective-permute-done.12.refs_2_.refs_4_
  35.7 0.0 collective-permute-start.15
  35.7 0.0 collective-permute-done.13.refs_3_
  35.7 1.3 %product.5.refs_1_.refs_5_ = f32[2,32,32,128]{3,2,1,0:T(8,128)S(1)} custom-call(f32[2,2,160,128]{3,2,1,0:T(8,128)S(1)} %order.5.refs_0_, f32[2,2,128,128]{3,2,1,0:T(8,128)S(1)} %order.6.refs_1_, f32[2,2,128,128]{3,2,1,0:T(8,128)S(1)} %collective-permute-done.12.refs_2_.refs_4_, f32[2,2,96,128]{3,2,1,0:T(8,128)S(1)} %collective-permute-done.13.refs_3_, ...), custom_call_target="tpu_custom_call" | custom-call | tf_op jit(solution)/shard_map/product/pallas_call | solution.py:268
  37.0 1.0 %collective-permute-done.7.refs_0_ = f32[2,2,96,128]{3,2,1,0:T(8,128)S(1)} collective-permute-done((f32[2,2,96,128]{3,2,1,0:T(8,128)S(1)}, f32[2,2,96,128]{3,2,1,0:T(8,128)S(1)}, u32[]{:S(2)}, u32[]{:S(2)}) %collective-permute-start.7) | collective-permute-done | bytes 196640 | tf_op jit(solution)/shard_map/ppermute | solution.py:281
  38.0 0.0 collective-permute-start.14
  38.0 0.0 collective-permute-done.17.refs_1_
  38.0 0.0 collective-permute-done.16.refs_0_
  38.0 1.3 %product.6.refs_2_ = f32[2,32,32,128]{3,2,1,0:T(8,128)S(1)} custom-call(f32[2,2,160,128]{3,2,1,0:T(8,128)S(1)} %collective-permute-done.16.refs_0_, f32[2,2,128,128]{3,2,1,0:T(8,128)S(1)} %collective-permute-done.17.refs_1_, f32[2,2,128,128]{3,2,1,0:T(8,128)S(1)} %collective-permute-done.15.refs_2_.refs_6_.refs_1_, f32[2,2,96,128]{3,2,1,0:T(8,128)S(1)} %order.7.refs_3_, ...), custom_call_target="tpu_custom_call" | custom-call | tf_op jit(solution)/shard_map/product/pallas_call | solution.py:268
  39.4 0.1 collective-permute-done.14.refs_0_
  39.5 1.3 %product.7 = f32[2,32,32,128]{3,2,1,0:T(8,128)} custom-call(f32[2,2,96,128]{3,2,1,0:T(8,128)S(1)} %collective-permute-done.14.refs_0_, f32[2,2,128,128]{3,2,1,0:T(8,128)S(1)} %collective-permute-done.15.refs_2_.refs_6_.refs_1_, f32[2,32,32,128]{3,2,1,0:T(8,128)S(1)} %product.6.refs_2_), custom_call_target="tpu_custom_call" | custom-call | tf_op jit(solution)/shard_map/product/pallas_call | solution.py:268
  (11 shorter events, 0.1 us)
Async XLA Ops:
  0.0 16.9 %collective-permute-start = (f32[8,32,256]{2,1,0:T(8,128)}, f32[8,32,256]{2,1,0:T(8,128)S(1)}, u32[]{:S(2)}, u32[]{:S(2)}) collective-permute-start(f32[8,32,256]{2,1,0:T(8,128)} %refs_0_.1), channel_id=1, source_target_pairs={{0,8},{4,12},{8,0},{12,4},{1,9},{5,13},{9,1},{13,5},{2,10},{6,14},... | collective-permute-start | bytes 786440 | tf_op jit(solution)/shard_map/ppermute | solution.py:281
  4.0 14.9 %collective-permute-start.1 = (f32[8,32,256]{2,1,0:T(8,128)}, f32[8,32,256]{2,1,0:T(8,128)S(1)}, u32[]{:S(2)}, u32[]{:S(2)}) collective-permute-start(f32[8,32,256]{2,1,0:T(8,128)} %refs_0_.1), channel_id=1, source_target_pairs={{0,4},{4,0},{8,12},{12,8},{1,5},{5,1},{9,13},{13,9},{2,6},{6,2},{1... | collective-permute-start | bytes 786440 | tf_op jit(solution)/shard_map/ppermute | solution.py:281
  6.7 7.6 %collective-permute-start.2 = (f32[4,32,512]{2,1,0:T(8,128)S(1)}, f32[4,32,512]{2,1,0:T(8,128)S(1)}, u32[]{:S(2)}, u32[]{:S(2)}) collective-permute-start(f32[4,32,512]{2,1,0:T(8,128)S(1)} %get-tuple-element.29), channel_id=1, source_target_pairs={{0,16},{16,0},{1,17},{17,1},{2,18},{18,2},{3,19},{19,3},{4,20},{20... | collective-permute-start | bytes 786440 | tf_op jit(solution)/shard_map/ppermute | solution.py:281
  8.3 0.9 %copy-start.1 = (f32[2,4,64,128]{3,2,1,0:T(8,128)S(1)}, f32[2,4,64,128]{3,2,1,0:T(8,128)}, u32[]{:S(2)}) copy-start(f32[2,4,64,128]{3,2,1,0:T(8,128)} %constant.32.clone.angles_ref) | copy-start | bytes 786436
  15.2 8.6 %collective-permute-start.5 = (f32[2,2,128,128]{3,2,1,0:T(8,128)S(1)}, f32[2,2,128,128]{3,2,1,0:T(8,128)S(1)}, u32[]{:S(2)}, u32[]{:S(2)}) collective-permute-start(f32[2,2,128,128]{3,2,1,0:T(8,128)S(1)} %get-tuple-element.19.refs_0_.refs_1_), channel_id=1, source_target_pairs={{0,1},{1,0},{2,3},{3,2},{4,5},{5,4},{6,7},{7,6},{8,9},{9,8},{10,11... | collective-permute-start | bytes 786440 | tf_op jit(solution)/shard_map/ppermute | solution.py:281
  15.3 3.6 %copy-start = (f32[8,32,256]{2,1,0:T(8,128)S(1)}, f32[8,32,256]{2,1,0:T(8,128)}, u32[]{:S(2)}) copy-start(f32[8,32,256]{2,1,0:T(8,128)} %refs_0_.1) | copy-start | bytes 786436
  15.3 8.7 %collective-permute-start.6 = (f32[2,2,128,128]{3,2,1,0:T(8,128)S(1)}, f32[2,2,128,128]{3,2,1,0:T(8,128)S(1)}, u32[]{:S(2)}, u32[]{:S(2)}) collective-permute-start(f32[2,2,128,128]{3,2,1,0:T(8,128)S(1)} %get-tuple-element.24), channel_id=1, source_target_pairs={{0,2},{1,3},{2,0},{3,1},{4,6},{5,7},{6,4},{7,5},{8,10},{9,11},{10,... | collective-permute-start | bytes 786440 | tf_op jit(solution)/shard_map/ppermute | solution.py:281
  16.9 6.9 %collective-permute-start.4 = (f32[5,32,256]{2,1,0:T(8,128)S(1)}, f32[5,32,256]{2,1,0:T(8,128)S(1)}, u32[]{:S(2)}, u32[]{:S(2)}) collective-permute-start(f32[5,32,256]{2,1,0:T(8,128)S(1)} %pick.2.refs_5_), channel_id=1, source_target_pairs={{0,4},{4,0},{8,12},{12,8},{1,5},{5,1},{9,13},{13,9},{2,6},{6,2},{1... | collective-permute-start | bytes 491528 | tf_op jit(solution)/shard_map/ppermute | solution.py:281
  17.4 8.6 %collective-permute-start.9 = (f32[2,2,128,128]{3,2,1,0:T(8,128)S(1)}, f32[2,2,128,128]{3,2,1,0:T(8,128)S(1)}, u32[]{:S(2)}, u32[]{:S(2)}) collective-permute-start(f32[2,2,128,128]{3,2,1,0:T(8,128)S(1)} %get-tuple-element.19.refs_0_.refs_1_), channel_id=1, source_target_pairs={{0,16},{16,0},{1,17},{17,1},{2,18},{18,2},{3,19},{19,3},{4,20},{20... | collective-permute-start | bytes 786440 | tf_op jit(solution)/shard_map/ppermute | solution.py:281
  20.4 6.3 %collective-permute-start.3 = (f32[3,32,256]{2,1,0:T(8,128)S(1)}, f32[3,32,256]{2,1,0:T(8,128)S(1)}, u32[]{:S(2)}, u32[]{:S(2)}) collective-permute-start(f32[3,32,256]{2,1,0:T(8,128)S(1)} %pick.3), channel_id=1, source_target_pairs={{0,4},{4,0},{8,12},{12,8},{1,5},{5,1},{9,13},{13,9},{2,6},{6,2},{1... | collective-permute-start | bytes 294920 | tf_op jit(solution)/shard_map/ppermute | solution.py:281
  24.5 10.7 %collective-permute-start.8 = (f32[2,2,160,128]{3,2,1,0:T(8,128)S(1)}, f32[2,2,160,128]{3,2,1,0:T(8,128)S(1)}, u32[]{:S(2)}, u32[]{:S(2)}) collective-permute-start(f32[2,2,160,128]{3,2,1,0:T(8,128)S(1)} %get-tuple-element.27), channel_id=1, source_target_pairs={{0,2},{1,3},{2,0},{3,1},{4,6},{5,7},{6,4},{7,5},{8,10},{9,11},{10,... | collective-permute-start | bytes 983048 | tf_op jit(solution)/shard_map/ppermute | solution.py:281
  26.1 3.1 %collective-permute-start.10 = (f32[2,2,160,128]{3,2,1,0:T(8,128)S(1)}, f32[2,2,160,128]{3,2,1,0:T(8,128)S(1)}, u32[]{:S(2)}, u32[]{:S(2)}) collective-permute-start(f32[2,2,160,128]{3,2,1,0:T(8,128)S(1)} %get-tuple-element.25.refs_5_.refs_1_.refs_0_), channel_id=1, source_target_pairs={{0,1},{1,0},{2,3},{3,2},{4,5},{5,4},{6,7},{7,6},{8,9},{9,8},{10,11... | collective-permute-start | bytes 983048 | tf_op jit(solution)/shard_map/ppermute | solution.py:281
  26.1 2.5 %collective-permute-start.11 = (f32[2,2,128,128]{3,2,1,0:T(8,128)S(1)}, f32[2,2,128,128]{3,2,1,0:T(8,128)S(1)}, u32[]{:S(2)}, u32[]{:S(2)}) collective-permute-start(f32[2,2,128,128]{3,2,1,0:T(8,128)S(1)} %order.4), channel_id=1, source_target_pairs={{0,1},{1,0},{2,3},{3,2},{4,5},{5,4},{6,7},{7,6},{8,9},{9,8},{10,11... | collective-permute-start | bytes 786440 | tf_op jit(solution)/shard_map/ppermute | solution.py:281
  27.1 8.6 %collective-permute-start.12 = (f32[2,2,128,128]{3,2,1,0:T(8,128)S(1)}, f32[2,2,128,128]{3,2,1,0:T(8,128)S(1)}, u32[]{:S(2)}, u32[]{:S(2)}) collective-permute-start(f32[2,2,128,128]{3,2,1,0:T(8,128)S(1)} %order.6.refs_1_), channel_id=1, source_target_pairs={{0,16},{16,0},{1,17},{17,1},{2,18},{18,2},{3,19},{19,3},{4,20},{20... | collective-permute-start | bytes 786440 | tf_op jit(solution)/shard_map/ppermute | solution.py:281
  28.6 7.1 %collective-permute-start.13 = (f32[2,2,96,128]{3,2,1,0:T(8,128)S(1)}, f32[2,2,96,128]{3,2,1,0:T(8,128)S(1)}, u32[]{:S(2)}, u32[]{:S(2)}) collective-permute-start(f32[2,2,96,128]{3,2,1,0:T(8,128)S(1)} %get-tuple-element.28.refs_6_.refs_1_), channel_id=1, source_target_pairs={{0,1},{1,0},{2,3},{3,2},{4,5},{5,4},{6,7},{7,6},{8,9},{9,8},{10,11... | collective-permute-start | bytes 589832 | tf_op jit(solution)/shard_map/ppermute | solution.py:281
  28.6 9.4 %collective-permute-start.7 = (f32[2,2,96,128]{3,2,1,0:T(8,128)S(1)}, f32[2,2,96,128]{3,2,1,0:T(8,128)S(1)}, u32[]{:S(2)}, u32[]{:S(2)}) collective-permute-start(f32[2,2,96,128]{3,2,1,0:T(8,128)S(1)} %get-tuple-element.26), channel_id=1, source_target_pairs={{0,2},{1,3},{2,0},{3,1},{4,6},{5,7},{6,4},{7,5},{8,10},{9,11},{10,... | collective-permute-start | bytes 589832 | tf_op jit(solution)/shard_map/ppermute | solution.py:281
  35.2 2.9 %collective-permute-start.16 = (f32[2,2,160,128]{3,2,1,0:T(8,128)S(1)}, f32[2,2,160,128]{3,2,1,0:T(8,128)S(1)}, u32[]{:S(2)}, u32[]{:S(2)}) collective-permute-start(f32[2,2,160,128]{3,2,1,0:T(8,128)S(1)} %order.5.refs_0_), channel_id=1, source_target_pairs={{0,1},{1,0},{2,3},{3,2},{4,5},{5,4},{6,7},{7,6},{8,9},{9,8},{10,11... | collective-permute-start | bytes 983048 | tf_op jit(solution)/shard_map/ppermute | solution.py:281
  35.2 2.9 %collective-permute-start.17 = (f32[2,2,128,128]{3,2,1,0:T(8,128)S(1)}, f32[2,2,128,128]{3,2,1,0:T(8,128)S(1)}, u32[]{:S(2)}, u32[]{:S(2)}) collective-permute-start(f32[2,2,128,128]{3,2,1,0:T(8,128)S(1)} %order.6.refs_1_), channel_id=1, source_target_pairs={{0,1},{1,0},{2,3},{3,2},{4,5},{5,4},{6,7},{7,6},{8,9},{9,8},{10,11... | collective-permute-start | bytes 786440 | tf_op jit(solution)/shard_map/ppermute | solution.py:281
  35.7 2.3 %collective-permute-start.15 = (f32[2,2,128,128]{3,2,1,0:T(8,128)S(1)}, f32[2,2,128,128]{3,2,1,0:T(8,128)S(1)}, u32[]{:S(2)}, u32[]{:S(2)}) collective-permute-start(f32[2,2,128,128]{3,2,1,0:T(8,128)S(1)} %collective-permute-done.12.refs_2_.refs_4_), channel_id=1, source_target_pairs={{0,1},{1,0},{2,3},{3,2},{4,5},{5,4},{6,7},{7,6},{8,9},{9,8},{10,11... | collective-permute-start | bytes 786440 | tf_op jit(solution)/shard_map/ppermute | solution.py:281
  38.0 1.4 %collective-permute-start.14 = (f32[2,2,96,128]{3,2,1,0:T(8,128)S(1)}, f32[2,2,96,128]{3,2,1,0:T(8,128)S(1)}, u32[]{:S(2)}, u32[]{:S(2)}) collective-permute-start(f32[2,2,96,128]{3,2,1,0:T(8,128)S(1)} %order.7.refs_3_), channel_id=1, source_target_pairs={{0,1},{1,0},{2,3},{3,2},{4,5},{5,4},{6,7},{7,6},{8,9},{9,8},{10,11... | collective-permute-start | bytes 589832 | tf_op jit(solution)/shard_map/ppermute | solution.py:281

commit v6 on v5

--- a/solution.py
+++ b/solution.py
@@ -74,6 +74,23 @@
         cost_estimate=cost(flops),
         name="pick",
     )(array, *after)
+
+
+def far_half(block):
+    out = jax.ShapeDtypeStruct((1,) + block.shape[1:], block.dtype)
+
+    def kernel(block_ref, out_ref):
+        out_ref[0] = block_ref[1]
+
+    return pl.pallas_call(
+        kernel,
+        out_shape=out,
+        in_specs=[VMEM],
+        out_specs=VMEM,
+        compiler_params=room(block, out),
+        cost_estimate=cost(),
+        name="far_half",
+    )(block)
 
 
 def tables_kernel(angles_ref, high_ref, low_ref):
@@ -210,17 +227,19 @@
         return pltpu.make_async_copy(out_ref.at[c, span], send_ref.at[c, span], sems.at[g, c])
 
     for number, (half, shot, shot_row, receiver, receiver_row, points) in enumerate(terms):
+        shot_half = min(half, in_refs[shot].shape[0] - 1)
+        receiver_half = min(half, in_refs[receiver].shape[0] - 1)
         before = out_ref if number else total_refs[0] if carried else None
 
         def shot_group(g, _):
             sums = [jnp.zeros((receivers, bins), jnp.float32)] * (3 * GROUP)
             for x in range(points):
                 span = slice(receiver_row + x * receivers, receiver_row + (x + 1) * receivers)
-                r_re, r_im = in_refs[receiver][half, 0, span, :], in_refs[receiver][half, 1, span, :]
+                r_re, r_im = in_refs[receiver][receiver_half, 0, span, :], in_refs[receiver][receiver_half, 1, span, :]
                 r_sum = r_re + r_im
                 for i in range(GROUP):
                     line = pl.ds(shot_row + x * shots + g * GROUP + i, 1)
-                    s_re, s_im = in_refs[shot][half, 0, line, :], in_refs[shot][half, 1, line, :]
+                    s_re, s_im = in_refs[shot][shot_half, 0, line, :], in_refs[shot][shot_half, 1, line, :]
                     s_sum = s_re + s_im
                     sums[3 * i] += s_re * r_re
                     sums[3 * i + 1] += s_im * r_im
@@ -374,19 +393,19 @@
             ]
 
         pairs = chips[1:]
-        first = [(0, 0, 0), (0, 0, 1), (1, 0, 0)]
-        total = product(sum([terms(*x) for x in first], []), shots, receivers)
+        s_far[1] = core(s_near[1])
+        total = product(sum([terms(*x) for x in [(0, 0, 0), (0, 0, 1), (1, 0, 0), (1, 0, 1)]], []), shots, receivers)
         for q in pairs:
             s_near[2 * q] = late(s_near[2 * q], total)
-        s_far[1] = core(s_near[1])
-        total = product(sum([terms(0, q, 0) for q in pairs] + [terms(1, 0, 1)], []), shots, receivers, total)
+        total = product(sum([terms(*x) for x in [(0, q, 0) for q in pairs]], []), shots, receivers, total)
+        for q in pairs:
+            s_far += [core(far_half(s_near[2 * q])), None]
+            r_far.append([core(far_half(block)) for block in r_near[q]])
+        total = product(sum([terms(0, q, 1) for q in pairs], []), shots, receivers, total)
         for q in pairs:
             s_near[2 * q + 1] = late(s_near[2 * q + 1], total)
-            s_far += [core(s_near[2 * q]), core(s_near[2 * q + 1])]
-            r_far.append([core(block) for block in r_near[q]])
-        second = [(0, q, 1) for q in pairs] + [(1, q, 0) for q in pairs]
-        after = [r_far[q][-1] for q in pairs]
-        total = product(sum([terms(*x) for x in second], []), shots, receivers, total, after)
+            s_far[2 * q + 1] = core(far_half(s_near[2 * q + 1]))
+        total = product(sum([terms(1, q, 0) for q in pairs], []), shots, receivers, total)
         total = product(sum([terms(1, q, 1) for q in pairs], []), shots, receivers, total, last=True)
         return total.transpose(3, 0, 1, 2)
 

time: 40.9 us -> 40.8 us (level)
  waiting for transfers between devices: 10.1 us -> 9.68 us
    pallas_call x4 -> x5, Pallas kernels: 6.1 us -> 6.09 us  [product(): pl.pallas_call(lambda *refs: product_kernel(described, len(blocks), len(c...]
  transfers between devices with their start and end apart: 18 -> 18, of which waited for: 6 -> 8; matrix products, arithmetic and copies ran while one was open for 5% -> 5% of each run, Pallas kernels for 23% -> 23%
where the time goes in v6:
time: 40.8 us; the launch traced here: 40.7 us
  starting transfers between devices  17.5 us (43%)
  Pallas kernels  10.5 us (26%)
  waiting for transfers between devices  9.68 us (24%)
  local copies, waits for them, and re-layouts  2.04 us (5%)
  other arithmetic  0.81 us (2%)
    ppermute x18, starting transfers between devices, exchange(): return lax.ppermute(block, axis, [(i, i ^ step) for i in range(size)])  17.5 us
    ppermute x18, waiting for transfers between devices, exchange(): return lax.ppermute(block, axis, [(i, i ^ step) for i in range(size)])  9.68 us
    pallas_call x5, Pallas kernels, product(): pl.pallas_call(lambda *refs: product_kernel(described, len(blocks), len(c...  6.09 us
    pallas_call x4, Pallas kernels, transform(): pl.pallas_call(lambda *refs: transform_kernel(steps, len(taper), len(adde...  3.19 us
    pallas_call x1, Pallas kernels, tables(): pl.pallas_call(tables_kernel, out_shape=out, in_specs=[VMEM], out_specs=[...  1.13 us
    dynamic_slice x1, local copies, waits for them, and re-layouts, own(): return lax.dynamic_slice_in_dim(array, (me ^ j) * part, part)  1.07 us
    unnamed x5, local copies, waits for them, and re-layouts  0.97 us
  transfers between devices with their start and end apart: 18, of which 8 were waited for; matrix products, arithmetic and copies ran while one was open for 5% of the time, Pallas kernels for 23%

profile of v6, /device:TPU:0, one launch (start us, length us, event | category | flops | bytes accessed | tf_op | source)
XLA Modules:
  0.0 40.7 jit_solution(13808464354540656171)
XLA Ops:
  0.0 4.0 %collective-permute-start = (f32[8,32,256]{2,1,0:T(8,128)}, f32[8,32,256]{2,1,0:T(8,128)S(1)}, u32[]{:S(2)}, u32[]{:S(2)}) collective-permute-start(f32[8,32,256]{2,1,0:T(8,128)} %refs_0_.1), channel_id=1, source_target_pairs={{0,8},{4,12},{8,0},{12,4},{1,9},{5,13},{9,1},{13,5},{2,10},{6,14},... | collective-permute-start | bytes 786440 | tf_op jit(solution)/shard_map/ppermute | solution.py:300
  4.0 1.6 %collective-permute-start.1 = (f32[8,32,256]{2,1,0:T(8,128)}, f32[8,32,256]{2,1,0:T(8,128)S(1)}, u32[]{:S(2)}, u32[]{:S(2)}) collective-permute-start(f32[8,32,256]{2,1,0:T(8,128)} %refs_0_.1), channel_id=1, source_target_pairs={{0,4},{4,0},{8,12},{12,8},{1,5},{5,1},{9,13},{13,9},{2,6},{6,2},{1... | collective-permute-start | bytes 786440 | tf_op jit(solution)/shard_map/ppermute | solution.py:300
  5.6 1.1 %constant_dynamic-slice_fusion = (f32[4,32,512]{2,1,0:T(8,128)S(1)}, f32[4,32,512]{2,1,0:T(8,128)S(1)}) fusion(f32[8,32,512]{2,1,0:T(8,128)} %param.7, s32[]{:T(128)S(6)} %select_n.7, s32[]{:T(128)S(6)} %select_n.6), kind=kLoop, calls=%fused_computation.2 | loop fusion | bytes 1048584 | tf_op jit(solution)/shard_map/dynamic_slice | solution.py:322
  6.7 1.6 %collective-permute-start.2 = (f32[4,32,512]{2,1,0:T(8,128)S(1)}, f32[4,32,512]{2,1,0:T(8,128)S(1)}, u32[]{:S(2)}, u32[]{:S(2)}) collective-permute-start(f32[4,32,512]{2,1,0:T(8,128)S(1)} %get-tuple-element.29), channel_id=1, source_target_pairs={{0,16},{16,0},{1,17},{17,1},{2,18},{18,2},{3,19},{19,3},{4,20},{20... | collective-permute-start | bytes 786440 | tf_op jit(solution)/shard_map/ppermute | solution.py:300
  8.3 0.9 %copy-done.1 = f32[2,4,64,128]{3,2,1,0:T(8,128)S(1)} copy-done((f32[2,4,64,128]{3,2,1,0:T(8,128)S(1)}, f32[2,4,64,128]{3,2,1,0:T(8,128)}, u32[]{:S(2)}) %copy-start.1) | copy-done | bytes 262168
  9.2 1.1 %tables.1 = (bf16[4,1024,256]{2,1,0:T(8,128)(2,1)S(1)}, bf16[4,1024,256]{2,1,0:T(8,128)(2,1)S(1)}) custom-call(f32[2,4,64,128]{3,2,1,0:T(8,128)S(1)} %copy-done.1), custom_call_target="tpu_custom_call" | custom-call | tf_op jit(solution)/shard_map/tables/pallas_call | solution.py:128
  10.3 0.8 %clamp_multiply_fusion.refs_4_ = f32[8,32,128]{2,1,0:T(8,128)S(1)} fusion(s32[8]{0:T(128)} %param.10, s32[8]{0:T(128)} %param.9, s32[32]{0:T(128)S(1)} %iota_add_fusion, f32[8]{0:T(128)} %param.8), kind=kLoop, calls=%fused_computation | loop fusion | flops 393216 | bytes 131296 | tf_op jit(solution)/shard_map/mul | solution.py:144
  11.2 3.1 %collective-permute-done.2.refs_1_ = f32[4,32,512]{2,1,0:T(8,128)S(1)} collective-permute-done((f32[4,32,512]{2,1,0:T(8,128)S(1)}, f32[4,32,512]{2,1,0:T(8,128)S(1)}, u32[]{:S(2)}, u32[]{:S(2)}) %collective-permute-start.2) | collective-permute-done | bytes 262176 | tf_op jit(solution)/shard_map/ppermute | solution.py:300
  14.2 1.0 %transform.4 = (f32[2,2,128,128]{3,2,1,0:T(8,128)S(1)}, f32[2,2,128,128]{3,2,1,0:T(8,128)S(1)}) custom-call(f32[4,32,512]{2,1,0:T(8,128)S(1)} %get-tuple-element.30.refs_0_, f32[4,32,512]{2,1,0:T(8,128)S(1)} %collective-permute-done.2.refs_1_, bf16[4,1024,256]{2,1,0:T(8,128)(2,1)S(1)} %get-tuple-element.17.refs_2_.refs_3_.refs_1_, ...), custom_call_target="tpu_custom_call" | custom-call | tf_op jit(solution)/shard_map/transform/pallas_call | solution.py:201
  15.2 0.1 collective-permute-start.5
  15.3 0.0 copy-start
  15.3 1.6 %collective-permute-start.6 = (f32[2,2,128,128]{3,2,1,0:T(8,128)S(1)}, f32[2,2,128,128]{3,2,1,0:T(8,128)S(1)}, u32[]{:S(2)}, u32[]{:S(2)}) collective-permute-start(f32[2,2,128,128]{3,2,1,0:T(8,128)S(1)} %get-tuple-element.24), channel_id=1, source_target_pairs={{0,2},{1,3},{2,0},{3,1},{4,6},{5,7},{6,4},{7,5},{8,10},{9,11},{10,... | collective-permute-start | bytes 786440 | tf_op jit(solution)/shard_map/ppermute | solution.py:300
  16.9 0.0 collective-permute-done.array_ref.refs_2_
  16.9 0.5 %collective-permute-start.4 = (f32[5,32,256]{2,1,0:T(8,128)S(1)}, f32[5,32,256]{2,1,0:T(8,128)S(1)}, u32[]{:S(2)}, u32[]{:S(2)}) collective-permute-start(f32[5,32,256]{2,1,0:T(8,128)S(1)} %pick.2.refs_5_), channel_id=1, source_target_pairs={{0,4},{4,0},{8,12},{12,8},{1,5},{5,1},{9,13},{13,9},{2,6},{6,2},{1... | collective-permute-start | bytes 491528 | tf_op jit(solution)/shard_map/ppermute | solution.py:300
  17.4 1.5 %collective-permute-start.9 = (f32[2,2,128,128]{3,2,1,0:T(8,128)S(1)}, f32[2,2,128,128]{3,2,1,0:T(8,128)S(1)}, u32[]{:S(2)}, u32[]{:S(2)}) collective-permute-start(f32[2,2,128,128]{3,2,1,0:T(8,128)S(1)} %get-tuple-element.19.refs_0_.refs_1_), channel_id=1, source_target_pairs={{0,16},{16,0},{1,17},{17,1},{2,18},{18,2},{3,19},{19,3},{4,20},{20... | collective-permute-start | bytes 786440 | tf_op jit(solution)/shard_map/ppermute | solution.py:300
  18.9 0.0 collective-permute-done.1.refs_1_
  18.9 1.4 %transform.5 = (f32[2,2,160,128]{3,2,1,0:T(8,128)S(1)}, f32[2,2,96,128]{3,2,1,0:T(8,128)S(1)}, f32[2,2,160,128]{3,2,1,0:T(8,128)S(1)}, f32[2,2,96,128]{3,2,1,0:T(8,128)S(1)}) custom-call(f32[8,32,256]{2,1,0:T(8,128)S(1)} %copy-done, f32[8,32,256]{2,1,0:T(8,128)S(1)} %collective-permute-done.1.refs_1_, ...), custom_call_target="tpu_custom_call" | custom-call | flops 1000000000 | tf_op jit(solution)/shard_map/transform/pallas_call | solution.py:201
  20.4 1.6 %collective-permute-start.3 = (f32[3,32,256]{2,1,0:T(8,128)S(1)}, f32[3,32,256]{2,1,0:T(8,128)S(1)}, u32[]{:S(2)}, u32[]{:S(2)}) collective-permute-start(f32[3,32,256]{2,1,0:T(8,128)S(1)} %pick.3), channel_id=1, source_target_pairs={{0,4},{4,0},{8,12},{12,8},{1,5},{5,1},{9,13},{13,9},{2,6},{6,2},{1... | collective-permute-start | bytes 294920 | tf_op jit(solution)/shard_map/ppermute | solution.py:300
  22.0 1.8 %collective-permute-done.4.refs_0_ = f32[5,32,256]{2,1,0:T(8,128)S(1)} collective-permute-done((f32[5,32,256]{2,1,0:T(8,128)S(1)}, f32[5,32,256]{2,1,0:T(8,128)S(1)}, u32[]{:S(2)}, u32[]{:S(2)}) %collective-permute-start.4) | collective-permute-done | bytes 163872 | tf_op jit(solution)/shard_map/ppermute | solution.py:300
  23.8 0.0 collective-permute-done.5.refs_5_.refs_4_
  23.8 0.2 collective-permute-done.6.refs_6_.refs_0_
  24.0 0.4 %transform.6 = (f32[2,2,160,128]{3,2,1,0:T(8,128)S(1)}, f32[2,2,160,128]{3,2,1,0:T(8,128)S(1)}) custom-call(f32[5,32,256]{2,1,0:T(8,128)S(1)} %collective-permute-done.4.refs_0_, bf16[4,1024,256]{2,1,0:T(8,128)(2,1)S(1)} %get-tuple-element.17.refs_2_.refs_3_.refs_1_, bf16[4,1024,256]{2,1,0:T(8,128)(2,1)S(1)} %get-tuple-element.18.refs_3_.refs_4_.refs_2_, ...), custom_call_target="tpu_custom_call" | custom-call | flops 2500000000 | tf_op jit(solution)/shard_map/transform/pallas_call | solution.py:201
  24.5 1.6 %collective-permute-start.8 = (f32[2,2,160,128]{3,2,1,0:T(8,128)S(1)}, f32[2,2,160,128]{3,2,1,0:T(8,128)S(1)}, u32[]{:S(2)}, u32[]{:S(2)}) collective-permute-start(f32[2,2,160,128]{3,2,1,0:T(8,128)S(1)} %get-tuple-element.27), channel_id=1, source_target_pairs={{0,2},{1,3},{2,0},{3,1},{4,6},{5,7},{6,4},{7,5},{8,10},{9,11},{10,... | collective-permute-start | bytes 983048 | tf_op jit(solution)/shard_map/ppermute | solution.py:300
  26.1 0.0 collective-permute-start.10
  26.1 0.0 collective-permute-done.9.refs_2_
  26.1 0.6 %collective-permute-start.11 = (f32[2,2,128,128]{3,2,1,0:T(8,128)S(1)}, f32[2,2,128,128]{3,2,1,0:T(8,128)S(1)}, u32[]{:S(2)}, u32[]{:S(2)}) collective-permute-start(f32[2,2,128,128]{3,2,1,0:T(8,128)S(1)} %order.4), channel_id=1, source_target_pairs={{0,1},{1,0},{2,3},{3,2},{4,5},{5,4},{6,7},{7,6},{8,9},{9,8},{10,11... | collective-permute-start | bytes 786440 | tf_op jit(solution)/shard_map/ppermute | solution.py:300
  26.7 0.0 collective-permute-done.3.refs_0_
  26.7 0.4 transform.7
  27.1 1.6 %collective-permute-start.15 = (f32[2,2,128,128]{3,2,1,0:T(8,128)S(1)}, f32[2,2,128,128]{3,2,1,0:T(8,128)S(1)}, u32[]{:S(2)}, u32[]{:S(2)}) collective-permute-start(f32[2,2,128,128]{3,2,1,0:T(8,128)S(1)} %order.6.block_ref.refs_1_), channel_id=1, source_target_pairs={{0,16},{16,0},{1,17},{17,1},{2,18},{18,2},{3,19},{19,3},{4,20},{20... | collective-permute-start | bytes 786440 | tf_op jit(solution)/shard_map/ppermute | solution.py:300
  28.6 1.4 %collective-permute-done.12.refs_7_ = f32[2,2,96,128]{3,2,1,0:T(8,128)S(1)} collective-permute-done((f32[2,2,96,128]{3,2,1,0:T(8,128)S(1)}, f32[2,2,96,128]{3,2,1,0:T(8,128)S(1)}, u32[]{:S(2)}, u32[]{:S(2)}) %collective-permute-start.12) | collective-permute-done | bytes 196640 | tf_op jit(solution)/shard_map/ppermute | solution.py:300
  30.1 0.5 %collective-permute-start.7 = (f32[2,2,96,128]{3,2,1,0:T(8,128)S(1)}, f32[2,2,96,128]{3,2,1,0:T(8,128)S(1)}, u32[]{:S(2)}, u32[]{:S(2)}) collective-permute-start(f32[2,2,96,128]{3,2,1,0:T(8,128)S(1)} %get-tuple-element.26), channel_id=1, source_target_pairs={{0,2},{1,3},{2,0},{3,1},{4,6},{5,7},{6,4},{7,5},{8,10},{9,11},{10,... | collective-permute-start | bytes 589832 | tf_op jit(solution)/shard_map/ppermute | solution.py:300
  30.6 0.0 collective-permute-done.11.refs_5_
  30.6 0.0 collective-permute-done.10.refs_3_
  30.6 2.6 %product.5.refs_1_.refs_3_ = f32[2,32,32,128]{3,2,1,0:T(8,128)S(1)} custom-call(f32[2,2,160,128]{3,2,1,0:T(8,128)S(1)} %get-tuple-element.25.refs_5_.refs_1_.refs_0_, f32[2,2,128,128]{3,2,1,0:T(8,128)S(1)} %get-tuple-element.19.refs_0_.refs_1_, f32[2,2,128,128]{3,2,1,0:T(8,128)S(1)} %collective-permute-done.9.refs_2_, ...), custom_call_target="tpu_custom_call" | custom-call | tf_op jit(solution)/shard_map/product/pallas_call | solution.py:287
  33.2 1.5 %collective-permute-done.8.refs_0_ = f32[2,2,160,128]{3,2,1,0:T(8,128)S(1)} collective-permute-done((f32[2,2,160,128]{3,2,1,0:T(8,128)S(1)}, f32[2,2,160,128]{3,2,1,0:T(8,128)S(1)}, u32[]{:S(2)}, u32[]{:S(2)}) %collective-permute-start.8) | collective-permute-done | bytes 327712 | tf_op jit(solution)/shard_map/ppermute | solution.py:300
  34.7 0.1 collective-permute-start.13
  34.8 0.6 %collective-permute-start.14 = (f32[1,2,128,128]{3,2,1,0:T(8,128)S(1)}, f32[1,2,128,128]{3,2,1,0:T(8,128)S(1)}, u32[]{:S(2)}, u32[]{:S(2)}) collective-permute-start(f32[1,2,128,128]{3,2,1,0:T(8,128)S(1)} %far_half.5), channel_id=1, source_target_pairs={{0,1},{1,0},{2,3},{3,2},{4,5},{5,4},{6,7},{7,6},{8,9},{9,8},{10,11... | collective-permute-start | bytes 393224 | tf_op jit(solution)/shard_map/ppermute | solution.py:300
  35.4 0.1 collective-permute-start.16
  35.5 0.9 %product.6.refs_3_ = f32[2,32,32,128]{3,2,1,0:T(8,128)S(1)} custom-call(f32[2,2,160,128]{3,2,1,0:T(8,128)S(1)} %order.5.block_ref.refs_0_, f32[2,2,128,128]{3,2,1,0:T(8,128)S(1)} %order.6.block_ref.refs_1_, f32[2,2,128,128]{3,2,1,0:T(8,128)S(1)} %collective-permute-done.15.block_ref.refs_2_.refs_1_, f32[2,32,32,128]{3,2,1,0:T(8,128)S(1)} %product.5.refs_1_.refs_3_), custom_call_target="tpu_custom_call" | custom-call | tf_op jit(solution)/shard_map/product/pallas_call | solution.py:287
  36.4 0.0 collective-permute-done.14.refs_1_
  36.4 0.4 %collective-permute-done.16.refs_2_.refs_1_ = f32[1,2,128,128]{3,2,1,0:T(8,128)S(1)} collective-permute-done((f32[1,2,128,128]{3,2,1,0:T(8,128)S(1)}, f32[1,2,128,128]{3,2,1,0:T(8,128)S(1)}, u32[]{:S(2)}, u32[]{:S(2)}) %collective-permute-start.16) | collective-permute-done | bytes 131104 | tf_op jit(solution)/shard_map/ppermute | solution.py:300
  36.8 0.0 collective-permute-done.13.refs_0_
  36.8 0.9 %product.7.refs_1_.refs_2_ = f32[2,32,32,128]{3,2,1,0:T(8,128)S(1)} custom-call(f32[1,2,160,128]{3,2,1,0:T(8,128)S(1)} %collective-permute-done.13.refs_0_, f32[1,2,128,128]{3,2,1,0:T(8,128)S(1)} %collective-permute-done.14.refs_1_, f32[1,2,128,128]{3,2,1,0:T(8,128)S(1)} %collective-permute-done.16.refs_2_.refs_1_, f32[2,32,32,128]{3,2,1,0:T(8,128)S(1)} %product.6.refs_3_), custom_call_target="tpu_custom_call" | custom-call | tf_op jit(solution)/shard_map/product/pallas_call | solution.py:287
  37.7 0.3 collective-permute-done.7.refs_0_
  38.0 0.1 collective-permute-start.17
  38.1 0.5 %product.8.refs_2_ = f32[2,32,32,128]{3,2,1,0:T(8,128)S(1)} custom-call(f32[2,2,96,128]{3,2,1,0:T(8,128)S(1)} %order.7.block_ref.refs_0_, f32[2,2,128,128]{3,2,1,0:T(8,128)S(1)} %collective-permute-done.15.block_ref.refs_2_.refs_1_, f32[2,32,32,128]{3,2,1,0:T(8,128)S(1)} %product.7.refs_1_.refs_2_), custom_call_target="tpu_custom_call" | custom-call | tf_op jit(solution)/shard_map/product/pallas_call | solution.py:287
  38.6 0.8 %collective-permute-done.17.refs_0_ = f32[1,2,96,128]{3,2,1,0:T(8,128)S(1)} collective-permute-done((f32[1,2,96,128]{3,2,1,0:T(8,128)S(1)}, f32[1,2,96,128]{3,2,1,0:T(8,128)S(1)}, u32[]{:S(2)}, u32[]{:S(2)}) %collective-permute-start.17) | collective-permute-done | bytes 98336 | tf_op jit(solution)/shard_map/ppermute | solution.py:300
  39.4 1.3 %product.9 = f32[2,32,32,128]{3,2,1,0:T(8,128)} custom-call(f32[1,2,96,128]{3,2,1,0:T(8,128)S(1)} %collective-permute-done.17.refs_0_, f32[1,2,128,128]{3,2,1,0:T(8,128)S(1)} %collective-permute-done.16.refs_2_.refs_1_, f32[2,32,32,128]{3,2,1,0:T(8,128)S(1)} %product.8.refs_2_), custom_call_target="tpu_custom_call" | custom-call | tf_op jit(solution)/shard_map/product/pallas_call | solution.py:287
  (16 shorter events, 0.1 us)
Async XLA Ops:
  0.0 16.9 %collective-permute-start = (f32[8,32,256]{2,1,0:T(8,128)}, f32[8,32,256]{2,1,0:T(8,128)S(1)}, u32[]{:S(2)}, u32[]{:S(2)}) collective-permute-start(f32[8,32,256]{2,1,0:T(8,128)} %refs_0_.1), channel_id=1, source_target_pairs={{0,8},{4,12},{8,0},{12,4},{1,9},{5,13},{9,1},{13,5},{2,10},{6,14},... | collective-permute-start | bytes 786440 | tf_op jit(solution)/shard_map/ppermute | solution.py:300
  4.0 14.9 %collective-permute-start.1 = (f32[8,32,256]{2,1,0:T(8,128)}, f32[8,32,256]{2,1,0:T(8,128)S(1)}, u32[]{:S(2)}, u32[]{:S(2)}) collective-permute-start(f32[8,32,256]{2,1,0:T(8,128)} %refs_0_.1), channel_id=1, source_target_pairs={{0,4},{4,0},{8,12},{12,8},{1,5},{5,1},{9,13},{13,9},{2,6},{6,2},{1... | collective-permute-start | bytes 786440 | tf_op jit(solution)/shard_map/ppermute | solution.py:300
  6.7 7.6 %collective-permute-start.2 = (f32[4,32,512]{2,1,0:T(8,128)S(1)}, f32[4,32,512]{2,1,0:T(8,128)S(1)}, u32[]{:S(2)}, u32[]{:S(2)}) collective-permute-start(f32[4,32,512]{2,1,0:T(8,128)S(1)} %get-tuple-element.29), channel_id=1, source_target_pairs={{0,16},{16,0},{1,17},{17,1},{2,18},{18,2},{3,19},{19,3},{4,20},{20... | collective-permute-start | bytes 786440 | tf_op jit(solution)/shard_map/ppermute | solution.py:300
  8.3 0.9 %copy-start.1 = (f32[2,4,64,128]{3,2,1,0:T(8,128)S(1)}, f32[2,4,64,128]{3,2,1,0:T(8,128)}, u32[]{:S(2)}) copy-start(f32[2,4,64,128]{3,2,1,0:T(8,128)} %constant.32.clone.angles_ref) | copy-start | bytes 786436
  15.2 8.6 %collective-permute-start.5 = (f32[2,2,128,128]{3,2,1,0:T(8,128)S(1)}, f32[2,2,128,128]{3,2,1,0:T(8,128)S(1)}, u32[]{:S(2)}, u32[]{:S(2)}) collective-permute-start(f32[2,2,128,128]{3,2,1,0:T(8,128)S(1)} %get-tuple-element.19.refs_0_.refs_1_), channel_id=1, source_target_pairs={{0,1},{1,0},{2,3},{3,2},{4,5},{5,4},{6,7},{7,6},{8,9},{9,8},{10,11... | collective-permute-start | bytes 786440 | tf_op jit(solution)/shard_map/ppermute | solution.py:300
  15.3 3.6 %copy-start = (f32[8,32,256]{2,1,0:T(8,128)S(1)}, f32[8,32,256]{2,1,0:T(8,128)}, u32[]{:S(2)}) copy-start(f32[8,32,256]{2,1,0:T(8,128)} %refs_0_.1) | copy-start | bytes 786436
  15.3 8.7 %collective-permute-start.6 = (f32[2,2,128,128]{3,2,1,0:T(8,128)S(1)}, f32[2,2,128,128]{3,2,1,0:T(8,128)S(1)}, u32[]{:S(2)}, u32[]{:S(2)}) collective-permute-start(f32[2,2,128,128]{3,2,1,0:T(8,128)S(1)} %get-tuple-element.24), channel_id=1, source_target_pairs={{0,2},{1,3},{2,0},{3,1},{4,6},{5,7},{6,4},{7,5},{8,10},{9,11},{10,... | collective-permute-start | bytes 786440 | tf_op jit(solution)/shard_map/ppermute | solution.py:300
  16.9 6.9 %collective-permute-start.4 = (f32[5,32,256]{2,1,0:T(8,128)S(1)}, f32[5,32,256]{2,1,0:T(8,128)S(1)}, u32[]{:S(2)}, u32[]{:S(2)}) collective-permute-start(f32[5,32,256]{2,1,0:T(8,128)S(1)} %pick.2.refs_5_), channel_id=1, source_target_pairs={{0,4},{4,0},{8,12},{12,8},{1,5},{5,1},{9,13},{13,9},{2,6},{6,2},{1... | collective-permute-start | bytes 491528 | tf_op jit(solution)/shard_map/ppermute | solution.py:300
  17.4 8.6 %collective-permute-start.9 = (f32[2,2,128,128]{3,2,1,0:T(8,128)S(1)}, f32[2,2,128,128]{3,2,1,0:T(8,128)S(1)}, u32[]{:S(2)}, u32[]{:S(2)}) collective-permute-start(f32[2,2,128,128]{3,2,1,0:T(8,128)S(1)} %get-tuple-element.19.refs_0_.refs_1_), channel_id=1, source_target_pairs={{0,16},{16,0},{1,17},{17,1},{2,18},{18,2},{3,19},{19,3},{4,20},{20... | collective-permute-start | bytes 786440 | tf_op jit(solution)/shard_map/ppermute | solution.py:300
  20.4 6.3 %collective-permute-start.3 = (f32[3,32,256]{2,1,0:T(8,128)S(1)}, f32[3,32,256]{2,1,0:T(8,128)S(1)}, u32[]{:S(2)}, u32[]{:S(2)}) collective-permute-start(f32[3,32,256]{2,1,0:T(8,128)S(1)} %pick.3), channel_id=1, source_target_pairs={{0,4},{4,0},{8,12},{12,8},{1,5},{5,1},{9,13},{13,9},{2,6},{6,2},{1... | collective-permute-start | bytes 294920 | tf_op jit(solution)/shard_map/ppermute | solution.py:300
  24.5 10.3 %collective-permute-start.8 = (f32[2,2,160,128]{3,2,1,0:T(8,128)S(1)}, f32[2,2,160,128]{3,2,1,0:T(8,128)S(1)}, u32[]{:S(2)}, u32[]{:S(2)}) collective-permute-start(f32[2,2,160,128]{3,2,1,0:T(8,128)S(1)} %get-tuple-element.27), channel_id=1, source_target_pairs={{0,2},{1,3},{2,0},{3,1},{4,6},{5,7},{6,4},{7,5},{8,10},{9,11},{10,... | collective-permute-start | bytes 983048 | tf_op jit(solution)/shard_map/ppermute | solution.py:300
  26.1 4.5 %collective-permute-start.10 = (f32[2,2,160,128]{3,2,1,0:T(8,128)S(1)}, f32[2,2,160,128]{3,2,1,0:T(8,128)S(1)}, u32[]{:S(2)}, u32[]{:S(2)}) collective-permute-start(f32[2,2,160,128]{3,2,1,0:T(8,128)S(1)} %get-tuple-element.25.refs_5_.refs_1_.refs_0_), channel_id=1, source_target_pairs={{0,1},{1,0},{2,3},{3,2},{4,5},{5,4},{6,7},{7,6},{8,9},{9,8},{10,11... | collective-permute-start | bytes 983048 | tf_op jit(solution)/shard_map/ppermute | solution.py:300
  26.1 4.5 %collective-permute-start.11 = (f32[2,2,128,128]{3,2,1,0:T(8,128)S(1)}, f32[2,2,128,128]{3,2,1,0:T(8,128)S(1)}, u32[]{:S(2)}, u32[]{:S(2)}) collective-permute-start(f32[2,2,128,128]{3,2,1,0:T(8,128)S(1)} %order.4), channel_id=1, source_target_pairs={{0,1},{1,0},{2,3},{3,2},{4,5},{5,4},{6,7},{7,6},{8,9},{9,8},{10,11... | collective-permute-start | bytes 786440 | tf_op jit(solution)/shard_map/ppermute | solution.py:300
  27.1 8.3 %collective-permute-start.15 = (f32[2,2,128,128]{3,2,1,0:T(8,128)S(1)}, f32[2,2,128,128]{3,2,1,0:T(8,128)S(1)}, u32[]{:S(2)}, u32[]{:S(2)}) collective-permute-start(f32[2,2,128,128]{3,2,1,0:T(8,128)S(1)} %order.6.block_ref.refs_1_), channel_id=1, source_target_pairs={{0,16},{16,0},{1,17},{17,1},{2,18},{18,2},{3,19},{19,3},{4,20},{20... | collective-permute-start | bytes 786440 | tf_op jit(solution)/shard_map/ppermute | solution.py:300
  28.6 1.4 %collective-permute-start.12 = (f32[2,2,96,128]{3,2,1,0:T(8,128)S(1)}, f32[2,2,96,128]{3,2,1,0:T(8,128)S(1)}, u32[]{:S(2)}, u32[]{:S(2)}) collective-permute-start(f32[2,2,96,128]{3,2,1,0:T(8,128)S(1)} %get-tuple-element.28.refs_6_.refs_1_), channel_id=1, source_target_pairs={{0,1},{1,0},{2,3},{3,2},{4,5},{5,4},{6,7},{7,6},{8,9},{9,8},{10,11... | collective-permute-start | bytes 589832 | tf_op jit(solution)/shard_map/ppermute | solution.py:300
  30.1 7.9 %collective-permute-start.7 = (f32[2,2,96,128]{3,2,1,0:T(8,128)S(1)}, f32[2,2,96,128]{3,2,1,0:T(8,128)S(1)}, u32[]{:S(2)}, u32[]{:S(2)}) collective-permute-start(f32[2,2,96,128]{3,2,1,0:T(8,128)S(1)} %get-tuple-element.26), channel_id=1, source_target_pairs={{0,2},{1,3},{2,0},{3,1},{4,6},{5,7},{6,4},{7,5},{8,10},{9,11},{10,... | collective-permute-start | bytes 589832 | tf_op jit(solution)/shard_map/ppermute | solution.py:300
  34.7 2.1 %collective-permute-start.13 = (f32[1,2,160,128]{3,2,1,0:T(8,128)S(1)}, f32[1,2,160,128]{3,2,1,0:T(8,128)S(1)}, u32[]{:S(2)}, u32[]{:S(2)}) collective-permute-start(f32[1,2,160,128]{3,2,1,0:T(8,128)S(1)} %far_half.4), channel_id=1, source_target_pairs={{0,1},{1,0},{2,3},{3,2},{4,5},{5,4},{6,7},{7,6},{8,9},{9,8},{10,11... | collective-permute-start | bytes 491528 | tf_op jit(solution)/shard_map/ppermute | solution.py:300
  34.8 1.6 %collective-permute-start.14 = (f32[1,2,128,128]{3,2,1,0:T(8,128)S(1)}, f32[1,2,128,128]{3,2,1,0:T(8,128)S(1)}, u32[]{:S(2)}, u32[]{:S(2)}) collective-permute-start(f32[1,2,128,128]{3,2,1,0:T(8,128)S(1)} %far_half.5), channel_id=1, source_target_pairs={{0,1},{1,0},{2,3},{3,2},{4,5},{5,4},{6,7},{7,6},{8,9},{9,8},{10,11... | collective-permute-start | bytes 393224 | tf_op jit(solution)/shard_map/ppermute | solution.py:300
  35.4 1.4 %collective-permute-start.16 = (f32[1,2,128,128]{3,2,1,0:T(8,128)S(1)}, f32[1,2,128,128]{3,2,1,0:T(8,128)S(1)}, u32[]{:S(2)}, u32[]{:S(2)}) collective-permute-start(f32[1,2,128,128]{3,2,1,0:T(8,128)S(1)} %far_half.6), channel_id=1, source_target_pairs={{0,1},{1,0},{2,3},{3,2},{4,5},{5,4},{6,7},{7,6},{8,9},{9,8},{10,11... | collective-permute-start | bytes 393224 | tf_op jit(solution)/shard_map/ppermute | solution.py:300
  38.0 1.4 %collective-permute-start.17 = (f32[1,2,96,128]{3,2,1,0:T(8,128)S(1)}, f32[1,2,96,128]{3,2,1,0:T(8,128)S(1)}, u32[]{:S(2)}, u32[]{:S(2)}) collective-permute-start(f32[1,2,96,128]{3,2,1,0:T(8,128)S(1)} %far_half.7), channel_id=1, source_target_pairs={{0,1},{1,0},{2,3},{3,2},{4,5},{5,4},{6,7},{7,6},{8,9},{9,8},{10,11... | collective-permute-start | bytes 294920 | tf_op jit(solution)/shard_map/ppermute | solution.py:300
